TPU v7x, 32 devices: a whole 2x2x4 slice. The times are simulated.
32 devices in a mesh: space: 8 (over z, core), date: 4 (over y, x).
Axes of the slice: x: 2, y: 2, z: 4, core: 2. Of those that a mesh axis runs over, the one named last changes fastest.
Arguments:
- acquisitions: bfloat16 [2, 160, 7, 1024], P(None, 'date', None, 'space'), may hold values from -80 to 80
- acquisition_day: int32 [160], replicated, may hold values from 0 to 1428, as said below
Outputs:
- linked: float32 [2, 160, 1024], P(None, 'date', 'space')
Inputs may be any that keep to these rules, and one draw needn't show every extreme that they name: `acquisition_day`: starts at 0 and rises by 6 or 12 days from one date to the next; (159) // 2 of the steps are 12 days.
All inputs are finite; a program needn't handle non-finite values.
Results may differ from a plain program's by a relative error of at most 0.0003.
Values may be sent and summed in bfloat16 or wider, within the bound.
No kernel may reach another device: no remote copies, remote signals or barrier semaphores. Data moves between devices by JAX's collectives and lax.ppermute only.
A program may use at most 64 MiB of HBM per device.

v0:
```python
import math

import jax
import jax.numpy as jnp
from jax import lax
from jax.sharding import PartitionSpec as P

DATES = 160
RIM = 10
ITERS = 2
POWER = 4


epsilon = 1e-06
reweight_gain = 4.0
taper_days = 360.0


def extended(shard, sides, width):
    for axis, dim in sides:
        devices, length = (lax.axis_size(axis), shard.shape[dim])
        up = [(i, (i + 1) % devices) for i in range(devices - 1)]
        down = [(j, i) for i, j in up]
        last = lax.slice_in_dim(shard, length - width, length, axis=dim)
        first = lax.slice_in_dim(shard, 0, width, axis=dim)
        before = lax.ppermute(last, axis, up)
        after = lax.ppermute(first, axis, down)
        shard = jnp.concatenate([before, shard, after], axis=dim)
    return shard


def box_range(field, width):
    total = field[..., 0:width]
    for offset in range(1, 2 * RIM + 1):
        total = total + field[..., offset : offset + width]
    return total


def pixel_weight(intensity_sum):
    return 1.0 / (intensity_sum / DATES + epsilon)


def power_sums(panel, weight, width):
    values = panel.astype(jnp.float32)
    intensity = (values[0] * values[0] + values[1] * values[1]) * weight
    return box_range(jnp.sum(intensity, axis=1), width)


def coherence_block(rows, columns, weight, width, row_power, column_power, row_days, column_days):
    rows_scaled = rows.astype(jnp.float32) * weight
    columns_float = columns.astype(jnp.float32)
    real_sum = None
    imag_sum = None
    for line in range(rows.shape[2]):
        left_real = rows_scaled[0, :, line][:, None, :]
        left_imag = rows_scaled[1, :, line][:, None, :]
        right_real = columns_float[0, :, line][None]
        right_imag = columns_float[1, :, line][None]
        real_term = left_real * right_real + left_imag * right_imag
        imag_term = left_imag * right_real - left_real * right_imag
        real_sum = real_term if real_sum is None else real_sum + real_term
        imag_sum = imag_term if imag_sum is None else imag_sum + imag_term
    taper = jnp.exp(-jnp.abs(row_days[:, None] - column_days[None, :]) / taper_days)
    factor = (
        taper[:, :, None]
        * lax.rsqrt(row_power + epsilon)[:, None, :]
        * lax.rsqrt(column_power + epsilon)[None, :, :]
    )
    return jnp.stack([box_range(real_sum, width) * factor, box_range(imag_sum, width) * factor])


def apply_matrix(matrix, vector):
    real_part = jnp.sum(matrix[0] * vector[0][None] - matrix[1] * vector[1][None], axis=1)
    imag_part = jnp.sum(matrix[0] * vector[1][None] + matrix[1] * vector[0][None], axis=1)
    return jnp.stack([real_part, imag_part])


def reweight(coherence, rows, columns):
    row_length = jnp.sqrt(rows[0] * rows[0] + rows[1] * rows[1])
    column_length = jnp.sqrt(columns[0] * columns[0] + columns[1] * columns[1])
    magnitude = jnp.sqrt(coherence[0] * coherence[0] + coherence[1] * coherence[1])
    along_real = coherence[0] * columns[0][None] - coherence[1] * columns[1][None]
    along_imag = coherence[0] * columns[1][None] + coherence[1] * columns[0][None]
    agree = rows[0][:, None] * along_real + rows[1][:, None] * along_imag
    spread = row_length[:, None] * column_length[None] * magnitude - agree
    return coherence / (1.0 + reweight_gain * spread)


def unit_shared(vector):
    local_sum = jnp.sum(vector[0] * vector[0] + vector[1] * vector[1], axis=0)
    total = lax.psum(local_sum, "date")
    return vector * lax.rsqrt(total / DATES + epsilon)


def local(acquisitions, acquisition_day):
    date_dev = acquisitions.shape[1]
    width = acquisitions.shape[3]
    power_scale = 1.0 / math.sqrt(DATES)
    days = acquisition_day.astype(jnp.float32)
    padded = extended(acquisitions, (("space", 3),), RIM)
    first = lax.axis_index("date") * date_dev
    values = padded.astype(jnp.float32)
    local_intensity = jnp.sum(values[0] * values[0] + values[1] * values[1], axis=0)
    weight = pixel_weight(lax.psum(local_intensity, "date"))
    own_days = lax.dynamic_slice_in_dim(days, first, date_dev, 0)
    own_power = power_sums(padded, weight, width)
    add_piece = lax.all_gather(padded, "date", axis=1, tiled=True)
    piece_power = power_sums(add_piece, weight, width)
    block = coherence_block(
        padded, add_piece, weight, width, own_power, piece_power, own_days, days
    )
    linked = unit_shared(jnp.sum(block, axis=2))
    for outer in range(ITERS):
        whole = lax.all_gather(linked, "date", axis=1, tiled=True)
        matrix = reweight(block, linked, whole)
        iterate = apply_matrix(matrix, whole) * power_scale
        for inner in range(POWER - 1):
            iterate = (
                apply_matrix(matrix, lax.all_gather(iterate, "date", axis=1, tiled=True))
                * power_scale
            )
        linked = unit_shared(iterate)
    return linked


def solution(mesh):
    return jax.shard_map(
        local,
        mesh=mesh,
        in_specs=(P(None, "date", None, "space"), P()),
        out_specs=P(None, "date", "space"),
        check_vma=False,
    )
```

profile of v0, /device:TPU:0, one launch (start us, length us, event | category | flops | bytes accessed | tf_op | source)
XLA Modules:
  0.0 520.8 jit_solution(2036769832488146833)
XLA Ops:
  1.1 2.4 collective-permute-start
  5.6 3.3 collective-permute-done.1
  10.1 10.1 %psum.28 = f32[7,148]{1,0:T(8,128)S(1)} all-reduce(f32[7,148]{1,0:T(8,128)S(1)} %fusion.13), channel_id=1, replica_groups=mesh['space'=8,'date'=4] {'date'}, use_global_device_ids=true, to_apply=%region_1.0 | all-reduce | flops 1036 | bytes 8288 | tf_op jit(solution)/shard_map/psum | solution.py:104
  20.3 17.2 %all_gather.27 = bf16[2,160,7,148]{3,1,2,0:T(8,128)(2,1)S(1)} all-gather(bf16[2,40,7,148]{3,1,2,0:T(8,128)(2,1)S(1)} %get-tuple-element.22), channel_id=1, replica_groups=mesh['space'=8,'date'=4] {'date'}, dimensions={1}, use_global_device_ids=true | all-gather | bytes 828800 | tf_op jit(solution)/shard_map/all_gather | solution.py:107
  38.2 14.4 %subtract_add_fusion = f32[40,160,148]{2,1,0:T(8,128)} fusion(f32[160,148]{1,0:T(8,128)S(1)} %get-tuple-element.24, f32[40,148]{1,0:T(8,128)S(1)} %get-tuple-element.38, f32[160,148]{1,0:T(8,128)S(1)} %get-tuple-element.25, f32[40,148]{1,0:T(8,128)S(1)} %get-tuple-element.39, f32[160,148]{1,0:T(8,128)S(1)} %get-tuple-element.26, ...), kind=kLoop, calls=%fused_computation.1 | loop fusion | flops 25574400 | bytes 5446400 | tf_op jit(solution)/shard_map/add | solution.py:62
  52.6 14.3 %add_add_fusion = f32[40,160,148]{2,1,0:T(8,128)} fusion(f32[160,148]{1,0:T(8,128)S(1)} %get-tuple-element.24, f32[40,148]{1,0:T(8,128)S(1)} %get-tuple-element.38, f32[160,148]{1,0:T(8,128)S(1)} %get-tuple-element.25, f32[40,148]{1,0:T(8,128)S(1)} %get-tuple-element.39, f32[160,148]{1,0:T(8,128)S(1)} %get-tuple-element.26, ...), kind=kLoop, calls=%fused_computation.2 | loop fusion | flops 25574400 | bytes 5446400 | tf_op jit(solution)/shard_map/add | solution.py:61
  67.6 66.6 %fusion.29 = f32[1,40,160,128]{3,2,1,0:T(8,128)S(1)} fusion(f32[160,128]{1,0:T(8,128)S(1)} %fusion.12, f32[40,128]{1,0:T(8,128)S(1)} %fusion.25, f32[40,160]{1,0:T(8,128)S(1)} %multiply_exponential_fusion, f32[40,160,148]{2,1,0:T(8,128)} %subtract_add_fusion), kind=kLoop, calls=%fused_computation.215 | loop fusion | flops 18841600 | bytes 72217600 | tf_op jit(solution)/shard_map/stack | solution.py:69
  134.2 69.8 %fusion.28 = f32[1,40,160,128]{3,2,1,0:T(8,128)} fusion(f32[160,128]{1,0:T(8,128)S(1)} %fusion.12, f32[40,128]{1,0:T(8,128)S(1)} %fusion.25, f32[40,160]{1,0:T(8,128)S(1)} %multiply_exponential_fusion, f32[40,160,148]{2,1,0:T(8,128)} %add_add_fusion), kind=kLoop, calls=%fused_computation.214 | loop fusion | flops 18841600 | bytes 72217600 | tf_op jit(solution)/shard_map/stack | solution.py:69
  204.0 2.7 fusion.2
  206.8 8.9 %psum.29 = f32[128]{0:T(128)S(1)} all-reduce(f32[128]{0:T(128)S(1)} %fusion.23), channel_id=1, replica_groups=mesh['space'=8,'date'=4] {'date'}, use_global_device_ids=true, to_apply=%region_6.0 | all-reduce | flops 128 | bytes 1024 | tf_op jit(solution)/shard_map/psum | solution.py:91
  216.3 8.7 %all_gather.28 = f32[2,160,128]{2,1,0:T(8,128)S(1)} all-gather(f32[2,40,128]{2,1,0:T(8,128)S(1)} %broadcast_multiply_fusion.1), channel_id=1, replica_groups=mesh['space'=8,'date'=4] {'date'}, dimensions={1}, use_global_device_ids=true | all-gather | bytes 204800 | tf_op jit(solution)/shard_map/all_gather | solution.py:114
  225.7 99.0 %multiply_add_fusion.1 = f32[40,160,128]{2,1,0:T(8,128)} fusion(f32[40,128]{1,0:T(8,128)S(1)} %get-tuple-element.74, f32[160,128]{1,0:T(8,128)S(1)} %get-tuple-element.67, f32[160,128]{1,0:T(8,128)} %get-tuple-element.68, f32[40,128]{1,0:T(8,128)S(1)} %get-tuple-element.73, f32[160,128]{1,0:T(8,128)} %get-tuple-element.66, f32[40,128]{1,0:T(8,128)} %add_sqrt_fusion.2, ...), kind=kLoop, calls=%fused_computation.69 | loop fusion | flops 49971200 | bytes 141337600 | tf_op jit(solution)/shard_map/add | solution.py:86
  324.7 3.4 fusion.1
  329.5 8.0 %all_gather.29 = f32[2,160,128]{2,1,0:T(8,128)S(1)} all-gather(f32[2,40,128]{2,1,0:T(8,128)S(1)} %maximum_multiply_fusion), channel_id=1, replica_groups=mesh['space'=8,'date'=4] {'date'}, dimensions={1}, use_global_device_ids=true | all-gather | bytes 204800 | tf_op jit(solution)/shard_map/all_gather | solution.py:119
  339.0 8.7 %all_gather.30 = f32[2,160,128]{2,1,0:T(8,128)S(1)} all-gather(f32[2,40,128]{2,1,0:T(8,128)S(1)} %maximum_multiply_fusion.1), channel_id=1, replica_groups=mesh['space'=8,'date'=4] {'date'}, dimensions={1}, use_global_device_ids=true | all-gather | bytes 204800 | tf_op jit(solution)/shard_map/all_gather | solution.py:119
  349.2 8.0 %all_gather.31 = f32[2,160,128]{2,1,0:T(8,128)S(1)} all-gather(f32[2,40,128]{2,1,0:T(8,128)S(1)} %maximum_multiply_fusion.2), channel_id=1, replica_groups=mesh['space'=8,'date'=4] {'date'}, dimensions={1}, use_global_device_ids=true | all-gather | bytes 204800 | tf_op jit(solution)/shard_map/all_gather | solution.py:119
  358.7 8.9 %psum.30 = f32[128]{0:T(128)S(1)} all-reduce(f32[128]{0:T(128)S(1)} %fusion.21), channel_id=1, replica_groups=mesh['space'=8,'date'=4] {'date'}, use_global_device_ids=true, to_apply=%region_16.0 | all-reduce | flops 128 | bytes 1024 | tf_op jit(solution)/shard_map/psum | solution.py:91
  368.3 8.4 %all_gather.32 = f32[2,160,128]{2,1,0:T(8,128)S(1)} all-gather(f32[2,40,128]{2,1,0:T(8,128)S(1)} %fusion.16), channel_id=1, replica_groups=mesh['space'=8,'date'=4] {'date'}, dimensions={1}, use_global_device_ids=true | all-gather | bytes 204800 | tf_op jit(solution)/shard_map/all_gather | solution.py:114
  377.4 99.0 %multiply_add_fusion = f32[40,160,128]{2,1,0:T(8,128)} fusion(f32[40,128]{1,0:T(8,128)S(1)} %get-tuple-element.72, f32[160,128]{1,0:T(8,128)S(1)} %get-tuple-element.58, f32[160,128]{1,0:T(8,128)} %get-tuple-element.59, f32[40,128]{1,0:T(8,128)S(1)} %get-tuple-element.71, f32[160,128]{1,0:T(8,128)} %get-tuple-element.57, f32[40,128]{1,0:T(8,128)} %add_sqrt_fusion.1, ...), kind=kLoop, calls=%fused_computation.60 | loop fusion | flops 49971200 | bytes 141337600 | tf_op jit(solution)/shard_map/add | solution.py:86
  476.5 3.4 fusion
  481.3 8.5 %all_gather.33 = f32[2,160,128]{2,1,0:T(8,128)S(1)} all-gather(f32[2,40,128]{2,1,0:T(8,128)S(1)} %maximum_multiply_fusion.3), channel_id=1, replica_groups=mesh['space'=8,'date'=4] {'date'}, dimensions={1}, use_global_device_ids=true | all-gather | bytes 204800 | tf_op jit(solution)/shard_map/all_gather | solution.py:119
  491.3 8.5 %all_gather.34 = f32[2,160,128]{2,1,0:T(8,128)S(1)} all-gather(f32[2,40,128]{2,1,0:T(8,128)S(1)} %maximum_multiply_fusion.4), channel_id=1, replica_groups=mesh['space'=8,'date'=4] {'date'}, dimensions={1}, use_global_device_ids=true | all-gather | bytes 204800 | tf_op jit(solution)/shard_map/all_gather | solution.py:119
  501.3 8.0 %all_gather.35 = f32[2,160,128]{2,1,0:T(8,128)S(1)} all-gather(f32[2,40,128]{2,1,0:T(8,128)S(1)} %maximum_multiply_fusion.5), channel_id=1, replica_groups=mesh['space'=8,'date'=4] {'date'}, dimensions={1}, use_global_device_ids=true | all-gather | bytes 204800 | tf_op jit(solution)/shard_map/all_gather | solution.py:119
  510.8 8.9 %psum.31 = f32[128]{0:T(128)S(1)} all-reduce(f32[128]{0:T(128)S(1)} %fusion.19), channel_id=1, replica_groups=mesh['space'=8,'date'=4] {'date'}, use_global_device_ids=true, to_apply=%region_26.0 | all-reduce | flops 128 | bytes 1024 | tf_op jit(solution)/shard_map/psum | solution.py:91
  (58 shorter events, 21.0 us)
Async XLA Ops:
  1.1 4.5 collective-permute-start
  3.5 5.4 %collective-permute-start.1 = (bf16[2,40,7,10]{3,1,2,0:T(8,128)(2,1)S(1)}, bf16[2,40,7,10]{3,1,2,0:T(8,128)(2,1)S(1)}, u32[]{:S(2)}, u32[]{:S(2)}) collective-permute-start(bf16[2,40,7,10]{3,1,2,0:T(8,128)(2,1)S(1)} %get-tuple-element.70), channel_id=1, source_target_pairs={{4,0},{8,4},{12,8},{16,12},{20,16},{24,20},{28,24},{5,1},{9,5},{13... | collective-permute-start | bytes 33608 | tf_op jit(solution)/shard_map/ppermute | solution.py:27
  324.7 3.4 copy-start.1
  476.5 3.4 copy-start
where the time goes:
time: 530 us; the launch traced here: 521 us
  other arithmetic  391 us (74%)
  blocking collectives  121 us (23%)
    add x2, other arithmetic, reweight(): return coherence / (1.0 + reweight_gain * spread)  198 us
    another operation x2, other arithmetic, coherence_block(): jnp.stack([box_range(real_sum, width) * factor, box_range(imag_sum, width...  136 us
    all_gather x6, blocking collectives, local(): lax.all_gather(iterate, 'date', axis=1, tiled=True)  49.7 us
    psum x3, blocking collectives, unit_shared(): total = lax.psum(local_sum, 'date')  26.8 us
    all_gather x1, blocking collectives, local(): add_piece = lax.all_gather(padded, 'date', axis=1, tiled=True)  17.2 us
    all_gather x2, blocking collectives, local(): whole = lax.all_gather(linked, 'date', axis=1, tiled=True)  17.1 us
    add x1, other arithmetic, coherence_block(): imag_sum = imag_term if imag_sum is None else imag_sum + imag_term  14.4 us
    add x1, other arithmetic, coherence_block(): real_sum = real_term if real_sum is None else real_sum + real_term  14.3 us
  transfers between devices with their start and end apart: 2, of which 1 were waited for; matrix products, arithmetic and copies ran while one was open for 0% of the time, Pallas kernels for 0%

commit v1 on v0

v1 whole, which is shorter than its diff:
```python
import functools
import math

import jax
import jax.numpy as jnp
from jax import lax
from jax.experimental import pallas as pl
from jax.experimental.pallas import tpu as pltpu
from jax.sharding import PartitionSpec as P

DATES = 160
RIM = 10
LINES = 7
ITERS = 2
POWER = 4
LANES = 128
PART = 256

epsilon = 1e-06
reweight_gain = 4.0
taper_days = 360.0

f32 = jnp.float32
bf16 = jnp.bfloat16
VMEM = pl.BlockSpec(memory_space=pltpu.VMEM)


class Plan:
    def __init__(self, shape, n_date):
        self.n_date = n_date
        self.own = shape[1]
        self.width = shape[3]
        self.cols = self.width // n_date
        self.pix = min(16, self.cols)
        self.halves = self.cols // self.pix
        self.groups = LANES // self.pix
        self.blocks = DATES // self.groups
        self.span = self.pix + 2 * RIM
        self.left = [d for d in range(n_date) if d * self.cols < RIM]
        self.right = [d for d in range(n_date) if (d + 1) * self.cols + RIM > self.width]


def pack_kernel(plan, x_ref, *refs):
    n_date, width, span = plan.n_date, plan.width, plan.span
    main, halo, plane = refs[:n_date], refs[n_date : 2 * n_date], refs[2 * n_date]
    me = lax.axis_index("date")
    for part in range(2):
        plane[part, :, 0:LINES, :] = x_ref[part].astype(f32)
    lane = lax.broadcasted_iota(jnp.int32, (1, LANES), 1)

    def place(first, low, high):
        tiles = [[jnp.zeros((plan.own, LANES), f32) for _ in range(PART // LANES)] for _ in range(2)]
        for line in range(LINES):
            start = line * span
            shift = lax.rem(start - first + 4 * LANES, LANES)
            for part in range(2):
                moved = pltpu.roll(plane[part, :, line, :], shift, 1)
                for tile in range(PART // LANES):
                    at = lane + tile * LANES - start
                    if start < (tile + 1) * LANES and start + span > tile * LANES:
                        inside = (at >= low) & (at < high)
                        tiles[part][tile] = jnp.where(inside, moved, tiles[part][tile])
        return [tile.astype(bf16) for part in tiles for tile in part]

    for r in range(n_date):
        dest = lax.rem(me + r, n_date)
        for half in range(plan.halves):
            first = dest * plan.cols + half * plan.pix - RIM
            low = jnp.maximum(0, -first)
            high = jnp.minimum(span, width - first)
            for k, tile in enumerate(place(first, low, high)):
                main[r][:, half * 2 * PART + k * LANES : half * 2 * PART + (k + 1) * LANES] = tile
        to_right = dest <= plan.left[-1]
        first = jnp.where(
            to_right,
            dest * plan.cols - RIM + width,
            dest * plan.cols + (plan.halves - 1) * plan.pix - RIM - width,
        )
        low = jnp.maximum(0, -first)
        high = jnp.minimum(span, width - first)
        for k, tile in enumerate(place(first, low, high)):
            halo[r][:, k * LANES : (k + 1) * LANES] = tile


def group_sum(x, pix):
    step = LANES // 2
    while step >= pix:
        x = x + pltpu.roll(x, step, 1)
        step //= 2
    return x


def link_kernel(plan, *refs):
    n_date, own, pix, halves = plan.n_date, plan.own, plan.pix, plan.halves
    groups, blocks = plan.groups, plan.blocks
    main, halo = refs[:n_date], refs[n_date : 2 * n_date]
    mask_ref, rep_ref, days_ref, out_ref = refs[2 * n_date : 2 * n_date + 4]
    (s_ref, left_ref, high_ref, low_ref, a_ref, raw_ref, cr_ref, ci_ref, ca_ref,
     mr_ref, mi_ref, ms_ref, y_ref, v_ref, ty_ref, tv_ref) = refs[2 * n_date + 4 :]
    me = lax.axis_index("date")
    nt = (((1,), (1,)), ((), ()))
    rows = [slice(b, b + 40) for b in range(0, DATES, 40)]
    sub = lax.broadcasted_iota(jnp.int32, (groups, LANES), 0)
    lane = lax.broadcasted_iota(jnp.int32, (groups, LANES), 1)
    diag = jnp.where(lane // pix == sub, 1.0, 0.0).astype(f32)

    def to_rows(y):
        return [
            jnp.sum(y[b * groups : (b + 1) * groups] * diag, axis=0, keepdims=True) for b in range(blocks)
        ]

    is_left = (me <= plan.left[-1]).astype(f32)
    is_right = (me >= plan.right[0]).astype(f32)
    for r in range(n_date):
        block = slice(r * own, (r + 1) * own)
        edge = halo[r][...].astype(f32)
        for h in range(halves):
            s = main[r][:, h * 2 * PART : (h + 1) * 2 * PART].astype(f32)
            if h == 0:
                s = s + edge * is_left
            if h == halves - 1:
                s = s + edge * is_right
            s_ref[h, block, :] = s

    grow = jnp.exp(days_ref[...] * (1.0 / taper_days))
    decay = jnp.exp(days_ref[...] * (-1.0 / taper_days))
    for h in range(halves):
        sr, si = s_ref[h, :, 0:PART], s_ref[h, :, PART : 2 * PART]
        left_ref[h, 0:DATES, 0:PART] = sr.astype(bf16)
        left_ref[h, 0:DATES, PART : 2 * PART] = si.astype(bf16)
        left_ref[h, DATES : 2 * DATES, 0:PART] = si.astype(bf16)
        left_ref[h, DATES : 2 * DATES, PART : 2 * PART] = (-sr).astype(bf16)
        intensity = sr * sr + si * si
        weight = 1.0 / (jnp.sum(intensity, axis=0, keepdims=True) / DATES + epsilon)
        for part, s in enumerate((sr, si)):
            at = slice(part * PART, (part + 1) * PART)
            scaled = s * weight
            high = scaled.astype(bf16).astype(f32)
            high_ref[h, :, at] = high
            low_ref[h, :, at] = scaled - high
        weighted = intensity * weight
        high = weighted.astype(bf16)
        low = (weighted - high.astype(f32)).astype(bf16)
        power = lax.dot_general(high, rep_ref[...], nt, preferred_element_type=f32)
        power = power + lax.dot_general(low, rep_ref[...], nt, preferred_element_type=f32)
        root = lax.rsqrt(power + epsilon)
        for k, t in enumerate((grow, decay)):
            y = t * root
            ty_ref[k, h] = y
            for b, row in enumerate(to_rows(y)):
                tv_ref[k, h, b : b + 1, :] = row

    per = 2 if blocks % 2 == 0 else 1
    unit = max(1, 16 // pix)

    def build(h, first):
        for p in range(per):
            for g in range(0, groups, unit):
                for k, ref in enumerate((high_ref, low_ref)):
                    rows16 = jnp.concatenate(
                        [
                            jnp.broadcast_to(ref[h, pl.ds((first + p) * groups + g + u, 1), :], (pix, 2 * PART))
                            for u in range(unit)
                        ],
                        axis=0,
                    )
                    at = p * LANES + g * pix
                    a_ref[h, k, at : at + 16, :] = rows16.astype(bf16) * mask_ref[...]

    def multiply(h):
        total = lax.dot_general(left_ref[h], a_ref[h, 0], nt, preferred_element_type=f32)
        raw_ref[h] = total + lax.dot_general(left_ref[h], a_ref[h, 1], nt, preferred_element_type=f32)

    def normalise(h, first):
        for p in range(per):
            b = first + p
            grow_row = tv_ref[0, h, pl.ds(b, 1), :]
            decay_row = tv_ref[1, h, pl.ds(b, 1), :]
            at = slice(p * LANES, (p + 1) * LANES)
            for part in rows:
                shifted = slice(part.start + DATES, part.stop + DATES)
                factor = jnp.minimum(ty_ref[0, h, part] * decay_row, ty_ref[1, h, part] * grow_row)
                cr = raw_ref[h, part, at] * factor
                ci = raw_ref[h, shifted, at] * factor
                square = cr * cr + ci * ci
                cr_ref[h, b, part, :] = cr
                ci_ref[h, b, part, :] = ci
                ca_ref[h, b, part, :] = square * lax.rsqrt(jnp.maximum(square, 1e-36))
                y_ref[0, h, part] += cr
                y_ref[1, h, part] += ci

    y_ref[...] = jnp.zeros(y_ref.shape, f32)

    def coherence(step, carry):
        for h in range(halves):
            build(h, step * per)
        for h in range(halves):
            multiply(h)
        for h in range(halves):
            normalise(h, step * per)
        return carry

    lax.fori_loop(0, blocks // per, coherence, 0)

    def unit_vector(scale, times):
        for h in range(halves):
            yr = group_sum(y_ref[0, h], pix) * scale
            yi = group_sum(y_ref[1, h], pix) * scale
            mean = jnp.sum(yr * yr + yi * yi, axis=0, keepdims=True) / DATES
            inv = lax.rsqrt(mean + epsilon)
            yr, yi = yr * inv, yi * inv
            y_ref[0, h] = yr
            y_ref[1, h] = yi

    def as_rows():
        for h in range(halves):
            for k in range(3):
                for b, row in enumerate(to_rows(y_ref[k, h])):
                    v_ref[k, h, b : b + 1, :] = row

    def first_step():
        for h in range(halves):
            yr, yi = y_ref[0, h], y_ref[1, h]
            square = yr * yr + yi * yi
            y_ref[2, h] = square * lax.rsqrt(jnp.maximum(square, 1e-36))
        as_rows()

        def body(b, carry):
            for h in range(halves):
                lr, li = v_ref[0, h, pl.ds(b, 1), :], v_ref[1, h, pl.ds(b, 1), :]
                la = v_ref[2, h, pl.ds(b, 1), :] * reweight_gain
                lr4, li4 = lr * reweight_gain, li * reweight_gain
                sum_r = jnp.zeros((8, LANES), f32)
                sum_i = jnp.zeros((8, LANES), f32)
                for part in rows:
                    cr, ci = cr_ref[h, b, part, :], ci_ref[h, b, part, :]
                    yr, yi = y_ref[0, h, part], y_ref[1, h, part]
                    pr = cr * yr + ci * yi
                    pi = cr * yi - ci * yr
                    den = (1.0 + ca_ref[h, b, part, :] * (y_ref[2, h, part] * la)) - (lr4 * pr + li4 * pi)
                    g = 1.0 / den
                    mr, mi = cr * g, ci * g
                    mr_ref[h, b, part, :] = mr
                    mi_ref[h, b, part, :] = mi
                    ms_ref[h, b, part, :] = mr + mi
                    sum_r = sum_r + jnp.sum((pr * g).reshape(5, 8, LANES), axis=0)
                    sum_i = sum_i + jnp.sum((pi * g).reshape(5, 8, LANES), axis=0)
                set_row(h, b, jnp.sum(sum_r, axis=0, keepdims=True), jnp.sum(sum_i, axis=0, keepdims=True))
            return carry

        lax.fori_loop(0, blocks, body, 0)

    def set_row(h, b, vr, vi):
        tv_ref[0, h, pl.ds(b, 1), :] = vr
        tv_ref[1, h, pl.ds(b, 1), :] = vi

    def rows_to_lanes():
        for h in range(halves):
            vr, vi = tv_ref[0, h], tv_ref[1, h]
            v_ref[0, h] = vr
            v_ref[1, h] = vi - vr
            v_ref[2, h] = vr + vi
        for h in range(halves):
            for part in rows:
                zero = jnp.zeros((40, LANES), f32)

                def body(b, acc, h=h, part=part):
                    v0, v1, v2 = (v_ref[k, h, pl.ds(b, 1), :] for k in range(3))
                    return (
                        acc[0] + ms_ref[h, b, part, :] * v0,
                        acc[1] + mr_ref[h, b, part, :] * v1,
                        acc[2] + mi_ref[h, b, part, :] * v2,
                    )

                k1, k2, k3 = lax.fori_loop(0, blocks, body, (zero, zero, zero), unroll=5)
                y_ref[0, h, part] = k1 - k3
                y_ref[1, h, part] = k1 + k2

    def lanes_to_rows():
        for h in range(halves):
            yr = group_sum(y_ref[0, h], pix)
            yi = group_sum(y_ref[1, h], pix)
            y_ref[0, h] = yr
            y_ref[1, h] = yi - yr
            y_ref[2, h] = yr + yi
        for h in range(halves):

            def body(step, carry, h=h):
                sums = [[jnp.zeros((8, LANES), f32) for _ in range(3)] for _ in range(per)]
                for part in rows:
                    y0, y1, y2 = (y_ref[k, h, part] for k in range(3))
                    for p in range(per):
                        b = step * per + p
                        for k, (m, y) in enumerate(((ms_ref, y0), (mi_ref, y1), (mr_ref, y2))):
                            sums[p][k] += jnp.sum((m[h, b, part, :] * y).reshape(5, 8, LANES), axis=0)
                for p in range(per):
                    k1, k2, k3 = (jnp.sum(s, axis=0, keepdims=True) for s in sums[p])
                    set_row(h, step * per + p, k1 + k2, k3 - k1)
                return carry

            lax.fori_loop(0, blocks // per, body, 0, unroll=2 if blocks // per % 2 == 0 else 1)

    unit_vector(1.0, 1.0)
    for outer in range(ITERS):
        first_step()
        for step in range(1, POWER):
            if step % 2:
                rows_to_lanes()
            else:
                lanes_to_rows()
        unit_vector(1.0 / math.sqrt(DATES) ** POWER, 1.0)

    spread = lax.broadcasted_iota(jnp.int32, (1, LANES), 1) // pix % halves
    for k in range(2):
        value = y_ref[k, 0]
        for h in range(1, halves):
            value = jnp.where(spread == h, y_ref[k, h], value)
        out_ref[k] = value


def local(acquisitions, acquisition_day):
    n_date, n_space = lax.axis_size("date"), lax.axis_size("space")
    plan = Plan(acquisitions.shape, n_date)
    own, pix, halves, groups, blocks = plan.own, plan.pix, plan.halves, plan.groups, plan.blocks
    me = lax.axis_index("date")

    packed = pl.pallas_call(
        functools.partial(pack_kernel, plan),
        out_shape=[jax.ShapeDtypeStruct((own, halves * 2 * PART), bf16)] * n_date
        + [jax.ShapeDtypeStruct((own, 2 * PART), bf16)] * n_date,
        in_specs=[VMEM],
        out_specs=[VMEM] * (2 * n_date),
        scratch_shapes=[pltpu.VMEM((2, own, 8, LANES), f32)],
        compiler_params=pltpu.CompilerParams(vmem_limit_bytes=32 * 2**20),
    )(acquisitions)
    main, halo = list(packed[:n_date]), list(packed[n_date:])
    for r in range(1, n_date):
        main[r] = lax.ppermute(main[r], "date", [(i, (i + r) % n_date) for i in range(n_date)])
    for r in range(n_date):
        pairs = []
        for s in range(n_space):
            for k in range(n_date):
                d = (k + r) % n_date
                if d in plan.left and s + 1 < n_space:
                    pairs.append((s * n_date + k, (s + 1) * n_date + d))
                if d in plan.right and s > 0:
                    pairs.append((s * n_date + k, (s - 1) * n_date + d))
        halo[r] = lax.ppermute(halo[r], ("space", "date"), pairs)

    lanes = jnp.arange(PART)
    line, column = lanes // plan.span, lanes % plan.span
    offset = column[None, :] - jnp.arange(pix)[:, None]
    inside = (line < LINES)[None, :] & (offset >= 0) & (offset <= 2 * RIM)
    mask = jnp.tile(inside.astype(bf16), (16 // pix, 2))
    rep = jnp.tile(inside.astype(bf16), (groups, 1))
    order = lax.rem(me + n_date - jnp.arange(n_date), n_date)
    days = acquisition_day.astype(f32).reshape(n_date, own)[order].reshape(DATES, 1)
    days = jnp.broadcast_to(days, (DATES, LANES))

    matrix = pltpu.VMEM((halves, blocks, DATES, LANES), f32)
    per = 2 if blocks % 2 == 0 else 1
    out = pl.pallas_call(
        functools.partial(link_kernel, plan),
        out_shape=jax.ShapeDtypeStruct((2, DATES, LANES), f32),
        in_specs=[VMEM] * (2 * n_date + 3),
        out_specs=VMEM,
        scratch_shapes=[
            pltpu.VMEM((halves, DATES, 2 * PART), f32),
            pltpu.VMEM((halves, 2 * DATES, 2 * PART), bf16),
            pltpu.VMEM((halves, DATES, 2 * PART), f32),
            pltpu.VMEM((halves, DATES, 2 * PART), f32),
            pltpu.VMEM((halves, 2, per * LANES, 2 * PART), bf16),
            pltpu.VMEM((halves, 2 * DATES, per * LANES), f32),
        ]
        + [matrix] * 6
        + [
            pltpu.VMEM((3, halves, DATES, LANES), f32),
            pltpu.VMEM((3, halves, blocks, LANES), f32),
            pltpu.VMEM((2, halves, DATES, LANES), f32),
            pltpu.VMEM((2, halves, blocks, LANES), f32),
        ],
        compiler_params=pltpu.CompilerParams(vmem_limit_bytes=56 * 2**20),
    )(*main, *halo, mask, rep, days)

    lane_owner = jnp.arange(LANES) // plan.cols
    result = out[:, 0:own]
    for r in range(1, n_date):
        piece = out[:, r * own : (r + 1) * own]
        piece = lax.ppermute(piece, "date", [(i, (i - r) % n_date) for i in range(n_date)])
        result = jnp.where(lane_owner == lax.rem(me + r, n_date), piece, result)
    return result


def solution(mesh):
    return jax.shard_map(
        local,
        mesh=mesh,
        in_specs=(P(None, "date", None, "space"), P()),
        out_specs=P(None, "date", "space"),
        check_vma=False,
    )
```

time: 530 us -> 55.7 us (0.11); the launches traced: 521 us -> 55.1 us
  other arithmetic: 391 us -> 1.47 us
  blocking collectives: 121 us -> 0 us
  Pallas kernels: 0 us -> 23.3 us
  starting transfers between devices: 3.66 us -> 20.8 us
    add x4 -> x0, other arithmetic: 227 us -> none  [the longest x2 198 us: reweight(): return coherence / (1.0 + reweight_gain * spread)]
    another operation x2 -> x0, other arithmetic: 136 us -> none  [coherence_block(): jnp.stack([box_range(real_sum, width) * factor, box_range(imag_sum, width...]
    all_gather x9 -> x0, blocking collectives: 84 us -> none  [the longest x6 49.7 us: local(): lax.all_gather(iterate, 'date', axis=1, tiled=True)]
    psum x4 -> x0, blocking collectives: 36.8 us -> none  [the longest x3 26.8 us: unit_shared(): total = lax.psum(local_sum, 'date')]
    pallas_call x0 -> x2, Pallas kernels: none -> 23.3 us  [the longest x1 21.3 us: local(): pl.pallas_call(functools.partial(link_kernel, plan), out_shape=jax.ShapeD...]
    ppermute x2 -> x10, starting transfers between devices: 3.66 us -> 20.8 us  [the longest x3 11.6 us: local(): lax.ppermute(piece, 'date', [(i, (i - r) % n_date) for i in range(n_date)])]
    reduce_sum x15 -> x0, other arithmetic: 14.7 us -> none  [the longest x8 11.6 us: apply_matrix(): jnp.sum(matrix[0] * vector[0][None] - matrix[1] * vector[1][None], axis=1)]
    div x3 -> x0, other arithmetic: 6.73 us -> none  [the longest x2 6.72 us: reweight(): return coherence / (1.0 + reweight_gain * spread)]
  transfers between devices with their start and end apart: 2 -> 10, of which waited for: 1 -> 4; matrix products, arithmetic and copies ran while one was open for 0% -> 3% of each run, Pallas kernels for 0% -> 0%
where the time goes in v1:
time: 55.7 us; the launch traced here: 55.1 us
  Pallas kernels  23.3 us (42%)
  starting transfers between devices  20.8 us (37%)
  local copies, waits for them, and re-layouts  5.23 us (9%)
  waiting for transfers between devices  4.05 us (7%)
  other arithmetic  1.47 us (3%)
    pallas_call x1, Pallas kernels, local(): pl.pallas_call(functools.partial(link_kernel, plan), out_shape=jax.ShapeD...  21.3 us
    ppermute x3, starting transfers between devices, local(): lax.ppermute(piece, 'date', [(i, (i - r) % n_date) for i in range(n_date)])  11.6 us
    ppermute x3, starting transfers between devices, local(): lax.ppermute(main[r], 'date', [(i, (i + r) % n_date) for i in range(n_dat...  5.89 us
    ppermute x3, waiting for transfers between devices, local(): lax.ppermute(piece, 'date', [(i, (i - r) % n_date) for i in range(n_date)])  3.95 us
    ppermute x4, starting transfers between devices, local(): halo[r] = lax.ppermute(halo[r], ('space', 'date'), pairs)  3.26 us
    unnamed x20, local copies, waits for them, and re-layouts  2.28 us
    pallas_call x1, Pallas kernels, local(): pl.pallas_call(functools.partial(pack_kernel, plan), out_shape=[jax.Shape...  2.01 us
    select_n x1, other arithmetic, local(): result = jnp.where(lane_owner == lax.rem(me + r, n_date), piece, result)  1.41 us
  transfers between devices with their start and end apart: 10, of which 4 were waited for; matrix products, arithmetic and copies ran while one was open for 3% of the time, Pallas kernels for 0%

profile of v1, /device:TPU:0, one launch (start us, length us, event | category | flops | bytes accessed | tf_op | source)
XLA Modules:
  0.0 55.1 jit_solution(10379152360664419870)
XLA Ops:
  0.0 0.9 %copy.3.x_ref = bf16[2,40,7,128]{3,2,1,0:T(8,128)(2,1)S(1)} copy(bf16[2,40,7,128]{3,1,2,0:T(8,128)(2,1)} %param.2) | data formatting | bytes 286720 | tf_op args[0]
  0.9 2.0 %shard_map.28 = (bf16[40,1024]{1,0:T(8,128)(2,1)S(1)}, bf16[40,1024]{1,0:T(8,128)(2,1)S(1)}, bf16[40,1024]{1,0:T(8,128)(2,1)S(1)}, bf16[40,1024]{1,0:T(8,128)(2,...) custom-call(bf16[2,40,7,128]{3,2,1,0:T(8,128)(2,1)S(1)} %copy.3.x_ref), custom_call_target="tpu_custom_call" | custom-call | tf_op jit(solution)/shard_map/pallas_call | solution.py:327
  3.0 0.6 %copy-done = bf16[40,1024]{1,0:T(8,128)(2,1)} copy-done((bf16[40,1024]{1,0:T(8,128)(2,1)}, bf16[40,1024]{1,0:T(8,128)(2,1)S(1)}, u32[]{:S(2)}) %copy-start) | copy-done | bytes 81944
  3.6 2.9 %collective-permute-start = (bf16[40,1024]{1,0:T(8,128)(2,1)S(1)}, bf16[40,1024]{1,0:T(8,128)(2,1)S(1)}, u32[]{:S(2)}, u32[]{:S(2)}) collective-permute-start(bf16[40,1024]{1,0:T(8,128)(2,1)S(1)} %get-tuple-element.14), channel_id=1, source_target_pairs={{0,1},{1,2},{2,3},{3,0},{4,5},{5,6},{6,7},{7,4},{8,9},{9,10},{10,1... | collective-permute-start | bytes 245768 | tf_op jit(solution)/shard_map/ppermute | solution.py:338
  6.5 1.5 %collective-permute-start.1 = (bf16[40,1024]{1,0:T(8,128)(2,1)S(1)}, bf16[40,1024]{1,0:T(8,128)(2,1)S(1)}, u32[]{:S(2)}, u32[]{:S(2)}) collective-permute-start(bf16[40,1024]{1,0:T(8,128)(2,1)S(1)} %get-tuple-element.15), channel_id=1, source_target_pairs={{0,2},{1,3},{2,0},{3,1},{4,6},{5,7},{6,4},{7,5},{8,10},{9,11},{10,... | collective-permute-start | bytes 245768 | tf_op jit(solution)/shard_map/ppermute | solution.py:338
  8.1 1.4 %collective-permute-start.2 = (bf16[40,1024]{1,0:T(8,128)(2,1)S(1)}, bf16[40,1024]{1,0:T(8,128)(2,1)S(1)}, u32[]{:S(2)}, u32[]{:S(2)}) collective-permute-start(bf16[40,1024]{1,0:T(8,128)(2,1)S(1)} %get-tuple-element.16), channel_id=1, source_target_pairs={{0,3},{1,0},{2,1},{3,2},{4,7},{5,4},{6,5},{7,6},{8,11},{9,8},{10,9... | collective-permute-start | bytes 245768 | tf_op jit(solution)/shard_map/ppermute | solution.py:338
  9.5 1.3 %collective-permute-start.3 = (bf16[40,512]{1,0:T(8,128)(2,1)S(1)}, bf16[40,512]{1,0:T(8,128)(2,1)S(1)}, u32[]{:S(2)}, u32[]{:S(2)}) collective-permute-start(bf16[40,512]{1,0:T(8,128)(2,1)S(1)} %get-tuple-element.17), channel_id=1, source_target_pairs={{0,4},{4,8},{7,3},{8,12},{11,7},{12,16},{15,11},{16,20},{19,15},{2... | collective-permute-start | bytes 122888 | tf_op jit(solution)/shard_map/ppermute | solution.py:348
  10.8 0.7 %collective-permute-start.4 = (bf16[40,512]{1,0:T(8,128)(2,1)S(1)}, bf16[40,512]{1,0:T(8,128)(2,1)S(1)}, u32[]{:S(2)}, u32[]{:S(2)}) collective-permute-start(bf16[40,512]{1,0:T(8,128)(2,1)S(1)} %get-tuple-element.18), channel_id=1, source_target_pairs={{3,4},{6,3},{7,8},{10,7},{11,12},{14,11},{15,16},{18,15},{19,20},{... | collective-permute-start | bytes 122888 | tf_op jit(solution)/shard_map/ppermute | solution.py:348
  11.5 0.1 collective-permute-done.3.refs_4_
  11.6 0.7 %collective-permute-start.5 = (bf16[40,512]{1,0:T(8,128)(2,1)S(1)}, bf16[40,512]{1,0:T(8,128)(2,1)S(1)}, u32[]{:S(2)}, u32[]{:S(2)}) collective-permute-start(bf16[40,512]{1,0:T(8,128)(2,1)S(1)} %get-tuple-element.19), channel_id=1, source_target_pairs={{2,4},{5,3},{6,8},{9,7},{10,12},{13,11},{14,16},{17,15},{18,20},{2... | collective-permute-start | bytes 122888 | tf_op jit(solution)/shard_map/ppermute | solution.py:348
  12.3 0.7 %collective-permute-start.6 = (bf16[40,512]{1,0:T(8,128)(2,1)S(1)}, bf16[40,512]{1,0:T(8,128)(2,1)S(1)}, u32[]{:S(2)}, u32[]{:S(2)}) collective-permute-start(bf16[40,512]{1,0:T(8,128)(2,1)S(1)} %get-tuple-element.20), channel_id=1, source_target_pairs={{1,4},{4,3},{5,8},{8,7},{9,12},{12,11},{13,16},{16,15},{17,20},{20... | collective-permute-start | bytes 122888 | tf_op jit(solution)/shard_map/ppermute | solution.py:348
  13.0 0.6 %copy.4 = bf16[2,8,2,256]{3,1,2,0:T(8,128)(2,1)} copy(bf16[2,8,2,256]{3,2,1,0:T(2,128)(2,1)S(1)} %bitcast.7) | data formatting | bytes 32768
  13.7 0.1 reshape.86
  13.8 0.6 %gather_fusion = f32[4,40]{1,0:T(4,128)S(1)} fusion(f32[4,40]{1,0:T(4,128)S(1)} %reshape.86, s32[1024]{0:T(1024)S(1)} %pad_clamp_fusion), kind=kCustom, calls=%fused_computation | custom fusion | bytes 1296 | tf_op jit(solution)/shard_map/gather | solution.py:357
  14.5 0.7 %tile.20 = bf16[8,16,256]{2,1,0:T(8,128)(2,1)} broadcast(bf16[16,256]{1,0:T(8,128)(2,1)S(1)} %fusion.6), dimensions={1,2} | broadcast | bytes 73728 | tf_op jit(solution)/shard_map/tile | solution.py:355
  15.2 0.7 %broadcast_in_dim.23.refs_10_ = f32[160,128]{1,0:T(8,128)} broadcast(f32[160]{0:T(256)S(1)} %broadcast_in_dim.22), dimensions={0} | broadcast | bytes 82560 | tf_op jit(solution)/shard_map/broadcast_in_dim | solution.py:358
  15.9 21.3 %shard_map.29 = f32[2,160,128]{2,1,0:T(8,128)} custom-call(bf16[40,1024]{1,0:T(8,128)(2,1)} %copy-done, bf16[40,1024]{1,0:T(8,128)(2,1)} %copy-done.1, bf16[40,1024]{1,0:T(8,128)(2,1)} %copy-done.2, bf16[40,1024]{1,0:T(8,128)(2,1)} %copy-done.3, bf16[40,512]{1,0:T(8,128)(2,1)} %copy-done.4, bf16[40,512]{1,0:T(8,128)(2,1)} %copy-done.5, ...), custom_call_target="tpu_custom_call" | custom-call | tf_op jit(solution)/shard_map/pallas_call | solution.py:362
  37.2 0.8 %fusion.12 = (f32[2,40,128]{2,1,0:T(8,128)S(1)}, f32[2,40,128]{2,1,0:T(8,128)S(1)}, f32[2,40,128]{2,1,0:T(8,128)S(1)}) fusion(f32[2,160,128]{2,1,0:T(8,128)} %shard_map.29), kind=kLoop, calls=%fused_computation.31 | loop fusion | bytes 245760 | tf_op jit(solution)/shard_map/slice | solution.py:388
  38.1 10.1 %collective-permute-start.7 = (f32[2,40,128]{2,1,0:T(8,128)S(1)}, f32[2,40,128]{2,1,0:T(8,128)S(1)}, u32[]{:S(2)}, u32[]{:S(2)}) collective-permute-start(f32[2,40,128]{2,1,0:T(8,128)S(1)} %get-tuple-element.23), channel_id=1, source_target_pairs={{0,1},{1,2},{2,3},{3,0},{4,5},{5,6},{6,7},{7,4},{8,9},{9,10},{10,1... | collective-permute-start | bytes 122888 | tf_op jit(solution)/shard_map/ppermute | solution.py:389
  48.2 1.5 %collective-permute-start.8 = (f32[2,40,128]{2,1,0:T(8,128)S(1)}, f32[2,40,128]{2,1,0:T(8,128)S(1)}, u32[]{:S(2)}, u32[]{:S(2)}) collective-permute-start(f32[2,40,128]{2,1,0:T(8,128)S(1)} %get-tuple-element.22), channel_id=1, source_target_pairs={{0,2},{1,3},{2,0},{3,1},{4,6},{5,7},{6,4},{7,5},{8,10},{9,11},{10,... | collective-permute-start | bytes 122888 | tf_op jit(solution)/shard_map/ppermute | solution.py:389
  49.7 1.4 %collective-permute-done.7 = f32[2,40,128]{2,1,0:T(8,128)S(1)} collective-permute-done((f32[2,40,128]{2,1,0:T(8,128)S(1)}, f32[2,40,128]{2,1,0:T(8,128)S(1)}, u32[]{:S(2)}, u32[]{:S(2)}) %collective-permute-start.7) | collective-permute-done | bytes 40992 | tf_op jit(solution)/shard_map/ppermute | solution.py:389
  51.1 1.5 %collective-permute-done.8 = f32[2,40,128]{2,1,0:T(8,128)S(1)} collective-permute-done((f32[2,40,128]{2,1,0:T(8,128)S(1)}, f32[2,40,128]{2,1,0:T(8,128)S(1)}, u32[]{:S(2)}, u32[]{:S(2)}) %collective-permute-start.8) | collective-permute-done | bytes 40992 | tf_op jit(solution)/shard_map/ppermute | solution.py:389
  52.6 1.1 %collective-permute-done.9 = f32[2,40,128]{2,1,0:T(8,128)S(1)} collective-permute-done((f32[2,40,128]{2,1,0:T(8,128)S(1)}, f32[2,40,128]{2,1,0:T(8,128)S(1)}, u32[]{:S(2)}, u32[]{:S(2)}) %collective-permute-start.9) | collective-permute-done | bytes 40992 | tf_op jit(solution)/shard_map/ppermute | solution.py:389
  53.7 1.4 %fusion.1 = f32[2,40,128]{2,1,0:T(8,128)} fusion(f32[2,40,128]{2,1,0:T(8,128)S(1)} %collective-permute-done.7, f32[2,40,128]{2,1,0:T(8,128)S(1)} %collective-permute-done.8, f32[2,40,128]{2,1,0:T(8,128)S(1)} %collective-permute-done.9, f32[2,160,128]{2,1,0:T(8,128)} %shard_map.29, pred[128]{0:T(512)(128)(4,1)S(1)} %get-tuple-element.24, ...), kind=kLoop, calls=%fused_computation.3 | loop fusion | flops 30720 | bytes 205184 | tf_op jit(solution)/shard_map/jit(_where)/select_n | solution.py:390
  (34 shorter events, 0.3 us)
Async XLA Ops:
  3.0 0.6 %copy-start = (bf16[40,1024]{1,0:T(8,128)(2,1)}, bf16[40,1024]{1,0:T(8,128)(2,1)S(1)}, u32[]{:S(2)}) copy-start(bf16[40,1024]{1,0:T(8,128)(2,1)S(1)} %get-tuple-element.13.refs_0_) | copy-start | bytes 245764
  3.6 10.9 %collective-permute-start = (bf16[40,1024]{1,0:T(8,128)(2,1)S(1)}, bf16[40,1024]{1,0:T(8,128)(2,1)S(1)}, u32[]{:S(2)}, u32[]{:S(2)}) collective-permute-start(bf16[40,1024]{1,0:T(8,128)(2,1)S(1)} %get-tuple-element.14), channel_id=1, source_target_pairs={{0,1},{1,2},{2,3},{3,0},{4,5},{5,6},{6,7},{7,4},{8,9},{9,10},{10,1... | collective-permute-start | bytes 245768 | tf_op jit(solution)/shard_map/ppermute | solution.py:338
  6.5 8.0 %collective-permute-start.1 = (bf16[40,1024]{1,0:T(8,128)(2,1)S(1)}, bf16[40,1024]{1,0:T(8,128)(2,1)S(1)}, u32[]{:S(2)}, u32[]{:S(2)}) collective-permute-start(bf16[40,1024]{1,0:T(8,128)(2,1)S(1)} %get-tuple-element.15), channel_id=1, source_target_pairs={{0,2},{1,3},{2,0},{3,1},{4,6},{5,7},{6,4},{7,5},{8,10},{9,11},{10,... | collective-permute-start | bytes 245768 | tf_op jit(solution)/shard_map/ppermute | solution.py:338
  8.1 6.5 %collective-permute-start.2 = (bf16[40,1024]{1,0:T(8,128)(2,1)S(1)}, bf16[40,1024]{1,0:T(8,128)(2,1)S(1)}, u32[]{:S(2)}, u32[]{:S(2)}) collective-permute-start(bf16[40,1024]{1,0:T(8,128)(2,1)S(1)} %get-tuple-element.16), channel_id=1, source_target_pairs={{0,3},{1,0},{2,1},{3,2},{4,7},{5,4},{6,5},{7,6},{8,11},{9,8},{10,9... | collective-permute-start | bytes 245768 | tf_op jit(solution)/shard_map/ppermute | solution.py:338
  9.5 2.1 %collective-permute-start.3 = (bf16[40,512]{1,0:T(8,128)(2,1)S(1)}, bf16[40,512]{1,0:T(8,128)(2,1)S(1)}, u32[]{:S(2)}, u32[]{:S(2)}) collective-permute-start(bf16[40,512]{1,0:T(8,128)(2,1)S(1)} %get-tuple-element.17), channel_id=1, source_target_pairs={{0,4},{4,8},{7,3},{8,12},{11,7},{12,16},{15,11},{16,20},{19,15},{2... | collective-permute-start | bytes 122888 | tf_op jit(solution)/shard_map/ppermute | solution.py:348
  10.8 1.5 %collective-permute-start.4 = (bf16[40,512]{1,0:T(8,128)(2,1)S(1)}, bf16[40,512]{1,0:T(8,128)(2,1)S(1)}, u32[]{:S(2)}, u32[]{:S(2)}) collective-permute-start(bf16[40,512]{1,0:T(8,128)(2,1)S(1)} %get-tuple-element.18), channel_id=1, source_target_pairs={{3,4},{6,3},{7,8},{10,7},{11,12},{14,11},{15,16},{18,15},{19,20},{... | collective-permute-start | bytes 122888 | tf_op jit(solution)/shard_map/ppermute | solution.py:348
  11.6 2.7 %copy-start.4 = (bf16[40,512]{1,0:T(8,128)(2,1)}, bf16[40,512]{1,0:T(8,128)(2,1)S(1)}, u32[]{:S(2)}) copy-start(bf16[40,512]{1,0:T(8,128)(2,1)S(1)} %collective-permute-done.3.refs_4_) | copy-start | bytes 122884
  11.6 2.8 %collective-permute-start.5 = (bf16[40,512]{1,0:T(8,128)(2,1)S(1)}, bf16[40,512]{1,0:T(8,128)(2,1)S(1)}, u32[]{:S(2)}, u32[]{:S(2)}) collective-permute-start(bf16[40,512]{1,0:T(8,128)(2,1)S(1)} %get-tuple-element.19), channel_id=1, source_target_pairs={{2,4},{5,3},{6,8},{9,7},{10,12},{13,11},{14,16},{17,15},{18,20},{2... | collective-permute-start | bytes 122888 | tf_op jit(solution)/shard_map/ppermute | solution.py:348
  12.3 2.1 %copy-start.5 = (bf16[40,512]{1,0:T(8,128)(2,1)}, bf16[40,512]{1,0:T(8,128)(2,1)S(1)}, u32[]{:S(2)}) copy-start(bf16[40,512]{1,0:T(8,128)(2,1)S(1)} %collective-permute-done.4.refs_5_) | copy-start | bytes 122884
  12.3 2.1 %collective-permute-start.6 = (bf16[40,512]{1,0:T(8,128)(2,1)S(1)}, bf16[40,512]{1,0:T(8,128)(2,1)S(1)}, u32[]{:S(2)}, u32[]{:S(2)}) collective-permute-start(bf16[40,512]{1,0:T(8,128)(2,1)S(1)} %get-tuple-element.20), channel_id=1, source_target_pairs={{1,4},{4,3},{5,8},{8,7},{9,12},{12,11},{13,16},{16,15},{17,20},{20... | collective-permute-start | bytes 122888 | tf_op jit(solution)/shard_map/ppermute | solution.py:348
  13.0 0.7 %copy-start.8 = (s32[160]{0:T(256)S(1)}, s32[160]{0:T(256)}, u32[]{:S(2)}) copy-start(s32[160]{0:T(256)} %param.3) | copy-start | bytes 1924
  14.4 1.5 %copy-start.6 = (bf16[40,512]{1,0:T(8,128)(2,1)}, bf16[40,512]{1,0:T(8,128)(2,1)S(1)}, u32[]{:S(2)}) copy-start(bf16[40,512]{1,0:T(8,128)(2,1)S(1)} %collective-permute-done.5.refs_6_) | copy-start | bytes 122884
  14.5 1.5 %copy-start.7 = (bf16[40,512]{1,0:T(8,128)(2,1)}, bf16[40,512]{1,0:T(8,128)(2,1)S(1)}, u32[]{:S(2)}) copy-start(bf16[40,512]{1,0:T(8,128)(2,1)S(1)} %collective-permute-done.6.refs_7_) | copy-start | bytes 122884
  14.5 1.4 %copy-start.1 = (bf16[40,1024]{1,0:T(8,128)(2,1)}, bf16[40,1024]{1,0:T(8,128)(2,1)S(1)}, u32[]{:S(2)}) copy-start(bf16[40,1024]{1,0:T(8,128)(2,1)S(1)} %collective-permute-done.refs_1_) | copy-start | bytes 245764
  14.5 1.4 %copy-start.2 = (bf16[40,1024]{1,0:T(8,128)(2,1)}, bf16[40,1024]{1,0:T(8,128)(2,1)S(1)}, u32[]{:S(2)}) copy-start(bf16[40,1024]{1,0:T(8,128)(2,1)S(1)} %collective-permute-done.1.refs_2_) | copy-start | bytes 245764
  14.5 1.4 %copy-start.3 = (bf16[40,1024]{1,0:T(8,128)(2,1)}, bf16[40,1024]{1,0:T(8,128)(2,1)S(1)}, u32[]{:S(2)}) copy-start(bf16[40,1024]{1,0:T(8,128)(2,1)S(1)} %collective-permute-done.2.refs_3_) | copy-start | bytes 245764
  38.1 13.0 %collective-permute-start.7 = (f32[2,40,128]{2,1,0:T(8,128)S(1)}, f32[2,40,128]{2,1,0:T(8,128)S(1)}, u32[]{:S(2)}, u32[]{:S(2)}) collective-permute-start(f32[2,40,128]{2,1,0:T(8,128)S(1)} %get-tuple-element.23), channel_id=1, source_target_pairs={{0,1},{1,2},{2,3},{3,0},{4,5},{5,6},{6,7},{7,4},{8,9},{9,10},{10,1... | collective-permute-start | bytes 122888 | tf_op jit(solution)/shard_map/ppermute | solution.py:389
  48.2 4.4 %collective-permute-start.8 = (f32[2,40,128]{2,1,0:T(8,128)S(1)}, f32[2,40,128]{2,1,0:T(8,128)S(1)}, u32[]{:S(2)}, u32[]{:S(2)}) collective-permute-start(f32[2,40,128]{2,1,0:T(8,128)S(1)} %get-tuple-element.22), channel_id=1, source_target_pairs={{0,2},{1,3},{2,0},{3,1},{4,6},{5,7},{6,4},{7,5},{8,10},{9,11},{10,... | collective-permute-start | bytes 122888 | tf_op jit(solution)/shard_map/ppermute | solution.py:389
  49.7 4.0 %collective-permute-start.9 = (f32[2,40,128]{2,1,0:T(8,128)S(1)}, f32[2,40,128]{2,1,0:T(8,128)S(1)}, u32[]{:S(2)}, u32[]{:S(2)}) collective-permute-start(f32[2,40,128]{2,1,0:T(8,128)S(1)} %get-tuple-element.21), channel_id=1, source_target_pairs={{0,3},{1,0},{2,1},{3,2},{4,7},{5,4},{6,5},{7,6},{8,11},{9,8},{10,9... | collective-permute-start | bytes 122888 | tf_op jit(solution)/shard_map/ppermute | solution.py:389

commit v2 on v0

v2 whole, which is shorter than its diff:
```python
import functools
import math

import jax
import jax.numpy as jnp
from jax import lax
from jax.experimental import pallas as pl
from jax.experimental.pallas import tpu as pltpu
from jax.sharding import PartitionSpec as P

DATES = 160
RIM = 10
LINES = 7
ITERS = 2
POWER = 4
LANES = 128
PART = 256

epsilon = 1e-06
reweight_gain = 4.0
taper_days = 360.0

f32 = jnp.float32
bf16 = jnp.bfloat16
VMEM = pl.BlockSpec(memory_space=pltpu.VMEM)


class Plan:
    def __init__(self, shape, n_date):
        self.n_date = n_date
        self.own = shape[1]
        self.width = shape[3]
        self.cols = self.width // n_date
        self.pix = min(16, self.cols)
        self.halves = self.cols // self.pix
        assert self.halves <= 2
        self.groups = LANES // self.pix
        self.blocks = DATES // self.groups
        self.per = 2 if self.blocks % 2 == 0 else 1
        self.span = self.pix + 2 * RIM
        self.left = [d for d in range(n_date) if d * self.cols < RIM]
        self.right = [n_date - 1 - d for d in self.left]
        self.message = self.halves * 2 * PART + PART

    def half(self, dest, slot):
        if self.halves == 1:
            return 0
        return jnp.where(dest <= self.left[-1], 1 - slot, slot)


def pack_kernel(plan, x_ref, *refs):
    n_date, width, span = plan.n_date, plan.width, plan.span
    main, plane = refs[:n_date], refs[n_date]
    me = lax.axis_index("date")
    plane[...] = x_ref[...].astype(f32)
    lane = lax.broadcasted_iota(jnp.int32, (1, LANES), 1)
    tile_count = PART // LANES

    def place(tiles, part, first, low, high, lead=0):
        for line in range(LINES):
            start = line * span
            shift = lax.rem(start + lead - first + 4 * LANES, LANES)
            moved = pltpu.roll(plane[part, line], shift, 1)
            for tile in range(tile_count):
                if start - 16 < (tile + 1) * LANES and start + span + 16 > tile * LANES:
                    at = lane + (tile * LANES - start) - lead
                    tiles[tile] = jnp.where((at >= low) & (at < high), moved, tiles[tile])

    def blank():
        return [jnp.zeros((plan.own, LANES), f32) for _ in range(tile_count)]

    def put(r, base, tiles):
        for k, tile in enumerate(tiles):
            main[r][:, base + k * LANES : base + (k + 1) * LANES] = tile.astype(bf16)

    for r in range(n_date):
        dest = lax.rem(me + r, n_date)
        for slot in range(plan.halves):
            first = dest * plan.cols + plan.half(dest, slot) * plan.pix - RIM
            low = jnp.maximum(0, -first)
            high = jnp.minimum(span, width - first)
            for part in range(2):
                tiles = blank()
                place(tiles, part, first, low, high)
                put(r, (slot * 2 + part) * PART, tiles)
        other = n_date - 1 - dest
        after = dest >= plan.right[-1]
        first = jnp.where(after, other * plan.cols - RIM + width, (other + 1) * plan.cols - plan.pix - RIM - width)
        low = jnp.where(after, 0, jnp.maximum(0, -first))
        high = jnp.where(after, jnp.minimum(RIM, width - first), span)
        low = jnp.where(after, low, jnp.maximum(low, span - RIM))
        tiles = blank()
        place(tiles, 0, first, low, high)
        place(tiles, 1, first, low, high, jnp.where(after, RIM, -RIM))
        put(r, plan.halves * 2 * PART, tiles)


def group_sum(x, pix):
    step = LANES // 2
    while step >= pix:
        x = x + pltpu.roll(x, step, 1)
        step //= 2
    return x


def link_kernel(plan, slot, *refs):
    n_date, own, pix = plan.n_date, plan.own, plan.pix
    groups, blocks, per, span = plan.groups, plan.blocks, plan.per, plan.span
    last = slot == plan.halves - 1
    main, days_ref, refs = refs[:n_date], refs[n_date], refs[n_date + 1 :]
    edge_ref = before_ref = None
    if last:
        edge_ref, refs = refs[0], refs[1:]
        if slot:
            before_ref, refs = refs[0], refs[1:]
    outs, refs = refs[: n_date if last else 1], refs[n_date if last else 1 :]
    (s_ref, left_ref, high_ref, low_ref, a_ref, raw_ref, cr_ref, ci_ref, ca_ref,
     mr_ref, mi_ref, ms_ref, y_ref, v_ref, ty_ref, tv_ref) = refs
    me = lax.axis_index("date")
    nt = (((1,), (1,)), ((), ()))
    rows = [slice(b, b + 40) for b in range(0, DATES, 40)]
    sub = lax.broadcasted_iota(jnp.int32, (groups, LANES), 0)
    lane = lax.broadcasted_iota(jnp.int32, (groups, LANES), 1)
    diag = jnp.where(lane // pix == sub, 1.0, 0.0).astype(f32)

    column = lax.broadcasted_iota(jnp.int32, (16, PART), 1)
    for _line in range(1, LINES):
        column = jnp.where(column >= span, column - span, column)
    spot = lax.broadcasted_iota(jnp.int32, (16, PART), 1)
    offset = column - lax.rem(lax.broadcasted_iota(jnp.int32, (16, PART), 0), pix)
    inside = (offset >= 0) & (offset <= 2 * RIM) & (spot < LINES * span)
    inside = jnp.where(inside, 1.0, 0.0).astype(f32)
    mask = jnp.concatenate([inside, inside], axis=1).astype(bf16)
    rep = jnp.concatenate([inside] * (LANES // 16), axis=0).astype(bf16)

    def to_rows(y):
        return [
            jnp.sum(y[b * groups : (b + 1) * groups] * diag, axis=0, keepdims=True) for b in range(blocks)
        ]

    for r in range(n_date):
        s_ref[r * own : (r + 1) * own, :] = main[r][:, slot * 2 * PART : (slot + 1) * 2 * PART].astype(f32)
    if last:
        is_left = me <= plan.left[-1]
        is_edge = is_left | (me >= plan.right[-1])
        edge = edge_ref[...].astype(f32)
        raw_ref[0:DATES, 0:PART] = edge
        raw_ref[DATES : 2 * DATES, 0:PART] = edge

        @pl.when(is_edge)
        def _():
            start = lax.rem(3 * n_date - 1 - 2 * me, n_date) * own
            got = raw_ref[pl.ds(pl.multiple_of(start, 8), DATES), 0:PART]
            at = lax.broadcasted_iota(jnp.int32, (1, PART), 1)
            col = at
            for _line in range(1, LINES):
                col = jnp.where(col >= span, col - span, col)
            start = jnp.where(is_left, 0, span - RIM)
            valid = (col >= start) & (col < start + RIM) & (at < LINES * span)
            s_ref[:, 0:PART] = jnp.where(valid, s_ref[:, 0:PART] + got, s_ref[:, 0:PART])
            back = jnp.where(is_left, PART - RIM, RIM)
            got = pltpu.roll(got, back, 1)
            s_ref[:, PART : 2 * PART] = jnp.where(valid, s_ref[:, PART : 2 * PART] + got, s_ref[:, PART : 2 * PART])

    for r in range(n_date):
        first = lax.rem(me + n_date - r, n_date) * own
        for t in range(own):
            day = days_ref[first + t].astype(f32)
            y_ref[0, r * own + t : r * own + t + 1, :] = jnp.broadcast_to(day, (1, LANES))
    days = y_ref[0]
    grow = jnp.exp(days * (1.0 / taper_days))
    decay = jnp.exp(days * (-1.0 / taper_days))
    sr, si = s_ref[:, 0:PART], s_ref[:, PART : 2 * PART]
    left_ref[0:DATES, 0:PART] = sr.astype(bf16)
    left_ref[0:DATES, PART : 2 * PART] = si.astype(bf16)
    left_ref[DATES : 2 * DATES, 0:PART] = si.astype(bf16)
    left_ref[DATES : 2 * DATES, PART : 2 * PART] = (-sr).astype(bf16)
    intensity = sr * sr + si * si
    weight = 1.0 / (jnp.sum(intensity, axis=0, keepdims=True) / DATES + epsilon)
    for part, s in enumerate((sr, si)):
        at = slice(part * PART, (part + 1) * PART)
        scaled = s * weight
        high = scaled.astype(bf16).astype(f32)
        high_ref[:, at] = high
        low_ref[:, at] = scaled - high
    weighted = intensity * weight
    high = weighted.astype(bf16)
    low = (weighted - high.astype(f32)).astype(bf16)
    power = lax.dot_general(high, rep, nt, preferred_element_type=f32)
    power = power + lax.dot_general(low, rep, nt, preferred_element_type=f32)
    root = lax.rsqrt(power + epsilon)
    for k, t in enumerate((grow, decay)):
        y = t * root
        ty_ref[k] = y
        for b, row in enumerate(to_rows(y)):
            tv_ref[k, b : b + 1, :] = row

    unit = max(1, 16 // pix)

    def build(first):
        for p in range(per):
            for g in range(0, groups, unit):
                for k, ref in enumerate((high_ref, low_ref)):
                    rows16 = jnp.concatenate(
                        [
                            jnp.broadcast_to(ref[pl.ds((first + p) * groups + g + u, 1), :], (pix, 2 * PART))
                            for u in range(unit)
                        ],
                        axis=0,
                    )
                    at = p * LANES + g * pix
                    a_ref[k, at : at + 16, :] = rows16.astype(bf16) * mask

    def multiply():
        total = lax.dot_general(left_ref[...], a_ref[0], nt, preferred_element_type=f32)
        raw_ref[...] = total + lax.dot_general(left_ref[...], a_ref[1], nt, preferred_element_type=f32)

    def normalise(first):
        for p in range(per):
            b = first + p
            grow_row = tv_ref[0, pl.ds(b, 1), :]
            decay_row = tv_ref[1, pl.ds(b, 1), :]
            at = slice(p * LANES, (p + 1) * LANES)
            for part in rows:
                shifted = slice(part.start + DATES, part.stop + DATES)
                factor = jnp.minimum(ty_ref[0, part] * decay_row, ty_ref[1, part] * grow_row)
                cr = raw_ref[part, at] * factor
                ci = raw_ref[shifted, at] * factor
                square = cr * cr + ci * ci
                cr_ref[b, part, :] = cr
                ci_ref[b, part, :] = ci
                ca_ref[b, part, :] = square * lax.rsqrt(jnp.maximum(square, 1e-36))
                y_ref[0, part] += cr
                y_ref[1, part] += ci

    y_ref[...] = jnp.zeros(y_ref.shape, f32)

    def coherence(step, carry):
        build(step * per)
        multiply()
        normalise(step * per)
        return carry

    lax.fori_loop(0, blocks // per, coherence, 0)

    def unit_vector(scale):
        yr = group_sum(y_ref[0], pix) * scale
        yi = group_sum(y_ref[1], pix) * scale
        mean = jnp.sum(yr * yr + yi * yi, axis=0, keepdims=True) / DATES
        inv = lax.rsqrt(mean + epsilon)
        y_ref[0] = yr * inv
        y_ref[1] = yi * inv

    def first_step():
        yr, yi = y_ref[0], y_ref[1]
        square = yr * yr + yi * yi
        y_ref[2] = square * lax.rsqrt(jnp.maximum(square, 1e-36))
        for k in range(3):
            for b, row in enumerate(to_rows(y_ref[k])):
                v_ref[k, b : b + 1, :] = row

        def body(b, carry):
            la = v_ref[2, pl.ds(b, 1), :] * reweight_gain
            lr4 = v_ref[0, pl.ds(b, 1), :] * reweight_gain
            li4 = v_ref[1, pl.ds(b, 1), :] * reweight_gain
            sum_r = jnp.zeros((8, LANES), f32)
            sum_i = jnp.zeros((8, LANES), f32)
            for part in rows:
                cr, ci = cr_ref[b, part, :], ci_ref[b, part, :]
                yr, yi = y_ref[0, part], y_ref[1, part]
                pr = cr * yr + ci * yi
                pi = cr * yi - ci * yr
                den = (1.0 + ca_ref[b, part, :] * (y_ref[2, part] * la)) - (lr4 * pr + li4 * pi)
                g = 1.0 / den
                mr, mi = cr * g, ci * g
                mr_ref[b, part, :] = mr
                mi_ref[b, part, :] = mi
                ms_ref[b, part, :] = mr + mi
                sum_r = sum_r + jnp.sum((pr * g).reshape(5, 8, LANES), axis=0)
                sum_i = sum_i + jnp.sum((pi * g).reshape(5, 8, LANES), axis=0)
            set_row(b, jnp.sum(sum_r, axis=0, keepdims=True), jnp.sum(sum_i, axis=0, keepdims=True))
            return carry

        lax.fori_loop(0, blocks, body, 0)

    def set_row(b, vr, vi):
        tv_ref[0, pl.ds(b, 1), :] = vr
        tv_ref[1, pl.ds(b, 1), :] = vi

    def rows_to_lanes():
        vr, vi = tv_ref[0], tv_ref[1]
        v_ref[0] = vr
        v_ref[1] = vi - vr
        v_ref[2] = vr + vi
        for part in rows:
            zero = jnp.zeros((40, LANES), f32)

            def body(b, acc, part=part):
                v0, v1, v2 = (v_ref[k, pl.ds(b, 1), :] for k in range(3))
                return (
                    acc[0] + ms_ref[b, part, :] * v0,
                    acc[1] + mr_ref[b, part, :] * v1,
                    acc[2] + mi_ref[b, part, :] * v2,
                )

            k1, k2, k3 = lax.fori_loop(0, blocks, body, (zero, zero, zero), unroll=5)
            y_ref[0, part] = k1 - k3
            y_ref[1, part] = k1 + k2

    def lanes_to_rows():
        yr = group_sum(y_ref[0], pix)
        yi = group_sum(y_ref[1], pix)
        y_ref[0] = yr
        y_ref[1] = yi - yr
        y_ref[2] = yr + yi

        def body(step, carry):
            sums = [[jnp.zeros((8, LANES), f32) for _ in range(3)] for _ in range(per)]
            for part in rows:
                y0, y1, y2 = (y_ref[k, part] for k in range(3))
                for p in range(per):
                    b = step * per + p
                    for k, (m, y) in enumerate(((ms_ref, y0), (mi_ref, y1), (mr_ref, y2))):
                        sums[p][k] += jnp.sum((m[b, part, :] * y).reshape(5, 8, LANES), axis=0)
            for p in range(per):
                k1, k2, k3 = (jnp.sum(s, axis=0, keepdims=True) for s in sums[p])
                set_row(step * per + p, k1 + k2, k3 - k1)
            return carry

        lax.fori_loop(0, blocks // per, body, 0, unroll=2 if blocks // per % 2 == 0 else 1)

    unit_vector(1.0)
    for outer in range(ITERS):
        first_step()
        for step in range(1, POWER):
            if step % 2:
                rows_to_lanes()
            else:
                lanes_to_rows()
        unit_vector(1.0 / math.sqrt(DATES) ** POWER)

    if not last:
        outs[0][...] = y_ref[0:2]
        return
    place = lax.rem(lax.broadcasted_iota(jnp.int32, (1, LANES), 1) // pix, plan.halves)
    here = place == plan.half(me, slot)
    for r in range(n_date):
        at = slice(r * own, (r + 1) * own)
        for k in range(2):
            value = y_ref[k, at]
            if slot:
                value = jnp.where(here, value, before_ref[k, at])
            outs[r][k] = value


def link(plan, slot, main, days, *more):
    last = slot == plan.halves - 1
    matrix = pltpu.VMEM((plan.blocks, DATES, LANES), f32)
    samples = pltpu.VMEM((DATES, 2 * PART), f32)
    if last:
        shapes = [jax.ShapeDtypeStruct((2, plan.own, LANES), f32)] * plan.n_date
    else:
        shapes = [jax.ShapeDtypeStruct((2, DATES, LANES), f32)]
    return pl.pallas_call(
        functools.partial(link_kernel, plan, slot),
        out_shape=shapes,
        in_specs=[VMEM] * plan.n_date + [pl.BlockSpec(memory_space=pltpu.SMEM)] + [VMEM] * len(more),
        out_specs=[VMEM] * len(shapes),
        scratch_shapes=[
            samples,
            pltpu.VMEM((2 * DATES, 2 * PART), bf16),
            samples,
            samples,
            pltpu.VMEM((2, plan.per * LANES, 2 * PART), bf16),
            pltpu.VMEM((2 * DATES, PART), f32),
        ]
        + [matrix] * 6
        + [
            pltpu.VMEM((3, DATES, LANES), f32),
            pltpu.VMEM((3, plan.blocks, LANES), f32),
            pltpu.VMEM((2, DATES, LANES), f32),
            pltpu.VMEM((2, plan.blocks, LANES), f32),
        ],
        compiler_params=pltpu.CompilerParams(vmem_limit_bytes=24 * 2**20),
    )(*main, days, *more)


def local(acquisitions, acquisition_day):
    n_date, n_space = lax.axis_size("date"), lax.axis_size("space")
    plan = Plan(acquisitions.shape, n_date)
    own = plan.own
    me = lax.axis_index("date")

    main = pl.pallas_call(
        functools.partial(pack_kernel, plan),
        out_shape=[jax.ShapeDtypeStruct((own, plan.message), bf16)] * n_date,
        in_specs=[VMEM],
        out_specs=[VMEM] * n_date,
        scratch_shapes=[pltpu.VMEM((2, LINES, own, LANES), f32)],
        compiler_params=pltpu.CompilerParams(vmem_limit_bytes=24 * 2**20),
    )(jnp.transpose(acquisitions, (0, 2, 1, 3)))
    main = list(main)
    for r in range(1, n_date):
        main[r] = lax.ppermute(main[r], "date", [(i, (i + r) % n_date) for i in range(n_date)])
    swap = []
    for s in range(n_space - 1):
        for d in plan.left:
            before, after = s * n_date + n_date - 1 - d, (s + 1) * n_date + d
            swap += [(before, after), (after, before)]
    edge = jnp.concatenate([m[:, plan.halves * 2 * PART :] for m in main], axis=0)
    edge = lax.ppermute(edge, ("space", "date"), swap)

    if plan.halves == 1:
        out = link(plan, 0, main, acquisition_day, edge)
    else:
        (before,) = link(plan, 0, main, acquisition_day)
        out = link(plan, 1, main, acquisition_day, edge, before)

    lane_owner = jnp.arange(LANES) // plan.cols
    result = out[0]
    for r in range(1, n_date):
        piece = lax.ppermute(out[r], "date", [(i, (i - r) % n_date) for i in range(n_date)])
        result = jnp.where(lane_owner == lax.rem(me + r, n_date), piece, result)
    return result


def solution(mesh):
    return jax.shard_map(
        local,
        mesh=mesh,
        in_specs=(P(None, "date", None, "space"), P()),
        out_specs=P(None, "date", "space"),
        check_vma=False,
    )
```

time: 530 us -> 45.3 us (0.09)
  the two profiles are of different devices: /device:TPU:0 before, /device:TPU:1 now
where the time goes in v2:
time: 45.3 us; the launch traced here: 45.1 us
  Pallas kernels  24.5 us (54%)
  starting transfers between devices  11.9 us (26%)
  waiting for transfers between devices  7.02 us (15%)
  local copies, waits for them, and re-layouts  0.92 us (2%)
  other arithmetic  0.65 us (1%)
    pallas_call x2, Pallas kernels, link(): pl.pallas_call(functools.partial(link_kernel, plan, slot), out_shape=shap...  24 us
    ppermute x1, starting transfers between devices, local(): edge = lax.ppermute(edge, ('space', 'date'), swap)  4.83 us
    ppermute x3, waiting for transfers between devices, local(): lax.ppermute(main[r], 'date', [(i, (i + r) % n_date) for i in range(n_dat...  4.17 us
    ppermute x3, starting transfers between devices, local(): lax.ppermute(main[r], 'date', [(i, (i + r) % n_date) for i in range(n_dat...  3.59 us
    ppermute x3, starting transfers between devices, local(): lax.ppermute(out[r], 'date', [(i, (i - r) % n_date) for i in range(n_date)])  3.48 us
    ppermute x3, waiting for transfers between devices, local(): lax.ppermute(out[r], 'date', [(i, (i - r) % n_date) for i in range(n_date)])  2.84 us
    unnamed x4, local copies, waits for them, and re-layouts  0.91 us
  transfers between devices with their start and end apart: 7, of which 6 were waited for; matrix products, arithmetic and copies ran while one was open for 0% of the time, Pallas kernels for 26%

profile of v2, /device:TPU:1, one launch (start us, length us, event | category | flops | bytes accessed | tf_op | source)
XLA Modules:
  0.0 45.1 jit_solution(14196473513724921789)
XLA Ops:
  0.0 0.0 copy-start
  0.0 0.9 %copy-done = bf16[2,40,7,128]{3,1,2,0:T(8,128)(2,1)S(1)} copy-done((bf16[2,40,7,128]{3,1,2,0:T(8,128)(2,1)S(1)}, bf16[2,40,7,128]{3,1,2,0:T(8,128)(2,1)}, u32[]{:S(2)}) %copy-start) | copy-done | bytes 143384
  0.9 0.6 %shard_map.28 = (bf16[40,1280]{1,0:T(8,128)(2,1)S(1)}, bf16[40,1280]{1,0:T(8,128)(2,1)S(1)}, bf16[40,1280]{1,0:T(8,128)(2,1)S(1)}, bf16[40,1280]{1,0:T(8,128)(2,1)S(1)}) custom-call(bf16[2,7,40,128]{3,2,1,0:T(8,128)(2,1)S(1)} %bitcast.1), custom_call_target="tpu_custom_call" | custom-call | tf_op jit(solution)/shard_map/pallas_call | solution.py:394
  1.5 3.0 %collective-permute-start.2 = (bf16[40,1280]{1,0:T(8,128)(2,1)S(1)}, bf16[40,1280]{1,0:T(8,128)(2,1)S(1)}, u32[]{:S(2)}, u32[]{:S(2)}) collective-permute-start(bf16[40,1280]{1,0:T(8,128)(2,1)S(1)} %get-tuple-element.16), channel_id=1, source_target_pairs={{0,3},{1,0},{2,1},{3,2},{4,7},{5,4},{6,5},{7,6},{8,11},{9,8},{10,9... | collective-permute-start | bytes 307208 | tf_op jit(solution)/shard_map/ppermute | solution.py:404
  4.5 0.2 collective-permute-start.1
  4.7 0.3 collective-permute-start
  5.1 1.1 %collective-permute-done.2.refs_3_ = bf16[40,1280]{1,0:T(8,128)(2,1)S(1)} collective-permute-done((bf16[40,1280]{1,0:T(8,128)(2,1)S(1)}, bf16[40,1280]{1,0:T(8,128)(2,1)S(1)}, u32[]{:S(2)}, u32[]{:S(2)}) %collective-permute-start.2) | collective-permute-done | bytes 102432 | tf_op jit(solution)/shard_map/ppermute | solution.py:404
  6.2 1.8 %collective-permute-done.1.refs_2_ = bf16[40,1280]{1,0:T(8,128)(2,1)S(1)} collective-permute-done((bf16[40,1280]{1,0:T(8,128)(2,1)S(1)}, bf16[40,1280]{1,0:T(8,128)(2,1)S(1)}, u32[]{:S(2)}, u32[]{:S(2)}) %collective-permute-start.1) | collective-permute-done | bytes 102432 | tf_op jit(solution)/shard_map/ppermute | solution.py:404
  8.0 1.2 %collective-permute-done.refs_1_ = bf16[40,1280]{1,0:T(8,128)(2,1)S(1)} collective-permute-done((bf16[40,1280]{1,0:T(8,128)(2,1)S(1)}, bf16[40,1280]{1,0:T(8,128)(2,1)S(1)}, u32[]{:S(2)}, u32[]{:S(2)}) %collective-permute-start) | collective-permute-done | bytes 102432 | tf_op jit(solution)/shard_map/ppermute | solution.py:404
  9.3 0.0 copy-start.1
  9.3 4.8 %collective-permute-start.3 = (bf16[160,256]{1,0:T(8,128)(2,1)S(1)}, bf16[160,256]{1,0:T(8,128)(2,1)S(1)}, u32[]{:S(2)}, u32[]{:S(2)}) collective-permute-start(bf16[160,256]{1,0:T(8,128)(2,1)S(1)} %pad_maximum_fusion), channel_id=1, source_target_pairs={{3,4},{4,3},{7,8},{8,7},{11,12},{12,11},{15,16},{16,15},{19,20},{2... | collective-permute-start | bytes 245768 | tf_op jit(solution)/shard_map/ppermute | solution.py:411
  14.1 0.0 copy-done.1
  14.1 11.9 %shard_map.29.refs_6_ = f32[2,160,128]{2,1,0:T(8,128)S(1)} custom-call(bf16[40,1280]{1,0:T(8,128)(2,1)S(1)} %get-tuple-element.13.refs_0_, bf16[40,1280]{1,0:T(8,128)(2,1)S(1)} %collective-permute-done.refs_1_, bf16[40,1280]{1,0:T(8,128)(2,1)S(1)} %collective-permute-done.1.refs_2_, bf16[40,1280]{1,0:T(8,128)(2,1)S(1)} %collective-permute-done.2.refs_3_, ...), custom_call_target="tpu_custom_call" | custom-call | tf_op jit(solution)/shard_map/pallas_call | solution.py:364
  26.1 0.0 collective-permute-done.3.refs_5_
  26.1 12.1 %shard_map.30 = (f32[2,40,128]{2,1,0:T(8,128)S(1)}, f32[2,40,128]{2,1,0:T(8,128)S(1)}, f32[2,40,128]{2,1,0:T(8,128)S(1)}, f32[2,40,128]{2,1,0:T(8,128)S(1)}) custom-call(bf16[40,1280]{1,0:T(8,128)(2,1)S(1)} %get-tuple-element.13.refs_0_, bf16[40,1280]{1,0:T(8,128)(2,1)S(1)} %collective-permute-done.refs_1_, ...), custom_call_target="tpu_custom_call" | custom-call | tf_op jit(solution)/shard_map/pallas_call | solution.py:364
  38.1 0.1 collective-permute-start.4
  38.2 3.4 %collective-permute-start.5 = (f32[2,40,128]{2,1,0:T(8,128)S(1)}, f32[2,40,128]{2,1,0:T(8,128)S(1)}, u32[]{:S(2)}, u32[]{:S(2)}) collective-permute-start(f32[2,40,128]{2,1,0:T(8,128)S(1)} %get-tuple-element.18), channel_id=1, source_target_pairs={{0,2},{1,3},{2,0},{3,1},{4,6},{5,7},{6,4},{7,5},{8,10},{9,11},{10,... | collective-permute-start | bytes 122888 | tf_op jit(solution)/shard_map/ppermute | solution.py:422
  41.6 0.0 collective-permute-start.6
  41.6 1.1 %collective-permute-done.4 = f32[2,40,128]{2,1,0:T(8,128)S(1)} collective-permute-done((f32[2,40,128]{2,1,0:T(8,128)S(1)}, f32[2,40,128]{2,1,0:T(8,128)S(1)}, u32[]{:S(2)}, u32[]{:S(2)}) %collective-permute-start.4) | collective-permute-done | bytes 40992 | tf_op jit(solution)/shard_map/ppermute | solution.py:422
  42.7 0.4 collective-permute-done.5
  43.2 1.3 %collective-permute-done.6 = f32[2,40,128]{2,1,0:T(8,128)S(1)} collective-permute-done((f32[2,40,128]{2,1,0:T(8,128)S(1)}, f32[2,40,128]{2,1,0:T(8,128)S(1)}, u32[]{:S(2)}, u32[]{:S(2)}) %collective-permute-start.6) | collective-permute-done | bytes 40992 | tf_op jit(solution)/shard_map/ppermute | solution.py:422
  44.5 0.6 %select_select_fusion = f32[2,40,128]{2,1,0:T(8,128)} fusion(f32[2,40,128]{2,1,0:T(8,128)S(1)} %collective-permute-done.4, f32[2,40,128]{2,1,0:T(8,128)S(1)} %collective-permute-done.5, f32[2,40,128]{2,1,0:T(8,128)S(1)} %collective-permute-done.6, f32[2,40,128]{2,1,0:T(8,128)S(1)} %get-tuple-element.20, pred[128]{0:T(512)(128)(4,1)S(1)} %get-tuple-element.21, ...), kind=kLoop, calls=%fused_computation.1 | loop fusion | flops 30720 | bytes 205184 | tf_op jit(solution)/shard_map/jit(_where)/select_n | solution.py:423
  (7 shorter events, 0.0 us)
Async XLA Ops:
  0.0 0.9 %copy-start = (bf16[2,40,7,128]{3,1,2,0:T(8,128)(2,1)S(1)}, bf16[2,40,7,128]{3,1,2,0:T(8,128)(2,1)}, u32[]{:S(2)}) copy-start(bf16[2,40,7,128]{3,1,2,0:T(8,128)(2,1)} %param.2) | copy-start | bytes 430084
  1.5 4.7 %collective-permute-start.2 = (bf16[40,1280]{1,0:T(8,128)(2,1)S(1)}, bf16[40,1280]{1,0:T(8,128)(2,1)S(1)}, u32[]{:S(2)}, u32[]{:S(2)}) collective-permute-start(bf16[40,1280]{1,0:T(8,128)(2,1)S(1)} %get-tuple-element.16), channel_id=1, source_target_pairs={{0,3},{1,0},{2,1},{3,2},{4,7},{5,4},{6,5},{7,6},{8,11},{9,8},{10,9... | collective-permute-start | bytes 307208 | tf_op jit(solution)/shard_map/ppermute | solution.py:404
  4.5 3.5 %collective-permute-start.1 = (bf16[40,1280]{1,0:T(8,128)(2,1)S(1)}, bf16[40,1280]{1,0:T(8,128)(2,1)S(1)}, u32[]{:S(2)}, u32[]{:S(2)}) collective-permute-start(bf16[40,1280]{1,0:T(8,128)(2,1)S(1)} %get-tuple-element.15), channel_id=1, source_target_pairs={{0,2},{1,3},{2,0},{3,1},{4,6},{5,7},{6,4},{7,5},{8,10},{9,11},{10,... | collective-permute-start | bytes 307208 | tf_op jit(solution)/shard_map/ppermute | solution.py:404
  4.7 4.5 %collective-permute-start = (bf16[40,1280]{1,0:T(8,128)(2,1)S(1)}, bf16[40,1280]{1,0:T(8,128)(2,1)S(1)}, u32[]{:S(2)}, u32[]{:S(2)}) collective-permute-start(bf16[40,1280]{1,0:T(8,128)(2,1)S(1)} %get-tuple-element.14), channel_id=1, source_target_pairs={{0,1},{1,2},{2,3},{3,0},{4,5},{5,6},{6,7},{7,4},{8,9},{9,10},{10,1... | collective-permute-start | bytes 307208 | tf_op jit(solution)/shard_map/ppermute | solution.py:404
  9.3 4.9 %copy-start.1 = (s32[160]{0:T(256)S(1)}, s32[160]{0:T(256)}, u32[]{:S(2)}) copy-start(s32[160]{0:T(256)} %refs_4_.3) | copy-start | bytes 1924
  9.3 16.8 %collective-permute-start.3 = (bf16[160,256]{1,0:T(8,128)(2,1)S(1)}, bf16[160,256]{1,0:T(8,128)(2,1)S(1)}, u32[]{:S(2)}, u32[]{:S(2)}) collective-permute-start(bf16[160,256]{1,0:T(8,128)(2,1)S(1)} %pad_maximum_fusion), channel_id=1, source_target_pairs={{3,4},{4,3},{7,8},{8,7},{11,12},{12,11},{15,16},{16,15},{19,20},{2... | collective-permute-start | bytes 245768 | tf_op jit(solution)/shard_map/ppermute | solution.py:411
  38.1 4.6 %collective-permute-start.4 = (f32[2,40,128]{2,1,0:T(8,128)S(1)}, f32[2,40,128]{2,1,0:T(8,128)S(1)}, u32[]{:S(2)}, u32[]{:S(2)}) collective-permute-start(f32[2,40,128]{2,1,0:T(8,128)S(1)} %get-tuple-element.17), channel_id=1, source_target_pairs={{0,1},{1,2},{2,3},{3,0},{4,5},{5,6},{6,7},{7,4},{8,9},{9,10},{10,1... | collective-permute-start | bytes 122888 | tf_op jit(solution)/shard_map/ppermute | solution.py:422
  38.2 5.0 %collective-permute-start.5 = (f32[2,40,128]{2,1,0:T(8,128)S(1)}, f32[2,40,128]{2,1,0:T(8,128)S(1)}, u32[]{:S(2)}, u32[]{:S(2)}) collective-permute-start(f32[2,40,128]{2,1,0:T(8,128)S(1)} %get-tuple-element.18), channel_id=1, source_target_pairs={{0,2},{1,3},{2,0},{3,1},{4,6},{5,7},{6,4},{7,5},{8,10},{9,11},{10,... | collective-permute-start | bytes 122888 | tf_op jit(solution)/shard_map/ppermute | solution.py:422
  41.6 2.9 %collective-permute-start.6 = (f32[2,40,128]{2,1,0:T(8,128)S(1)}, f32[2,40,128]{2,1,0:T(8,128)S(1)}, u32[]{:S(2)}, u32[]{:S(2)}) collective-permute-start(f32[2,40,128]{2,1,0:T(8,128)S(1)} %get-tuple-element.19), channel_id=1, source_target_pairs={{0,3},{1,0},{2,1},{3,2},{4,7},{5,4},{6,5},{7,6},{8,11},{9,8},{10,9... | collective-permute-start | bytes 122888 | tf_op jit(solution)/shard_map/ppermute | solution.py:422

commit v3 on v2

--- a/solution.py
+++ b/solution.py
@@ -42,10 +42,14 @@
         self.right = [n_date - 1 - d for d in self.left]
         self.message = self.halves * 2 * PART + PART
 
-    def half(self, dest, slot):
+    def chunk(self, date):
+        odd = lax.rem(lax.axis_index("space"), 2) == 1
+        return jnp.where(odd, self.n_date - 1 - date, date)
+
+    def half(self, chunk, slot):
         if self.halves == 1:
             return 0
-        return jnp.where(dest <= self.left[-1], 1 - slot, slot)
+        return jnp.where(chunk <= self.left[-1], 1 - slot, slot)
 
 
 def pack_kernel(plan, x_ref, *refs):
@@ -74,17 +78,17 @@
             main[r][:, base + k * LANES : base + (k + 1) * LANES] = tile.astype(bf16)
 
     for r in range(n_date):
-        dest = lax.rem(me + r, n_date)
+        chunk = plan.chunk(lax.rem(me + r, n_date))
         for slot in range(plan.halves):
-            first = dest * plan.cols + plan.half(dest, slot) * plan.pix - RIM
+            first = chunk * plan.cols + plan.half(chunk, slot) * plan.pix - RIM
             low = jnp.maximum(0, -first)
             high = jnp.minimum(span, width - first)
             for part in range(2):
                 tiles = blank()
                 place(tiles, part, first, low, high)
                 put(r, (slot * 2 + part) * PART, tiles)
-        other = n_date - 1 - dest
-        after = dest >= plan.right[-1]
+        other = n_date - 1 - chunk
+        after = chunk >= plan.right[-1]
         first = jnp.where(after, other * plan.cols - RIM + width, (other + 1) * plan.cols - plan.pix - RIM - width)
         low = jnp.where(after, 0, jnp.maximum(0, -first))
         high = jnp.where(after, jnp.minimum(RIM, width - first), span)
@@ -115,8 +119,9 @@
             before_ref, refs = refs[0], refs[1:]
     outs, refs = refs[: n_date if last else 1], refs[n_date if last else 1 :]
     (s_ref, left_ref, high_ref, low_ref, a_ref, raw_ref, cr_ref, ci_ref, ca_ref,
-     mr_ref, mi_ref, ms_ref, y_ref, v_ref, ty_ref, tv_ref) = refs
+     mr_ref, mi_ref, ms_ref, y_ref, v_ref, ty_ref, tv_ref, a2_ref, raw2_ref) = refs
     me = lax.axis_index("date")
+    chunk = plan.chunk(me)
     nt = (((1,), (1,)), ((), ()))
     rows = [slice(b, b + 40) for b in range(0, DATES, 40)]
     sub = lax.broadcasted_iota(jnp.int32, (groups, LANES), 0)
@@ -141,16 +146,11 @@
     for r in range(n_date):
         s_ref[r * own : (r + 1) * own, :] = main[r][:, slot * 2 * PART : (slot + 1) * 2 * PART].astype(f32)
     if last:
-        is_left = me <= plan.left[-1]
-        is_edge = is_left | (me >= plan.right[-1])
-        edge = edge_ref[...].astype(f32)
-        raw_ref[0:DATES, 0:PART] = edge
-        raw_ref[DATES : 2 * DATES, 0:PART] = edge
-
-        @pl.when(is_edge)
+        is_left = chunk <= plan.left[-1]
+
+        @pl.when(is_left | (chunk >= plan.right[-1]))
         def _():
-            start = lax.rem(3 * n_date - 1 - 2 * me, n_date) * own
-            got = raw_ref[pl.ds(pl.multiple_of(start, 8), DATES), 0:PART]
+            got = edge_ref[...].astype(f32)
             at = lax.broadcasted_iota(jnp.int32, (1, PART), 1)
             col = at
             for _line in range(1, LINES):
@@ -158,23 +158,24 @@
             start = jnp.where(is_left, 0, span - RIM)
             valid = (col >= start) & (col < start + RIM) & (at < LINES * span)
             s_ref[:, 0:PART] = jnp.where(valid, s_ref[:, 0:PART] + got, s_ref[:, 0:PART])
-            back = jnp.where(is_left, PART - RIM, RIM)
-            got = pltpu.roll(got, back, 1)
+            got = pltpu.roll(got, jnp.where(is_left, PART - RIM, RIM), 1)
             s_ref[:, PART : 2 * PART] = jnp.where(valid, s_ref[:, PART : 2 * PART] + got, s_ref[:, PART : 2 * PART])
 
-    for r in range(n_date):
-        first = lax.rem(me + n_date - r, n_date) * own
-        for t in range(own):
-            day = days_ref[first + t].astype(f32)
-            y_ref[0, r * own + t : r * own + t + 1, :] = jnp.broadcast_to(day, (1, LANES))
-    days = y_ref[0]
-    grow = jnp.exp(days * (1.0 / taper_days))
-    decay = jnp.exp(days * (-1.0 / taper_days))
+    sub8 = lax.broadcasted_iota(jnp.int32, (8, LANES), 0)
+    for b in range(0, DATES, 8):
+        days = jnp.zeros((8, LANES), f32)
+        for t in range(8):
+            r, at = divmod(b + t, own)
+            day = days_ref[lax.rem(me + n_date - r, n_date) * own + at].astype(f32)
+            days = jnp.where(sub8 == t, day, days)
+        ty_ref[0, b : b + 8] = jnp.exp(days * (1.0 / taper_days))
+        ty_ref[1, b : b + 8] = jnp.exp(days * (-1.0 / taper_days))
     sr, si = s_ref[:, 0:PART], s_ref[:, PART : 2 * PART]
     left_ref[0:DATES, 0:PART] = sr.astype(bf16)
     left_ref[0:DATES, PART : 2 * PART] = si.astype(bf16)
     left_ref[DATES : 2 * DATES, 0:PART] = si.astype(bf16)
     left_ref[DATES : 2 * DATES, PART : 2 * PART] = (-sr).astype(bf16)
+    left_ref[:, 2 * PART :] = left_ref[:, : 2 * PART]
     intensity = sr * sr + si * si
     weight = 1.0 / (jnp.sum(intensity, axis=0, keepdims=True) / DATES + epsilon)
     for part, s in enumerate((sr, si)):
@@ -189,15 +190,15 @@
     power = lax.dot_general(high, rep, nt, preferred_element_type=f32)
     power = power + lax.dot_general(low, rep, nt, preferred_element_type=f32)
     root = lax.rsqrt(power + epsilon)
-    for k, t in enumerate((grow, decay)):
-        y = t * root
+    for k in range(2):
+        y = ty_ref[k] * root
         ty_ref[k] = y
         for b, row in enumerate(to_rows(y)):
             tv_ref[k, b : b + 1, :] = row
 
     unit = max(1, 16 // pix)
 
-    def build(first):
+    def build(first, a_ref):
         for p in range(per):
             for g in range(0, groups, unit):
                 for k, ref in enumerate((high_ref, low_ref)):
@@ -209,18 +210,19 @@
                         axis=0,
                     )
                     at = p * LANES + g * pix
-                    a_ref[k, at : at + 16, :] = rows16.astype(bf16) * mask
-
-    def multiply():
-        total = lax.dot_general(left_ref[...], a_ref[0], nt, preferred_element_type=f32)
-        raw_ref[...] = total + lax.dot_general(left_ref[...], a_ref[1], nt, preferred_element_type=f32)
-
-    def normalise(first):
+                    a_ref[at : at + 16, k * 2 * PART : (k + 1) * 2 * PART] = rows16.astype(bf16) * mask
+
+    def multiply(a_ref, raw_ref):
+        raw_ref[...] = lax.dot_general(left_ref[...], a_ref[...], nt, preferred_element_type=f32)
+
+    def normalise(first, raw_ref):
         for p in range(per):
             b = first + p
             grow_row = tv_ref[0, pl.ds(b, 1), :]
             decay_row = tv_ref[1, pl.ds(b, 1), :]
             at = slice(p * LANES, (p + 1) * LANES)
+            sum_r = jnp.zeros((8, LANES), f32)
+            sum_i = jnp.zeros((8, LANES), f32)
             for part in rows:
                 shifted = slice(part.start + DATES, part.stop + DATES)
                 factor = jnp.minimum(ty_ref[0, part] * decay_row, ty_ref[1, part] * grow_row)
@@ -230,18 +232,35 @@
                 cr_ref[b, part, :] = cr
                 ci_ref[b, part, :] = ci
                 ca_ref[b, part, :] = square * lax.rsqrt(jnp.maximum(square, 1e-36))
-                y_ref[0, part] += cr
-                y_ref[1, part] += ci
-
-    y_ref[...] = jnp.zeros(y_ref.shape, f32)
-
-    def coherence(step, carry):
-        build(step * per)
-        multiply()
-        normalise(step * per)
+                sum_r = sum_r + jnp.sum(cr.reshape(5, 8, LANES), axis=0)
+                sum_i = sum_i + jnp.sum(ci.reshape(5, 8, LANES), axis=0)
+            at = pl.ds(pl.multiple_of(b * groups, groups), groups)
+            y_ref[0, at] = jnp.sum(sum_r, axis=0, keepdims=True) * diag
+            y_ref[1, at] = -jnp.sum(sum_i, axis=0, keepdims=True) * diag
+
+
+    steps = blocks // per
+
+    def coherence(pair, carry):
+        step = 2 * pair
+        multiply(a2_ref, raw2_ref)
+        build((step + 2) * per, a_ref)
+        normalise(step * per, raw_ref)
+        multiply(a_ref, raw_ref)
+        build(jnp.minimum(step + 3, steps - 1) * per, a2_ref)
+        normalise((step + 1) * per, raw2_ref)
         return carry
 
-    lax.fori_loop(0, blocks // per, coherence, 0)
+    build(0, a_ref)
+    multiply(a_ref, raw_ref)
+    build(per, a2_ref)
+    lax.fori_loop(0, (steps - 1) // 2, coherence, 0)
+    if steps % 2 == 0:
+        multiply(a2_ref, raw2_ref)
+        normalise((steps - 2) * per, raw_ref)
+        normalise((steps - 1) * per, raw2_ref)
+    else:
+        normalise((steps - 1) * per, raw_ref)
 
     def unit_vector(scale):
         yr = group_sum(y_ref[0], pix) * scale
@@ -281,7 +300,7 @@
             set_row(b, jnp.sum(sum_r, axis=0, keepdims=True), jnp.sum(sum_i, axis=0, keepdims=True))
             return carry
 
-        lax.fori_loop(0, blocks, body, 0)
+        lax.fori_loop(0, blocks, body, 0, unroll=4 if blocks % 4 == 0 else 2)
 
     def set_row(b, vr, vi):
         tv_ref[0, pl.ds(b, 1), :] = vr
@@ -303,7 +322,7 @@
                     acc[2] + mi_ref[b, part, :] * v2,
                 )
 
-            k1, k2, k3 = lax.fori_loop(0, blocks, body, (zero, zero, zero), unroll=5)
+            k1, k2, k3 = lax.fori_loop(0, blocks, body, (zero, zero, zero), unroll=10)
             y_ref[0, part] = k1 - k3
             y_ref[1, part] = k1 + k2
 
@@ -343,7 +362,7 @@
         outs[0][...] = y_ref[0:2]
         return
     place = lax.rem(lax.broadcasted_iota(jnp.int32, (1, LANES), 1) // pix, plan.halves)
-    here = place == plan.half(me, slot)
+    here = place == plan.half(chunk, slot)
     for r in range(n_date):
         at = slice(r * own, (r + 1) * own)
         for k in range(2):
@@ -368,10 +387,10 @@
         out_specs=[VMEM] * len(shapes),
         scratch_shapes=[
             samples,
-            pltpu.VMEM((2 * DATES, 2 * PART), bf16),
+            pltpu.VMEM((2 * DATES, 4 * PART), bf16),
             samples,
             samples,
-            pltpu.VMEM((2, plan.per * LANES, 2 * PART), bf16),
+            pltpu.VMEM((plan.per * LANES, 4 * PART), bf16),
             pltpu.VMEM((2 * DATES, PART), f32),
         ]
         + [matrix] * 6
@@ -380,6 +399,8 @@
             pltpu.VMEM((3, plan.blocks, LANES), f32),
             pltpu.VMEM((2, DATES, LANES), f32),
             pltpu.VMEM((2, plan.blocks, LANES), f32),
+            pltpu.VMEM((plan.per * LANES, 4 * PART), bf16),
+            pltpu.VMEM((2 * DATES, PART), f32),
         ],
         compiler_params=pltpu.CompilerParams(vmem_limit_bytes=24 * 2**20),
     )(*main, days, *more)
@@ -404,8 +425,8 @@
         main[r] = lax.ppermute(main[r], "date", [(i, (i + r) % n_date) for i in range(n_date)])
     swap = []
     for s in range(n_space - 1):
-        for d in plan.left:
-            before, after = s * n_date + n_date - 1 - d, (s + 1) * n_date + d
+        for d in plan.right if s % 2 == 0 else plan.left:
+            before, after = s * n_date + d, (s + 1) * n_date + d
             swap += [(before, after), (after, before)]
     edge = jnp.concatenate([m[:, plan.halves * 2 * PART :] for m in main], axis=0)
     edge = lax.ppermute(edge, ("space", "date"), swap)
@@ -420,7 +441,7 @@
     result = out[0]
     for r in range(1, n_date):
         piece = lax.ppermute(out[r], "date", [(i, (i - r) % n_date) for i in range(n_date)])
-        result = jnp.where(lane_owner == lax.rem(me + r, n_date), piece, result)
+        result = jnp.where(lane_owner == plan.chunk(lax.rem(me + r, n_date)), piece, result)
     return result
 
 

time: 45.3 us -> 41.5 us (0.916)
  the two profiles are of different devices: /device:TPU:1 before, /device:TPU:11 now
where the time goes in v3:
time: 41.5 us; the launch traced here: 41.4 us
  Pallas kernels  21.1 us (51%)
  starting transfers between devices  11.1 us (27%)
  waiting for transfers between devices  7.58 us (18%)
  local copies, waits for them, and re-layouts  0.92 us (2%)
  other arithmetic  0.65 us (2%)
    pallas_call x2, Pallas kernels, link(): pl.pallas_call(functools.partial(link_kernel, plan, slot), out_shape=shap...  20.5 us
    ppermute x3, starting transfers between devices, local(): lax.ppermute(out[r], 'date', [(i, (i - r) % n_date) for i in range(n_date)])  6.74 us
    ppermute x3, waiting for transfers between devices, local(): lax.ppermute(out[r], 'date', [(i, (i - r) % n_date) for i in range(n_date)])  4.2 us
    ppermute x3, starting transfers between devices, local(): lax.ppermute(main[r], 'date', [(i, (i + r) % n_date) for i in range(n_dat...  3.66 us
    ppermute x3, waiting for transfers between devices, local(): lax.ppermute(main[r], 'date', [(i, (i + r) % n_date) for i in range(n_dat...  3.38 us
    unnamed x4, local copies, waits for them, and re-layouts  0.91 us
  transfers between devices with their start and end apart: 7, of which 6 were waited for; matrix products, arithmetic and copies ran while one was open for 0% of the time, Pallas kernels for 25%

profile of v3, /device:TPU:11, one launch (start us, length us, event | category | flops | bytes accessed | tf_op | source)
XLA Modules:
  0.0 41.4 jit_solution(7773610532864657876)
XLA Ops:
  0.0 0.0 copy-start
  0.0 0.9 %copy-done = bf16[2,40,7,128]{3,1,2,0:T(8,128)(2,1)S(1)} copy-done((bf16[2,40,7,128]{3,1,2,0:T(8,128)(2,1)S(1)}, bf16[2,40,7,128]{3,1,2,0:T(8,128)(2,1)}, u32[]{:S(2)}) %copy-start) | copy-done | bytes 143384
  0.9 0.6 %shard_map.28 = (bf16[40,1280]{1,0:T(8,128)(2,1)S(1)}, bf16[40,1280]{1,0:T(8,128)(2,1)S(1)}, bf16[40,1280]{1,0:T(8,128)(2,1)S(1)}, bf16[40,1280]{1,0:T(8,128)(2,1)S(1)}) custom-call(bf16[2,7,40,128]{3,2,1,0:T(8,128)(2,1)S(1)} %bitcast.1), custom_call_target="tpu_custom_call" | custom-call | tf_op jit(solution)/shard_map/pallas_call | solution.py:415
  1.5 0.3 collective-permute-start.2
  1.8 1.2 %collective-permute-start.1 = (bf16[40,1280]{1,0:T(8,128)(2,1)S(1)}, bf16[40,1280]{1,0:T(8,128)(2,1)S(1)}, u32[]{:S(2)}, u32[]{:S(2)}) collective-permute-start(bf16[40,1280]{1,0:T(8,128)(2,1)S(1)} %get-tuple-element.15), channel_id=1, source_target_pairs={{0,2},{1,3},{2,0},{3,1},{4,6},{5,7},{6,4},{7,5},{8,10},{9,11},{10,... | collective-permute-start | bytes 307208 | tf_op jit(solution)/shard_map/ppermute | solution.py:425
  3.0 2.1 %collective-permute-start = (bf16[40,1280]{1,0:T(8,128)(2,1)S(1)}, bf16[40,1280]{1,0:T(8,128)(2,1)S(1)}, u32[]{:S(2)}, u32[]{:S(2)}) collective-permute-start(bf16[40,1280]{1,0:T(8,128)(2,1)S(1)} %get-tuple-element.14), channel_id=1, source_target_pairs={{0,1},{1,2},{2,3},{3,0},{4,5},{5,6},{6,7},{7,4},{8,9},{9,10},{10,1... | collective-permute-start | bytes 307208 | tf_op jit(solution)/shard_map/ppermute | solution.py:425
  5.1 0.9 %collective-permute-done.2.refs_3_ = bf16[40,1280]{1,0:T(8,128)(2,1)S(1)} collective-permute-done((bf16[40,1280]{1,0:T(8,128)(2,1)S(1)}, bf16[40,1280]{1,0:T(8,128)(2,1)S(1)}, u32[]{:S(2)}, u32[]{:S(2)}) %collective-permute-start.2) | collective-permute-done | bytes 102432 | tf_op jit(solution)/shard_map/ppermute | solution.py:425
  6.0 1.7 %collective-permute-done.1.refs_2_ = bf16[40,1280]{1,0:T(8,128)(2,1)S(1)} collective-permute-done((bf16[40,1280]{1,0:T(8,128)(2,1)S(1)}, bf16[40,1280]{1,0:T(8,128)(2,1)S(1)}, u32[]{:S(2)}, u32[]{:S(2)}) %collective-permute-start.1) | collective-permute-done | bytes 102432 | tf_op jit(solution)/shard_map/ppermute | solution.py:425
  7.8 0.7 %collective-permute-done.refs_1_ = bf16[40,1280]{1,0:T(8,128)(2,1)S(1)} collective-permute-done((bf16[40,1280]{1,0:T(8,128)(2,1)S(1)}, bf16[40,1280]{1,0:T(8,128)(2,1)S(1)}, u32[]{:S(2)}, u32[]{:S(2)}) %collective-permute-start) | collective-permute-done | bytes 102432 | tf_op jit(solution)/shard_map/ppermute | solution.py:425
  8.5 0.0 copy-start.1
  8.5 0.7 %collective-permute-start.3 = (bf16[160,256]{1,0:T(8,128)(2,1)S(1)}, bf16[160,256]{1,0:T(8,128)(2,1)S(1)}, u32[]{:S(2)}, u32[]{:S(2)}) collective-permute-start(bf16[160,256]{1,0:T(8,128)(2,1)S(1)} %pad_maximum_fusion), channel_id=1, source_target_pairs={{3,7},{7,3},{4,8},{8,4},{11,15},{15,11},{12,16},{16,12},{19,23},{2... | collective-permute-start | bytes 245768 | tf_op jit(solution)/shard_map/ppermute | solution.py:432
  9.2 0.0 copy-done.1
  9.2 10.3 %shard_map.29.refs_6_ = f32[2,160,128]{2,1,0:T(8,128)S(1)} custom-call(bf16[40,1280]{1,0:T(8,128)(2,1)S(1)} %get-tuple-element.13.refs_0_, bf16[40,1280]{1,0:T(8,128)(2,1)S(1)} %collective-permute-done.refs_1_, bf16[40,1280]{1,0:T(8,128)(2,1)S(1)} %collective-permute-done.1.refs_2_, bf16[40,1280]{1,0:T(8,128)(2,1)S(1)} %collective-permute-done.2.refs_3_, ...), custom_call_target="tpu_custom_call" | custom-call | tf_op jit(solution)/shard_map/pallas_call | solution.py:383
  19.5 0.0 collective-permute-done.3.refs_5_
  19.5 10.3 %shard_map.30 = (f32[2,40,128]{2,1,0:T(8,128)S(1)}, f32[2,40,128]{2,1,0:T(8,128)S(1)}, f32[2,40,128]{2,1,0:T(8,128)S(1)}, f32[2,40,128]{2,1,0:T(8,128)S(1)}) custom-call(bf16[40,1280]{1,0:T(8,128)(2,1)S(1)} %get-tuple-element.13.refs_0_, bf16[40,1280]{1,0:T(8,128)(2,1)S(1)} %collective-permute-done.refs_1_, ...), custom_call_target="tpu_custom_call" | custom-call | tf_op jit(solution)/shard_map/pallas_call | solution.py:383
  29.8 1.2 %collective-permute-start.4 = (f32[2,40,128]{2,1,0:T(8,128)S(1)}, f32[2,40,128]{2,1,0:T(8,128)S(1)}, u32[]{:S(2)}, u32[]{:S(2)}) collective-permute-start(f32[2,40,128]{2,1,0:T(8,128)S(1)} %get-tuple-element.17), channel_id=1, source_target_pairs={{0,1},{1,2},{2,3},{3,0},{4,5},{5,6},{6,7},{7,4},{8,9},{9,10},{10,1... | collective-permute-start | bytes 122888 | tf_op jit(solution)/shard_map/ppermute | solution.py:443
  31.0 5.6 %collective-permute-start.5 = (f32[2,40,128]{2,1,0:T(8,128)S(1)}, f32[2,40,128]{2,1,0:T(8,128)S(1)}, u32[]{:S(2)}, u32[]{:S(2)}) collective-permute-start(f32[2,40,128]{2,1,0:T(8,128)S(1)} %get-tuple-element.18), channel_id=1, source_target_pairs={{0,2},{1,3},{2,0},{3,1},{4,6},{5,7},{6,4},{7,5},{8,10},{9,11},{10,... | collective-permute-start | bytes 122888 | tf_op jit(solution)/shard_map/ppermute | solution.py:443
  36.6 0.0 collective-permute-start.6
  36.6 0.2 collective-permute-done.4
  36.8 1.2 %collective-permute-done.5 = f32[2,40,128]{2,1,0:T(8,128)S(1)} collective-permute-done((f32[2,40,128]{2,1,0:T(8,128)S(1)}, f32[2,40,128]{2,1,0:T(8,128)S(1)}, u32[]{:S(2)}, u32[]{:S(2)}) %collective-permute-start.5) | collective-permute-done | bytes 40992 | tf_op jit(solution)/shard_map/ppermute | solution.py:443
  37.9 2.8 %collective-permute-done.6 = f32[2,40,128]{2,1,0:T(8,128)S(1)} collective-permute-done((f32[2,40,128]{2,1,0:T(8,128)S(1)}, f32[2,40,128]{2,1,0:T(8,128)S(1)}, u32[]{:S(2)}, u32[]{:S(2)}) %collective-permute-start.6) | collective-permute-done | bytes 40992 | tf_op jit(solution)/shard_map/ppermute | solution.py:443
  40.8 0.6 %select_select_fusion = f32[2,40,128]{2,1,0:T(8,128)} fusion(f32[2,40,128]{2,1,0:T(8,128)S(1)} %collective-permute-done.4, f32[2,40,128]{2,1,0:T(8,128)S(1)} %collective-permute-done.5, f32[2,40,128]{2,1,0:T(8,128)S(1)} %collective-permute-done.6, f32[2,40,128]{2,1,0:T(8,128)S(1)} %get-tuple-element.20, pred[128]{0:T(512)(128)(4,1)S(1)} %get-tuple-element.21, ...), kind=kLoop, calls=%fused_computation.1 | loop fusion | flops 30720 | bytes 205184 | tf_op jit(solution)/shard_map/jit(_where)/select_n | solution.py:444
  (7 shorter events, 0.0 us)
Async XLA Ops:
  0.0 0.9 %copy-start = (bf16[2,40,7,128]{3,1,2,0:T(8,128)(2,1)S(1)}, bf16[2,40,7,128]{3,1,2,0:T(8,128)(2,1)}, u32[]{:S(2)}) copy-start(bf16[2,40,7,128]{3,1,2,0:T(8,128)(2,1)} %param.2) | copy-start | bytes 430084
  1.5 4.6 %collective-permute-start.2 = (bf16[40,1280]{1,0:T(8,128)(2,1)S(1)}, bf16[40,1280]{1,0:T(8,128)(2,1)S(1)}, u32[]{:S(2)}, u32[]{:S(2)}) collective-permute-start(bf16[40,1280]{1,0:T(8,128)(2,1)S(1)} %get-tuple-element.16), channel_id=1, source_target_pairs={{0,3},{1,0},{2,1},{3,2},{4,7},{5,4},{6,5},{7,6},{8,11},{9,8},{10,9... | collective-permute-start | bytes 307208 | tf_op jit(solution)/shard_map/ppermute | solution.py:425
  1.8 6.0 %collective-permute-start.1 = (bf16[40,1280]{1,0:T(8,128)(2,1)S(1)}, bf16[40,1280]{1,0:T(8,128)(2,1)S(1)}, u32[]{:S(2)}, u32[]{:S(2)}) collective-permute-start(bf16[40,1280]{1,0:T(8,128)(2,1)S(1)} %get-tuple-element.15), channel_id=1, source_target_pairs={{0,2},{1,3},{2,0},{3,1},{4,6},{5,7},{6,4},{7,5},{8,10},{9,11},{10,... | collective-permute-start | bytes 307208 | tf_op jit(solution)/shard_map/ppermute | solution.py:425
  3.0 5.5 %collective-permute-start = (bf16[40,1280]{1,0:T(8,128)(2,1)S(1)}, bf16[40,1280]{1,0:T(8,128)(2,1)S(1)}, u32[]{:S(2)}, u32[]{:S(2)}) collective-permute-start(bf16[40,1280]{1,0:T(8,128)(2,1)S(1)} %get-tuple-element.14), channel_id=1, source_target_pairs={{0,1},{1,2},{2,3},{3,0},{4,5},{5,6},{6,7},{7,4},{8,9},{9,10},{10,1... | collective-permute-start | bytes 307208 | tf_op jit(solution)/shard_map/ppermute | solution.py:425
  8.5 0.7 %copy-start.1 = (s32[160]{0:T(256)S(1)}, s32[160]{0:T(256)}, u32[]{:S(2)}) copy-start(s32[160]{0:T(256)} %refs_4_.3) | copy-start | bytes 1924
  8.5 11.0 %collective-permute-start.3 = (bf16[160,256]{1,0:T(8,128)(2,1)S(1)}, bf16[160,256]{1,0:T(8,128)(2,1)S(1)}, u32[]{:S(2)}, u32[]{:S(2)}) collective-permute-start(bf16[160,256]{1,0:T(8,128)(2,1)S(1)} %pad_maximum_fusion), channel_id=1, source_target_pairs={{3,7},{7,3},{4,8},{8,4},{11,15},{15,11},{12,16},{16,12},{19,23},{2... | collective-permute-start | bytes 245768 | tf_op jit(solution)/shard_map/ppermute | solution.py:432
  29.8 6.9 %collective-permute-start.4 = (f32[2,40,128]{2,1,0:T(8,128)S(1)}, f32[2,40,128]{2,1,0:T(8,128)S(1)}, u32[]{:S(2)}, u32[]{:S(2)}) collective-permute-start(f32[2,40,128]{2,1,0:T(8,128)S(1)} %get-tuple-element.17), channel_id=1, source_target_pairs={{0,1},{1,2},{2,3},{3,0},{4,5},{5,6},{6,7},{7,4},{8,9},{9,10},{10,1... | collective-permute-start | bytes 122888 | tf_op jit(solution)/shard_map/ppermute | solution.py:443
  31.0 6.9 %collective-permute-start.5 = (f32[2,40,128]{2,1,0:T(8,128)S(1)}, f32[2,40,128]{2,1,0:T(8,128)S(1)}, u32[]{:S(2)}, u32[]{:S(2)}) collective-permute-start(f32[2,40,128]{2,1,0:T(8,128)S(1)} %get-tuple-element.18), channel_id=1, source_target_pairs={{0,2},{1,3},{2,0},{3,1},{4,6},{5,7},{6,4},{7,5},{8,10},{9,11},{10,... | collective-permute-start | bytes 122888 | tf_op jit(solution)/shard_map/ppermute | solution.py:443
  36.6 4.2 %collective-permute-start.6 = (f32[2,40,128]{2,1,0:T(8,128)S(1)}, f32[2,40,128]{2,1,0:T(8,128)S(1)}, u32[]{:S(2)}, u32[]{:S(2)}) collective-permute-start(f32[2,40,128]{2,1,0:T(8,128)S(1)} %get-tuple-element.19), channel_id=1, source_target_pairs={{0,3},{1,0},{2,1},{3,2},{4,7},{5,4},{6,5},{7,6},{8,11},{9,8},{10,9... | collective-permute-start | bytes 122888 | tf_op jit(solution)/shard_map/ppermute | solution.py:443

commit v4 on v3

--- a/solution.py
+++ b/solution.py
@@ -40,63 +40,90 @@
         self.span = self.pix + 2 * RIM
         self.left = [d for d in range(n_date) if d * self.cols < RIM]
         self.right = [n_date - 1 - d for d in self.left]
-        self.message = self.halves * 2 * PART + PART
+        if self.halves == 2:
+            self.pieces = [(0, self.pix), (LINES * self.pix, 2 * RIM), (PART, self.pix)]
+            self.tail, self.stride = PART, PART + LANES
+        else:
+            self.pieces = [(0, self.span)]
+            self.tail, self.stride = 0, PART
+        self.tail_width = self.pieces[-1][1]
+        self.tail_lanes = self.stride - self.tail
 
     def chunk(self, date):
         odd = lax.rem(lax.axis_index("space"), 2) == 1
         return jnp.where(odd, self.n_date - 1 - date, date)
 
+    def swapped(self, chunk):
+        return chunk <= self.left[-1]
+
     def half(self, chunk, slot):
         if self.halves == 1:
             return 0
-        return jnp.where(chunk <= self.left[-1], 1 - slot, slot)
+        return jnp.where(self.swapped(chunk), 1 - slot, slot)
 
 
 def pack_kernel(plan, x_ref, *refs):
-    n_date, width, span = plan.n_date, plan.width, plan.span
+    n_date, width = plan.n_date, plan.width
     main, plane = refs[:n_date], refs[n_date]
     me = lax.axis_index("date")
     plane[...] = x_ref[...].astype(f32)
     lane = lax.broadcasted_iota(jnp.int32, (1, LANES), 1)
-    tile_count = PART // LANES
-
-    def place(tiles, part, first, low, high, lead=0):
+    tile_count = plan.stride // LANES
+
+    def place(tiles, part, base, wide, first, low, high):
         for line in range(LINES):
-            start = line * span
-            shift = lax.rem(start + lead - first + 4 * LANES, LANES)
-            moved = pltpu.roll(plane[part, line], shift, 1)
+            start = base + line * wide
+            moved = pltpu.roll(plane[part, line], lax.rem(start - first + 8 * LANES, LANES), 1)
             for tile in range(tile_count):
-                if start - 16 < (tile + 1) * LANES and start + span + 16 > tile * LANES:
-                    at = lane + (tile * LANES - start) - lead
+                if start < (tile + 1) * LANES and start + wide > tile * LANES:
+                    at = lane + (tile * LANES - start)
                     tiles[tile] = jnp.where((at >= low) & (at < high), moved, tiles[tile])
-
-    def blank():
-        return [jnp.zeros((plan.own, LANES), f32) for _ in range(tile_count)]
-
-    def put(r, base, tiles):
-        for k, tile in enumerate(tiles):
-            main[r][:, base + k * LANES : base + (k + 1) * LANES] = tile.astype(bf16)
 
     for r in range(n_date):
         chunk = plan.chunk(lax.rem(me + r, n_date))
-        for slot in range(plan.halves):
-            first = chunk * plan.cols + plan.half(chunk, slot) * plan.pix - RIM
-            low = jnp.maximum(0, -first)
-            high = jnp.minimum(span, width - first)
-            for part in range(2):
-                tiles = blank()
-                place(tiles, part, first, low, high)
-                put(r, (slot * 2 + part) * PART, tiles)
-        other = n_date - 1 - chunk
-        after = chunk >= plan.right[-1]
-        first = jnp.where(after, other * plan.cols - RIM + width, (other + 1) * plan.cols - plan.pix - RIM - width)
-        low = jnp.where(after, 0, jnp.maximum(0, -first))
-        high = jnp.where(after, jnp.minimum(RIM, width - first), span)
-        low = jnp.where(after, low, jnp.maximum(low, span - RIM))
-        tiles = blank()
-        place(tiles, 0, first, low, high)
-        place(tiles, 1, first, low, high, jnp.where(after, RIM, -RIM))
-        put(r, plan.halves * 2 * PART, tiles)
+        swapped = plan.swapped(chunk)
+        window = chunk * plan.cols - RIM
+        far = window + plan.span
+        for part in range(2):
+            tiles = [jnp.zeros((plan.own, LANES), f32) for _ in range(tile_count)]
+            for k, (base, wide) in enumerate(plan.pieces):
+                if len(plan.pieces) == 1:
+                    first = window
+                elif k == 1:
+                    first = window + plan.pix
+                else:
+                    first = jnp.where(swapped == (k == 2), window, far)
+                low, high = jnp.maximum(0, -first), jnp.minimum(wide, width - first)
+                place(tiles, part, base, wide, first, low, high)
+            base, wide = plan.pieces[-1]
+            place(
+                tiles,
+                part,
+                base,
+                wide,
+                jnp.where(swapped, 0, width - wide),
+                jnp.where(swapped, 0, jnp.minimum(wide, width - first)),
+                jnp.where(swapped, -first, wide),
+            )
+            for k, tile in enumerate(tiles):
+                at = part * plan.stride + k * LANES
+                main[r][:, at : at + LANES] = tile.astype(bf16)
+
+
+def unpack_kernel(plan, *refs):
+    n_date, own = plan.n_date, plan.own
+    pieces, out_ref = refs[:n_date], refs[n_date]
+    me = lax.axis_index("date")
+    region = LANES // 4
+    owner = lax.broadcasted_iota(jnp.int32, (1, LANES), 1) // plan.cols
+    for quarter in range(4):
+        value = jnp.zeros((own // 2, LANES), f32)
+        for r in range(n_date):
+            chunk = plan.chunk(lax.rem(me + r, n_date))
+            shift = lax.rem(chunk * plan.cols // region + 4 - quarter, 4) * region
+            value = jnp.where(owner == chunk, pltpu.roll(pieces[r][...], shift, 1), value)
+        start = quarter % 2 * (own // 2)
+        out_ref[quarter // 2, start : start + own // 2, :] = value
 
 
 def group_sum(x, pix):
@@ -128,13 +155,21 @@
     lane = lax.broadcasted_iota(jnp.int32, (groups, LANES), 1)
     diag = jnp.where(lane // pix == sub, 1.0, 0.0).astype(f32)
 
-    column = lax.broadcasted_iota(jnp.int32, (16, PART), 1)
-    for _line in range(1, LINES):
-        column = jnp.where(column >= span, column - span, column)
     spot = lax.broadcasted_iota(jnp.int32, (16, PART), 1)
+    if plan.halves == 1:
+        layout = [(0, span, 0)]
+    elif last:
+        layout = [(0, 2 * RIM, plan.pix), (plan.tail - plan.pieces[1][0], pix, jnp.where(plan.swapped(chunk), 0, span))]
+    else:
+        layout = [(0, pix, jnp.where(plan.swapped(chunk), span, 0)), (plan.pieces[1][0], 2 * RIM, plan.pix)]
+    column = jnp.full((16, PART), -LANES, jnp.int32)
+    for base, wide, col in layout:
+        for line in range(LINES):
+            start = base + line * wide
+            column = jnp.where((spot >= start) & (spot < start + wide), spot - start + col, column)
+    column = column - plan.half(chunk, slot) * pix
     offset = column - lax.rem(lax.broadcasted_iota(jnp.int32, (16, PART), 0), pix)
-    inside = (offset >= 0) & (offset <= 2 * RIM) & (spot < LINES * span)
-    inside = jnp.where(inside, 1.0, 0.0).astype(f32)
+    inside = jnp.where((offset >= 0) & (offset <= 2 * RIM), 1.0, 0.0).astype(f32)
     mask = jnp.concatenate([inside, inside], axis=1).astype(bf16)
     rep = jnp.concatenate([inside] * (LANES // 16), axis=0).astype(bf16)
 
@@ -144,22 +179,34 @@
         ]
 
     for r in range(n_date):
-        s_ref[r * own : (r + 1) * own, :] = main[r][:, slot * 2 * PART : (slot + 1) * 2 * PART].astype(f32)
+        for part in range(2):
+            s = main[r][:, part * plan.stride : (part + 1) * plan.stride].astype(f32)
+            if slot:
+                s = pltpu.roll(s, plan.stride - plan.pieces[1][0], 1)
+            s_ref[r * own : (r + 1) * own, part * PART : (part + 1) * PART] = s[:, 0:PART]
     if last:
-        is_left = chunk <= plan.left[-1]
-
-        @pl.when(is_left | (chunk >= plan.right[-1]))
+        is_left = plan.swapped(chunk)
+        depth = jnp.where(is_left, chunk, n_date - 1 - chunk)
+        missing = RIM - depth * plan.cols
+        wide = plan.tail_width
+        base = plan.tail - plan.pieces[1][0] if plan.halves == 2 else 0
+
+        @pl.when(missing > 0)
         def _():
-            got = edge_ref[...].astype(f32)
-            at = lax.broadcasted_iota(jnp.int32, (1, PART), 1)
+            at = lax.broadcasted_iota(jnp.int32, (1, PART), 1) - base
             col = at
             for _line in range(1, LINES):
-                col = jnp.where(col >= span, col - span, col)
-            start = jnp.where(is_left, 0, span - RIM)
-            valid = (col >= start) & (col < start + RIM) & (at < LINES * span)
-            s_ref[:, 0:PART] = jnp.where(valid, s_ref[:, 0:PART] + got, s_ref[:, 0:PART])
-            got = pltpu.roll(got, jnp.where(is_left, PART - RIM, RIM), 1)
-            s_ref[:, PART : 2 * PART] = jnp.where(valid, s_ref[:, PART : 2 * PART] + got, s_ref[:, PART : 2 * PART])
+                col = jnp.where(col >= wide, col - wide, col)
+            low = jnp.where(is_left, 0, wide - missing)
+            valid = (col >= low) & (col < low + missing) & (at >= 0) & (at < LINES * wide)
+            shift = jnp.where(is_left, missing - wide, wide - missing) + base
+            for part in range(2):
+                got = edge_ref[:, part * plan.tail_lanes : (part + 1) * plan.tail_lanes].astype(f32)
+                if plan.tail_lanes < PART:
+                    got = jnp.concatenate([got, jnp.zeros((DATES, PART - plan.tail_lanes), f32)], axis=1)
+                got = pltpu.roll(got, lax.rem(shift + PART, PART), 1)
+                at_part = slice(part * PART, (part + 1) * PART)
+                s_ref[:, at_part] = jnp.where(valid, got, s_ref[:, at_part])
 
     sub8 = lax.broadcasted_iota(jnp.int32, (8, LANES), 0)
     for b in range(0, DATES, 8):
@@ -361,15 +408,19 @@
     if not last:
         outs[0][...] = y_ref[0:2]
         return
-    place = lax.rem(lax.broadcasted_iota(jnp.int32, (1, LANES), 1) // pix, plan.halves)
-    here = place == plan.half(chunk, slot)
+    lane_row = lax.broadcasted_iota(jnp.int32, (1, LANES), 1)
+    here = lax.rem(lane_row // pix, plan.halves) == plan.half(chunk, slot)
+    quarter = lane_row // (LANES // 4)
     for r in range(n_date):
-        at = slice(r * own, (r + 1) * own)
-        for k in range(2):
-            value = y_ref[k, at]
+        value = None
+        for q in range(4):
+            start = r * own + q % 2 * (own // 2)
+            at = slice(start, start + own // 2)
+            piece = y_ref[q // 2, at]
             if slot:
-                value = jnp.where(here, value, before_ref[k, at])
-            outs[r][k] = value
+                piece = jnp.where(here, piece, before_ref[q // 2, at])
+            value = piece if value is None else jnp.where(quarter == q, piece, value)
+        outs[r][...] = value
 
 
 def link(plan, slot, main, days, *more):
@@ -377,7 +428,7 @@
     matrix = pltpu.VMEM((plan.blocks, DATES, LANES), f32)
     samples = pltpu.VMEM((DATES, 2 * PART), f32)
     if last:
-        shapes = [jax.ShapeDtypeStruct((2, plan.own, LANES), f32)] * plan.n_date
+        shapes = [jax.ShapeDtypeStruct((plan.own // 2, LANES), f32)] * plan.n_date
     else:
         shapes = [jax.ShapeDtypeStruct((2, DATES, LANES), f32)]
     return pl.pallas_call(
@@ -410,11 +461,10 @@
     n_date, n_space = lax.axis_size("date"), lax.axis_size("space")
     plan = Plan(acquisitions.shape, n_date)
     own = plan.own
-    me = lax.axis_index("date")
 
     main = pl.pallas_call(
         functools.partial(pack_kernel, plan),
-        out_shape=[jax.ShapeDtypeStruct((own, plan.message), bf16)] * n_date,
+        out_shape=[jax.ShapeDtypeStruct((own, 2 * plan.stride), bf16)] * n_date,
         in_specs=[VMEM],
         out_specs=[VMEM] * n_date,
         scratch_shapes=[pltpu.VMEM((2, LINES, own, LANES), f32)],
@@ -428,7 +478,13 @@
         for d in plan.right if s % 2 == 0 else plan.left:
             before, after = s * n_date + d, (s + 1) * n_date + d
             swap += [(before, after), (after, before)]
-    edge = jnp.concatenate([m[:, plan.halves * 2 * PART :] for m in main], axis=0)
+    edge = jnp.concatenate(
+        [
+            jnp.concatenate([m[:, k * plan.stride + plan.tail : (k + 1) * plan.stride] for k in range(2)], axis=1)
+            for m in main
+        ],
+        axis=0,
+    )
     edge = lax.ppermute(edge, ("space", "date"), swap)
 
     if plan.halves == 1:
@@ -437,12 +493,16 @@
         (before,) = link(plan, 0, main, acquisition_day)
         out = link(plan, 1, main, acquisition_day, edge, before)
 
-    lane_owner = jnp.arange(LANES) // plan.cols
-    result = out[0]
+    pieces = [out[0]]
     for r in range(1, n_date):
-        piece = lax.ppermute(out[r], "date", [(i, (i - r) % n_date) for i in range(n_date)])
-        result = jnp.where(lane_owner == plan.chunk(lax.rem(me + r, n_date)), piece, result)
-    return result
+        pieces.append(lax.ppermute(out[r], "date", [(i, (i - r) % n_date) for i in range(n_date)]))
+    return pl.pallas_call(
+        functools.partial(unpack_kernel, plan),
+        out_shape=jax.ShapeDtypeStruct((2, own, plan.width), f32),
+        in_specs=[VMEM] * n_date,
+        out_specs=VMEM,
+        compiler_params=pltpu.CompilerParams(vmem_limit_bytes=24 * 2**20),
+    )(*pieces)
 
 
 def solution(mesh):

time: 41.5 us -> 41 us (0.988)
  the two profiles are of different devices: /device:TPU:11 before, /device:TPU:0 now
where the time goes in v4:
time: 41 us; the launch traced here: 40.8 us
  Pallas kernels  22.2 us (54%)
  starting transfers between devices  10.9 us (27%)
  waiting for transfers between devices  6.73 us (16%)
  local copies, waits for them, and re-layouts  0.92 us (2%)
    pallas_call x2, Pallas kernels, link(): pl.pallas_call(functools.partial(link_kernel, plan, slot), out_shape=shap...  20.8 us
    ppermute x3, starting transfers between devices, local(): lax.ppermute(main[r], 'date', [(i, (i + r) % n_date) for i in range(n_dat...  5.94 us
    ppermute x3, starting transfers between devices, local(): lax.ppermute(out[r], 'date', [(i, (i - r) % n_date) for i in range(n_date)])  4.27 us
    ppermute x3, waiting for transfers between devices, local(): lax.ppermute(out[r], 'date', [(i, (i - r) % n_date) for i in range(n_date)])  3.95 us
    ppermute x3, waiting for transfers between devices, local(): lax.ppermute(main[r], 'date', [(i, (i + r) % n_date) for i in range(n_dat...  2.78 us
    unnamed x4, local copies, waits for them, and re-layouts  0.91 us
  transfers between devices with their start and end apart: 7, of which 6 were waited for; matrix products, arithmetic and copies ran while one was open for 0% of the time, Pallas kernels for 25%

profile of v4, /device:TPU:0, one launch (start us, length us, event | category | flops | bytes accessed | tf_op | source)
XLA Modules:
  0.0 40.8 jit_solution(764854468332825727)
XLA Ops:
  0.0 0.0 copy-start
  0.0 0.9 %copy-done = bf16[2,40,7,128]{3,1,2,0:T(8,128)(2,1)S(1)} copy-done((bf16[2,40,7,128]{3,1,2,0:T(8,128)(2,1)S(1)}, bf16[2,40,7,128]{3,1,2,0:T(8,128)(2,1)}, u32[]{:S(2)}) %copy-start) | copy-done | bytes 143384
  0.9 0.7 %shard_map.28 = (bf16[40,768]{1,0:T(8,128)(2,1)S(1)}, bf16[40,768]{1,0:T(8,128)(2,1)S(1)}, bf16[40,768]{1,0:T(8,128)(2,1)S(1)}, bf16[40,768]{1,0:T(8,128)(2,1)S(1)}) custom-call(bf16[2,7,40,128]{3,2,1,0:T(8,128)(2,1)S(1)} %bitcast.1), custom_call_target="tpu_custom_call" | custom-call | tf_op jit(solution)/shard_map/pallas_call | solution.py:465
  1.6 3.0 %collective-permute-start = (bf16[40,768]{1,0:T(8,128)(2,1)S(1)}, bf16[40,768]{1,0:T(8,128)(2,1)S(1)}, u32[]{:S(2)}, u32[]{:S(2)}) collective-permute-start(bf16[40,768]{1,0:T(8,128)(2,1)S(1)} %get-tuple-element.14), channel_id=1, source_target_pairs={{0,1},{1,2},{2,3},{3,0},{4,5},{5,6},{6,7},{7,4},{8,9},{9,10},{10,1... | collective-permute-start | bytes 184328 | tf_op jit(solution)/shard_map/ppermute | solution.py:475
  4.6 1.5 %collective-permute-start.1 = (bf16[40,768]{1,0:T(8,128)(2,1)S(1)}, bf16[40,768]{1,0:T(8,128)(2,1)S(1)}, u32[]{:S(2)}, u32[]{:S(2)}) collective-permute-start(bf16[40,768]{1,0:T(8,128)(2,1)S(1)} %get-tuple-element.15), channel_id=1, source_target_pairs={{0,2},{1,3},{2,0},{3,1},{4,6},{5,7},{6,4},{7,5},{8,10},{9,11},{10,... | collective-permute-start | bytes 184328 | tf_op jit(solution)/shard_map/ppermute | solution.py:475
  6.1 1.4 %collective-permute-start.2 = (bf16[40,768]{1,0:T(8,128)(2,1)S(1)}, bf16[40,768]{1,0:T(8,128)(2,1)S(1)}, u32[]{:S(2)}, u32[]{:S(2)}) collective-permute-start(bf16[40,768]{1,0:T(8,128)(2,1)S(1)} %get-tuple-element.16), channel_id=1, source_target_pairs={{0,3},{1,0},{2,1},{3,2},{4,7},{5,4},{6,5},{7,6},{8,11},{9,8},{10,9... | collective-permute-start | bytes 184328 | tf_op jit(solution)/shard_map/ppermute | solution.py:475
  7.5 0.3 collective-permute-done.refs_1_
  7.8 1.1 %collective-permute-done.1.refs_2_ = bf16[40,768]{1,0:T(8,128)(2,1)S(1)} collective-permute-done((bf16[40,768]{1,0:T(8,128)(2,1)S(1)}, bf16[40,768]{1,0:T(8,128)(2,1)S(1)}, u32[]{:S(2)}, u32[]{:S(2)}) %collective-permute-start.1) | collective-permute-done | bytes 61472 | tf_op jit(solution)/shard_map/ppermute | solution.py:475
  8.9 1.5 %collective-permute-done.2.refs_3_ = bf16[40,768]{1,0:T(8,128)(2,1)S(1)} collective-permute-done((bf16[40,768]{1,0:T(8,128)(2,1)S(1)}, bf16[40,768]{1,0:T(8,128)(2,1)S(1)}, u32[]{:S(2)}, u32[]{:S(2)}) %collective-permute-start.2) | collective-permute-done | bytes 61472 | tf_op jit(solution)/shard_map/ppermute | solution.py:475
  10.3 0.0 copy-start.1
  10.3 0.7 %collective-permute-start.3 = (bf16[160,256]{1,0:T(8,128)(2,1)S(1)}, bf16[160,256]{1,0:T(8,128)(2,1)S(1)}, u32[]{:S(2)}, u32[]{:S(2)}) collective-permute-start(bf16[160,256]{1,0:T(8,128)(2,1)S(1)} %maximum_maximum_fusion), channel_id=1, source_target_pairs={{3,7},{7,3},{4,8},{8,4},{11,15},{15,11},{12,16},{16,12},{19,23},{2... | collective-permute-start | bytes 245768 | tf_op jit(solution)/shard_map/ppermute | solution.py:488
  11.0 0.0 copy-done.1
  11.0 10.3 %shard_map.29.refs_6_ = f32[2,160,128]{2,1,0:T(8,128)S(1)} custom-call(bf16[40,768]{1,0:T(8,128)(2,1)S(1)} %get-tuple-element.13.refs_0_, bf16[40,768]{1,0:T(8,128)(2,1)S(1)} %collective-permute-done.refs_1_, bf16[40,768]{1,0:T(8,128)(2,1)S(1)} %collective-permute-done.1.refs_2_, bf16[40,768]{1,0:T(8,128)(2,1)S(1)} %collective-permute-done.2.refs_3_, ...), custom_call_target="tpu_custom_call" | custom-call | tf_op jit(solution)/shard_map/pallas_call | solution.py:434
  21.3 0.0 collective-permute-done.3.refs_5_
  21.3 10.5 %shard_map.30 = (f32[20,128]{1,0:T(8,128)S(1)}, f32[20,128]{1,0:T(8,128)S(1)}, f32[20,128]{1,0:T(8,128)S(1)}, f32[20,128]{1,0:T(8,128)S(1)}) custom-call(bf16[40,768]{1,0:T(8,128)(2,1)S(1)} %get-tuple-element.13.refs_0_, bf16[40,768]{1,0:T(8,128)(2,1)S(1)} %collective-permute-done.refs_1_, bf16[40,768]{1,0:T(8,128)(2,1)S(1)} %collective-permute-done.1.refs_2_, ...), custom_call_target="tpu_custom_call" | custom-call | tf_op jit(solution)/shard_map/pallas_call | solution.py:434
  31.8 3.6 %collective-permute-start.4 = (f32[20,128]{1,0:T(8,128)S(1)}, f32[20,128]{1,0:T(8,128)S(1)}, u32[]{:S(2)}, u32[]{:S(2)}) collective-permute-start(f32[20,128]{1,0:T(8,128)S(1)} %get-tuple-element.18), channel_id=1, source_target_pairs={{0,3},{1,0},{2,1},{3,2},{4,7},{5,4},{6,5},{7,6},{8,11},{9,8},{10,9... | collective-permute-start | bytes 30728 | tf_op jit(solution)/shard_map/ppermute | solution.py:498
  35.5 0.0 collective-permute-start.5
  35.5 0.6 %collective-permute-start.6 = (f32[20,128]{1,0:T(8,128)S(1)}, f32[20,128]{1,0:T(8,128)S(1)}, u32[]{:S(2)}, u32[]{:S(2)}) collective-permute-start(f32[20,128]{1,0:T(8,128)S(1)} %get-tuple-element.20), channel_id=1, source_target_pairs={{0,1},{1,2},{2,3},{3,0},{4,5},{5,6},{6,7},{7,4},{8,9},{9,10},{10,1... | collective-permute-start | bytes 30728 | tf_op jit(solution)/shard_map/ppermute | solution.py:498
  36.1 0.8 %collective-permute-done.4.refs_1_ = f32[20,128]{1,0:T(8,128)S(1)} collective-permute-done((f32[20,128]{1,0:T(8,128)S(1)}, f32[20,128]{1,0:T(8,128)S(1)}, u32[]{:S(2)}, u32[]{:S(2)}) %collective-permute-start.4) | collective-permute-done | bytes 10272 | tf_op jit(solution)/shard_map/ppermute | solution.py:498
  36.9 2.3 %collective-permute-done.5.refs_2_ = f32[20,128]{1,0:T(8,128)S(1)} collective-permute-done((f32[20,128]{1,0:T(8,128)S(1)}, f32[20,128]{1,0:T(8,128)S(1)}, u32[]{:S(2)}, u32[]{:S(2)}) %collective-permute-start.5) | collective-permute-done | bytes 10272 | tf_op jit(solution)/shard_map/ppermute | solution.py:498
  39.2 0.9 %collective-permute-done.6.refs_3_ = f32[20,128]{1,0:T(8,128)S(1)} collective-permute-done((f32[20,128]{1,0:T(8,128)S(1)}, f32[20,128]{1,0:T(8,128)S(1)}, u32[]{:S(2)}, u32[]{:S(2)}) %collective-permute-start.6) | collective-permute-done | bytes 10272 | tf_op jit(solution)/shard_map/ppermute | solution.py:498
  40.1 0.7 %shard_map.31 = f32[2,40,128]{2,1,0:T(8,128)} custom-call(f32[20,128]{1,0:T(8,128)S(1)} %get-tuple-element.17.refs_0_, f32[20,128]{1,0:T(8,128)S(1)} %collective-permute-done.4.refs_1_, f32[20,128]{1,0:T(8,128)S(1)} %collective-permute-done.5.refs_2_, f32[20,128]{1,0:T(8,128)S(1)} %collective-permute-done.6.refs_3_), custom_call_target="tpu_custom_call" | custom-call | tf_op jit(solution)/shard_map/pallas_call | solution.py:499
  (5 shorter events, 0.0 us)
Async XLA Ops:
  0.0 0.9 %copy-start = (bf16[2,40,7,128]{3,1,2,0:T(8,128)(2,1)S(1)}, bf16[2,40,7,128]{3,1,2,0:T(8,128)(2,1)}, u32[]{:S(2)}) copy-start(bf16[2,40,7,128]{3,1,2,0:T(8,128)(2,1)} %param.2) | copy-start | bytes 430084
  1.6 6.2 %collective-permute-start = (bf16[40,768]{1,0:T(8,128)(2,1)S(1)}, bf16[40,768]{1,0:T(8,128)(2,1)S(1)}, u32[]{:S(2)}, u32[]{:S(2)}) collective-permute-start(bf16[40,768]{1,0:T(8,128)(2,1)S(1)} %get-tuple-element.14), channel_id=1, source_target_pairs={{0,1},{1,2},{2,3},{3,0},{4,5},{5,6},{6,7},{7,4},{8,9},{9,10},{10,1... | collective-permute-start | bytes 184328 | tf_op jit(solution)/shard_map/ppermute | solution.py:475
  4.6 4.3 %collective-permute-start.1 = (bf16[40,768]{1,0:T(8,128)(2,1)S(1)}, bf16[40,768]{1,0:T(8,128)(2,1)S(1)}, u32[]{:S(2)}, u32[]{:S(2)}) collective-permute-start(bf16[40,768]{1,0:T(8,128)(2,1)S(1)} %get-tuple-element.15), channel_id=1, source_target_pairs={{0,2},{1,3},{2,0},{3,1},{4,6},{5,7},{6,4},{7,5},{8,10},{9,11},{10,... | collective-permute-start | bytes 184328 | tf_op jit(solution)/shard_map/ppermute | solution.py:475
  6.1 4.2 %collective-permute-start.2 = (bf16[40,768]{1,0:T(8,128)(2,1)S(1)}, bf16[40,768]{1,0:T(8,128)(2,1)S(1)}, u32[]{:S(2)}, u32[]{:S(2)}) collective-permute-start(bf16[40,768]{1,0:T(8,128)(2,1)S(1)} %get-tuple-element.16), channel_id=1, source_target_pairs={{0,3},{1,0},{2,1},{3,2},{4,7},{5,4},{6,5},{7,6},{8,11},{9,8},{10,9... | collective-permute-start | bytes 184328 | tf_op jit(solution)/shard_map/ppermute | solution.py:475
  10.3 0.7 %copy-start.1 = (s32[160]{0:T(256)S(1)}, s32[160]{0:T(256)}, u32[]{:S(2)}) copy-start(s32[160]{0:T(256)} %refs_4_.3) | copy-start | bytes 1924
  10.3 11.0 %collective-permute-start.3 = (bf16[160,256]{1,0:T(8,128)(2,1)S(1)}, bf16[160,256]{1,0:T(8,128)(2,1)S(1)}, u32[]{:S(2)}, u32[]{:S(2)}) collective-permute-start(bf16[160,256]{1,0:T(8,128)(2,1)S(1)} %maximum_maximum_fusion), channel_id=1, source_target_pairs={{3,7},{7,3},{4,8},{8,4},{11,15},{15,11},{12,16},{16,12},{19,23},{2... | collective-permute-start | bytes 245768 | tf_op jit(solution)/shard_map/ppermute | solution.py:488
  31.8 5.0 %collective-permute-start.4 = (f32[20,128]{1,0:T(8,128)S(1)}, f32[20,128]{1,0:T(8,128)S(1)}, u32[]{:S(2)}, u32[]{:S(2)}) collective-permute-start(f32[20,128]{1,0:T(8,128)S(1)} %get-tuple-element.18), channel_id=1, source_target_pairs={{0,3},{1,0},{2,1},{3,2},{4,7},{5,4},{6,5},{7,6},{8,11},{9,8},{10,9... | collective-permute-start | bytes 30728 | tf_op jit(solution)/shard_map/ppermute | solution.py:498
  35.5 3.7 %collective-permute-start.5 = (f32[20,128]{1,0:T(8,128)S(1)}, f32[20,128]{1,0:T(8,128)S(1)}, u32[]{:S(2)}, u32[]{:S(2)}) collective-permute-start(f32[20,128]{1,0:T(8,128)S(1)} %get-tuple-element.19), channel_id=1, source_target_pairs={{0,2},{1,3},{2,0},{3,1},{4,6},{5,7},{6,4},{7,5},{8,10},{9,11},{10,... | collective-permute-start | bytes 30728 | tf_op jit(solution)/shard_map/ppermute | solution.py:498
  35.5 4.6 %collective-permute-start.6 = (f32[20,128]{1,0:T(8,128)S(1)}, f32[20,128]{1,0:T(8,128)S(1)}, u32[]{:S(2)}, u32[]{:S(2)}) collective-permute-start(f32[20,128]{1,0:T(8,128)S(1)} %get-tuple-element.20), channel_id=1, source_target_pairs={{0,1},{1,2},{2,3},{3,0},{4,5},{5,6},{6,7},{7,4},{8,9},{9,10},{10,1... | collective-permute-start | bytes 30728 | tf_op jit(solution)/shard_map/ppermute | solution.py:498

commit v5 on v4

--- a/solution.py
+++ b/solution.py
@@ -301,7 +301,8 @@
     build(0, a_ref)
     multiply(a_ref, raw_ref)
     build(per, a2_ref)
-    lax.fori_loop(0, (steps - 1) // 2, coherence, 0)
+    for pair in range((steps - 1) // 2):
+        coherence(pair, 0)
     if steps % 2 == 0:
         multiply(a2_ref, raw2_ref)
         normalise((steps - 2) * per, raw_ref)

time: 41 us -> 39.2 us (0.956)
  Pallas kernels: 22.2 us -> 20.4 us
    pallas_call x2, Pallas kernels: 20.8 us -> 19 us  [link(): pl.pallas_call(functools.partial(link_kernel, plan, slot), out_shape=shap...]
  transfers between devices with their start and end apart: 7 -> 7, of which waited for: 6 -> 6; matrix products, arithmetic and copies ran while one was open for 0% -> 0% of each run, Pallas kernels for 25% -> 24%
where the time goes in v5:
time: 39.2 us; the launch traced here: 39 us
  Pallas kernels  20.4 us (52%)
  starting transfers between devices  10.9 us (28%)
  waiting for transfers between devices  6.73 us (17%)
  local copies, waits for them, and re-layouts  0.92 us (2%)
    pallas_call x2, Pallas kernels, link(): pl.pallas_call(functools.partial(link_kernel, plan, slot), out_shape=shap...  19 us
    ppermute x3, starting transfers between devices, local(): lax.ppermute(main[r], 'date', [(i, (i + r) % n_date) for i in range(n_dat...  5.94 us
    ppermute x3, starting transfers between devices, local(): lax.ppermute(out[r], 'date', [(i, (i - r) % n_date) for i in range(n_date)])  4.28 us
    ppermute x3, waiting for transfers between devices, local(): lax.ppermute(out[r], 'date', [(i, (i - r) % n_date) for i in range(n_date)])  3.95 us
    ppermute x3, waiting for transfers between devices, local(): lax.ppermute(main[r], 'date', [(i, (i + r) % n_date) for i in range(n_dat...  2.78 us
    unnamed x4, local copies, waits for them, and re-layouts  0.91 us
  transfers between devices with their start and end apart: 7, of which 6 were waited for; matrix products, arithmetic and copies ran while one was open for 0% of the time, Pallas kernels for 24%

profile of v5, /device:TPU:0, one launch (start us, length us, event | category | flops | bytes accessed | tf_op | source)
XLA Modules:
  0.0 39.0 jit_solution(13272646116595035861)
XLA Ops:
  0.0 0.0 copy-start
  0.0 0.9 %copy-done = bf16[2,40,7,128]{3,1,2,0:T(8,128)(2,1)S(1)} copy-done((bf16[2,40,7,128]{3,1,2,0:T(8,128)(2,1)S(1)}, bf16[2,40,7,128]{3,1,2,0:T(8,128)(2,1)}, u32[]{:S(2)}) %copy-start) | copy-done | bytes 143384
  0.9 0.7 %shard_map.28 = (bf16[40,768]{1,0:T(8,128)(2,1)S(1)}, bf16[40,768]{1,0:T(8,128)(2,1)S(1)}, bf16[40,768]{1,0:T(8,128)(2,1)S(1)}, bf16[40,768]{1,0:T(8,128)(2,1)S(1)}) custom-call(bf16[2,7,40,128]{3,2,1,0:T(8,128)(2,1)S(1)} %bitcast.1), custom_call_target="tpu_custom_call" | custom-call | tf_op jit(solution)/shard_map/pallas_call | solution.py:466
  1.6 3.0 %collective-permute-start = (bf16[40,768]{1,0:T(8,128)(2,1)S(1)}, bf16[40,768]{1,0:T(8,128)(2,1)S(1)}, u32[]{:S(2)}, u32[]{:S(2)}) collective-permute-start(bf16[40,768]{1,0:T(8,128)(2,1)S(1)} %get-tuple-element.14), channel_id=1, source_target_pairs={{0,1},{1,2},{2,3},{3,0},{4,5},{5,6},{6,7},{7,4},{8,9},{9,10},{10,1... | collective-permute-start | bytes 184328 | tf_op jit(solution)/shard_map/ppermute | solution.py:476
  4.6 1.5 %collective-permute-start.1 = (bf16[40,768]{1,0:T(8,128)(2,1)S(1)}, bf16[40,768]{1,0:T(8,128)(2,1)S(1)}, u32[]{:S(2)}, u32[]{:S(2)}) collective-permute-start(bf16[40,768]{1,0:T(8,128)(2,1)S(1)} %get-tuple-element.15), channel_id=1, source_target_pairs={{0,2},{1,3},{2,0},{3,1},{4,6},{5,7},{6,4},{7,5},{8,10},{9,11},{10,... | collective-permute-start | bytes 184328 | tf_op jit(solution)/shard_map/ppermute | solution.py:476
  6.1 1.4 %collective-permute-start.2 = (bf16[40,768]{1,0:T(8,128)(2,1)S(1)}, bf16[40,768]{1,0:T(8,128)(2,1)S(1)}, u32[]{:S(2)}, u32[]{:S(2)}) collective-permute-start(bf16[40,768]{1,0:T(8,128)(2,1)S(1)} %get-tuple-element.16), channel_id=1, source_target_pairs={{0,3},{1,0},{2,1},{3,2},{4,7},{5,4},{6,5},{7,6},{8,11},{9,8},{10,9... | collective-permute-start | bytes 184328 | tf_op jit(solution)/shard_map/ppermute | solution.py:476
  7.5 0.3 collective-permute-done.refs_1_
  7.8 1.1 %collective-permute-done.1.refs_2_ = bf16[40,768]{1,0:T(8,128)(2,1)S(1)} collective-permute-done((bf16[40,768]{1,0:T(8,128)(2,1)S(1)}, bf16[40,768]{1,0:T(8,128)(2,1)S(1)}, u32[]{:S(2)}, u32[]{:S(2)}) %collective-permute-start.1) | collective-permute-done | bytes 61472 | tf_op jit(solution)/shard_map/ppermute | solution.py:476
  8.9 1.5 %collective-permute-done.2.refs_3_ = bf16[40,768]{1,0:T(8,128)(2,1)S(1)} collective-permute-done((bf16[40,768]{1,0:T(8,128)(2,1)S(1)}, bf16[40,768]{1,0:T(8,128)(2,1)S(1)}, u32[]{:S(2)}, u32[]{:S(2)}) %collective-permute-start.2) | collective-permute-done | bytes 61472 | tf_op jit(solution)/shard_map/ppermute | solution.py:476
  10.3 0.0 copy-start.1
  10.3 0.7 %collective-permute-start.3 = (bf16[160,256]{1,0:T(8,128)(2,1)S(1)}, bf16[160,256]{1,0:T(8,128)(2,1)S(1)}, u32[]{:S(2)}, u32[]{:S(2)}) collective-permute-start(bf16[160,256]{1,0:T(8,128)(2,1)S(1)} %maximum_maximum_fusion), channel_id=1, source_target_pairs={{3,7},{7,3},{4,8},{8,4},{11,15},{15,11},{12,16},{16,12},{19,23},{2... | collective-permute-start | bytes 245768 | tf_op jit(solution)/shard_map/ppermute | solution.py:489
  11.0 0.0 copy-done.1
  11.0 9.4 %shard_map.29.refs_6_ = f32[2,160,128]{2,1,0:T(8,128)S(1)} custom-call(bf16[40,768]{1,0:T(8,128)(2,1)S(1)} %get-tuple-element.13.refs_0_, bf16[40,768]{1,0:T(8,128)(2,1)S(1)} %collective-permute-done.refs_1_, bf16[40,768]{1,0:T(8,128)(2,1)S(1)} %collective-permute-done.1.refs_2_, bf16[40,768]{1,0:T(8,128)(2,1)S(1)} %collective-permute-done.2.refs_3_, ...), custom_call_target="tpu_custom_call" | custom-call | tf_op jit(solution)/shard_map/pallas_call | solution.py:435
  20.4 0.0 collective-permute-done.3.refs_5_
  20.4 9.6 %shard_map.30 = (f32[20,128]{1,0:T(8,128)S(1)}, f32[20,128]{1,0:T(8,128)S(1)}, f32[20,128]{1,0:T(8,128)S(1)}, f32[20,128]{1,0:T(8,128)S(1)}) custom-call(bf16[40,768]{1,0:T(8,128)(2,1)S(1)} %get-tuple-element.13.refs_0_, bf16[40,768]{1,0:T(8,128)(2,1)S(1)} %collective-permute-done.refs_1_, bf16[40,768]{1,0:T(8,128)(2,1)S(1)} %collective-permute-done.1.refs_2_, ...), custom_call_target="tpu_custom_call" | custom-call | tf_op jit(solution)/shard_map/pallas_call | solution.py:435
  30.1 3.6 %collective-permute-start.4 = (f32[20,128]{1,0:T(8,128)S(1)}, f32[20,128]{1,0:T(8,128)S(1)}, u32[]{:S(2)}, u32[]{:S(2)}) collective-permute-start(f32[20,128]{1,0:T(8,128)S(1)} %get-tuple-element.18), channel_id=1, source_target_pairs={{0,3},{1,0},{2,1},{3,2},{4,7},{5,4},{6,5},{7,6},{8,11},{9,8},{10,9... | collective-permute-start | bytes 30728 | tf_op jit(solution)/shard_map/ppermute | solution.py:499
  33.7 0.0 collective-permute-start.5
  33.7 0.6 %collective-permute-start.6 = (f32[20,128]{1,0:T(8,128)S(1)}, f32[20,128]{1,0:T(8,128)S(1)}, u32[]{:S(2)}, u32[]{:S(2)}) collective-permute-start(f32[20,128]{1,0:T(8,128)S(1)} %get-tuple-element.20), channel_id=1, source_target_pairs={{0,1},{1,2},{2,3},{3,0},{4,5},{5,6},{6,7},{7,4},{8,9},{9,10},{10,1... | collective-permute-start | bytes 30728 | tf_op jit(solution)/shard_map/ppermute | solution.py:499
  34.3 0.8 %collective-permute-done.4.refs_1_ = f32[20,128]{1,0:T(8,128)S(1)} collective-permute-done((f32[20,128]{1,0:T(8,128)S(1)}, f32[20,128]{1,0:T(8,128)S(1)}, u32[]{:S(2)}, u32[]{:S(2)}) %collective-permute-start.4) | collective-permute-done | bytes 10272 | tf_op jit(solution)/shard_map/ppermute | solution.py:499
  35.1 2.3 %collective-permute-done.5.refs_2_ = f32[20,128]{1,0:T(8,128)S(1)} collective-permute-done((f32[20,128]{1,0:T(8,128)S(1)}, f32[20,128]{1,0:T(8,128)S(1)}, u32[]{:S(2)}, u32[]{:S(2)}) %collective-permute-start.5) | collective-permute-done | bytes 10272 | tf_op jit(solution)/shard_map/ppermute | solution.py:499
  37.4 0.9 %collective-permute-done.6.refs_3_ = f32[20,128]{1,0:T(8,128)S(1)} collective-permute-done((f32[20,128]{1,0:T(8,128)S(1)}, f32[20,128]{1,0:T(8,128)S(1)}, u32[]{:S(2)}, u32[]{:S(2)}) %collective-permute-start.6) | collective-permute-done | bytes 10272 | tf_op jit(solution)/shard_map/ppermute | solution.py:499
  38.3 0.7 %shard_map.31 = f32[2,40,128]{2,1,0:T(8,128)} custom-call(f32[20,128]{1,0:T(8,128)S(1)} %get-tuple-element.17.refs_0_, f32[20,128]{1,0:T(8,128)S(1)} %collective-permute-done.4.refs_1_, f32[20,128]{1,0:T(8,128)S(1)} %collective-permute-done.5.refs_2_, f32[20,128]{1,0:T(8,128)S(1)} %collective-permute-done.6.refs_3_), custom_call_target="tpu_custom_call" | custom-call | tf_op jit(solution)/shard_map/pallas_call | solution.py:500
  (5 shorter events, 0.0 us)
Async XLA Ops:
  0.0 0.9 %copy-start = (bf16[2,40,7,128]{3,1,2,0:T(8,128)(2,1)S(1)}, bf16[2,40,7,128]{3,1,2,0:T(8,128)(2,1)}, u32[]{:S(2)}) copy-start(bf16[2,40,7,128]{3,1,2,0:T(8,128)(2,1)} %param.2) | copy-start | bytes 430084
  1.6 6.2 %collective-permute-start = (bf16[40,768]{1,0:T(8,128)(2,1)S(1)}, bf16[40,768]{1,0:T(8,128)(2,1)S(1)}, u32[]{:S(2)}, u32[]{:S(2)}) collective-permute-start(bf16[40,768]{1,0:T(8,128)(2,1)S(1)} %get-tuple-element.14), channel_id=1, source_target_pairs={{0,1},{1,2},{2,3},{3,0},{4,5},{5,6},{6,7},{7,4},{8,9},{9,10},{10,1... | collective-permute-start | bytes 184328 | tf_op jit(solution)/shard_map/ppermute | solution.py:476
  4.6 4.3 %collective-permute-start.1 = (bf16[40,768]{1,0:T(8,128)(2,1)S(1)}, bf16[40,768]{1,0:T(8,128)(2,1)S(1)}, u32[]{:S(2)}, u32[]{:S(2)}) collective-permute-start(bf16[40,768]{1,0:T(8,128)(2,1)S(1)} %get-tuple-element.15), channel_id=1, source_target_pairs={{0,2},{1,3},{2,0},{3,1},{4,6},{5,7},{6,4},{7,5},{8,10},{9,11},{10,... | collective-permute-start | bytes 184328 | tf_op jit(solution)/shard_map/ppermute | solution.py:476
  6.1 4.2 %collective-permute-start.2 = (bf16[40,768]{1,0:T(8,128)(2,1)S(1)}, bf16[40,768]{1,0:T(8,128)(2,1)S(1)}, u32[]{:S(2)}, u32[]{:S(2)}) collective-permute-start(bf16[40,768]{1,0:T(8,128)(2,1)S(1)} %get-tuple-element.16), channel_id=1, source_target_pairs={{0,3},{1,0},{2,1},{3,2},{4,7},{5,4},{6,5},{7,6},{8,11},{9,8},{10,9... | collective-permute-start | bytes 184328 | tf_op jit(solution)/shard_map/ppermute | solution.py:476
  10.3 0.7 %copy-start.1 = (s32[160]{0:T(256)S(1)}, s32[160]{0:T(256)}, u32[]{:S(2)}) copy-start(s32[160]{0:T(256)} %refs_4_.3) | copy-start | bytes 1924
  10.3 10.1 %collective-permute-start.3 = (bf16[160,256]{1,0:T(8,128)(2,1)S(1)}, bf16[160,256]{1,0:T(8,128)(2,1)S(1)}, u32[]{:S(2)}, u32[]{:S(2)}) collective-permute-start(bf16[160,256]{1,0:T(8,128)(2,1)S(1)} %maximum_maximum_fusion), channel_id=1, source_target_pairs={{3,7},{7,3},{4,8},{8,4},{11,15},{15,11},{12,16},{16,12},{19,23},{2... | collective-permute-start | bytes 245768 | tf_op jit(solution)/shard_map/ppermute | solution.py:489
  30.1 5.0 %collective-permute-start.4 = (f32[20,128]{1,0:T(8,128)S(1)}, f32[20,128]{1,0:T(8,128)S(1)}, u32[]{:S(2)}, u32[]{:S(2)}) collective-permute-start(f32[20,128]{1,0:T(8,128)S(1)} %get-tuple-element.18), channel_id=1, source_target_pairs={{0,3},{1,0},{2,1},{3,2},{4,7},{5,4},{6,5},{7,6},{8,11},{9,8},{10,9... | collective-permute-start | bytes 30728 | tf_op jit(solution)/shard_map/ppermute | solution.py:499
  33.7 3.7 %collective-permute-start.5 = (f32[20,128]{1,0:T(8,128)S(1)}, f32[20,128]{1,0:T(8,128)S(1)}, u32[]{:S(2)}, u32[]{:S(2)}) collective-permute-start(f32[20,128]{1,0:T(8,128)S(1)} %get-tuple-element.19), channel_id=1, source_target_pairs={{0,2},{1,3},{2,0},{3,1},{4,6},{5,7},{6,4},{7,5},{8,10},{9,11},{10,... | collective-permute-start | bytes 30728 | tf_op jit(solution)/shard_map/ppermute | solution.py:499
  33.7 4.6 %collective-permute-start.6 = (f32[20,128]{1,0:T(8,128)S(1)}, f32[20,128]{1,0:T(8,128)S(1)}, u32[]{:S(2)}, u32[]{:S(2)}) collective-permute-start(f32[20,128]{1,0:T(8,128)S(1)} %get-tuple-element.20), channel_id=1, source_target_pairs={{0,1},{1,2},{2,3},{3,0},{4,5},{5,6},{6,7},{7,4},{8,9},{9,10},{10,1... | collective-permute-start | bytes 30728 | tf_op jit(solution)/shard_map/ppermute | solution.py:499

commit v6 on v5

--- a/solution.py
+++ b/solution.py
@@ -119,7 +119,7 @@
     for quarter in range(4):
         value = jnp.zeros((own // 2, LANES), f32)
         for r in range(n_date):
-            chunk = plan.chunk(lax.rem(me + r, n_date))
+            chunk = plan.chunk(lax.rem(me + n_date - r, n_date))
             shift = lax.rem(chunk * plan.cols // region + 4 - quarter, 4) * region
             value = jnp.where(owner == chunk, pltpu.roll(pieces[r][...], shift, 1), value)
         start = quarter % 2 * (own // 2)
@@ -199,12 +199,13 @@
                 col = jnp.where(col >= wide, col - wide, col)
             low = jnp.where(is_left, 0, wide - missing)
             valid = (col >= low) & (col < low + missing) & (at >= 0) & (at < LINES * wide)
+            outermost = lax.axis_index("space") == jnp.where(is_left, 0, lax.axis_size("space") - 1)
             shift = jnp.where(is_left, missing - wide, wide - missing) + base
             for part in range(2):
                 got = edge_ref[:, part * plan.tail_lanes : (part + 1) * plan.tail_lanes].astype(f32)
                 if plan.tail_lanes < PART:
                     got = jnp.concatenate([got, jnp.zeros((DATES, PART - plan.tail_lanes), f32)], axis=1)
-                got = pltpu.roll(got, lax.rem(shift + PART, PART), 1)
+                got = jnp.where(outermost, 0.0, pltpu.roll(got, lax.rem(shift + PART, PART), 1))
                 at_part = slice(part * PART, (part + 1) * PART)
                 s_ref[:, at_part] = jnp.where(valid, got, s_ref[:, at_part])
 
@@ -415,7 +416,7 @@
     for r in range(n_date):
         value = None
         for q in range(4):
-            start = r * own + q % 2 * (own // 2)
+            start = (n_date - r) % n_date * own + q % 2 * (own // 2)
             at = slice(start, start + own // 2)
             piece = y_ref[q // 2, at]
             if slot:
@@ -479,6 +480,12 @@
         for d in plan.right if s % 2 == 0 else plan.left:
             before, after = s * n_date + d, (s + 1) * n_date + d
             swap += [(before, after), (after, before)]
+    idle = [d for d in range(n_date) if d not in plan.left + plan.right]
+    for d in plan.left:
+        swap += [(d, (n_space - 1) * n_date + d), ((n_space - 1) * n_date + d, d)]
+    for s in range(n_space):
+        for one, two in zip(idle[0::2], idle[1::2]):
+            swap += [(s * n_date + one, s * n_date + two), (s * n_date + two, s * n_date + one)]
     edge = jnp.concatenate(
         [
             jnp.concatenate([m[:, k * plan.stride + plan.tail : (k + 1) * plan.stride] for k in range(2)], axis=1)
@@ -494,9 +501,9 @@
         (before,) = link(plan, 0, main, acquisition_day)
         out = link(plan, 1, main, acquisition_day, edge, before)
 
-    pieces = [out[0]]
-    for r in range(1, n_date):
-        pieces.append(lax.ppermute(out[r], "date", [(i, (i - r) % n_date) for i in range(n_date)]))
+    pieces = list(out)
+    for k in range(1, n_date):
+        pieces[k] = lax.ppermute(out[k], "date", [(i, (i + k) % n_date) for i in range(n_date)])
     return pl.pallas_call(
         functools.partial(unpack_kernel, plan),
         out_shape=jax.ShapeDtypeStruct((2, own, plan.width), f32),

time: 39.2 us -> 37.6 us (0.959)
  waiting for transfers between devices: 6.73 us -> 4.58 us
  starting transfers between devices: 10.9 us -> 11.4 us
    ppermute x3, waiting for transfers between devices: 3.95 us -> 1.8 us  [local(): lax.ppermute(out[k], 'date', [(i, (i + k) % n_date) for i in range(n_date)])]
    ppermute x1, starting transfers between devices: 0.67 us -> 1.99 us  [local(): edge = lax.ppermute(edge, ('space', 'date'), swap)]
    ppermute x3, starting transfers between devices: 4.28 us -> 3.5 us  [local(): lax.ppermute(out[k], 'date', [(i, (i + k) % n_date) for i in range(n_date)])]
  transfers between devices with their start and end apart: 7 -> 7, of which waited for: 6 -> 5; matrix products, arithmetic and copies ran while one was open for 0% -> 0% of each run, Pallas kernels for 24% -> 25%
where the time goes in v6:
time: 37.6 us; the launch traced here: 37.4 us
  Pallas kernels  20.4 us (54%)
  starting transfers between devices  11.4 us (30%)
  waiting for transfers between devices  4.58 us (12%)
  local copies, waits for them, and re-layouts  0.92 us (2%)
    pallas_call x2, Pallas kernels, link(): pl.pallas_call(functools.partial(link_kernel, plan, slot), out_shape=shap...  19 us
    ppermute x3, starting transfers between devices, local(): lax.ppermute(main[r], 'date', [(i, (i + r) % n_date) for i in range(n_dat...  5.94 us
    ppermute x3, starting transfers between devices, local(): lax.ppermute(out[k], 'date', [(i, (i + k) % n_date) for i in range(n_date)])  3.5 us
    ppermute x3, waiting for transfers between devices, local(): lax.ppermute(main[r], 'date', [(i, (i + r) % n_date) for i in range(n_dat...  2.78 us
    ppermute x1, starting transfers between devices, local(): edge = lax.ppermute(edge, ('space', 'date'), swap)  1.99 us
    ppermute x3, waiting for transfers between devices, local(): lax.ppermute(out[k], 'date', [(i, (i + k) % n_date) for i in range(n_date)])  1.8 us
    unnamed x4, local copies, waits for them, and re-layouts  0.91 us
  transfers between devices with their start and end apart: 7, of which 5 were waited for; matrix products, arithmetic and copies ran while one was open for 0% of the time, Pallas kernels for 25%

profile of v6, /device:TPU:0, one launch (start us, length us, event | category | flops | bytes accessed | tf_op | source)
XLA Modules:
  0.0 37.4 jit_solution(2727603180912847137)
XLA Ops:
  0.0 0.0 copy-start
  0.0 0.9 %copy-done = bf16[2,40,7,128]{3,1,2,0:T(8,128)(2,1)S(1)} copy-done((bf16[2,40,7,128]{3,1,2,0:T(8,128)(2,1)S(1)}, bf16[2,40,7,128]{3,1,2,0:T(8,128)(2,1)}, u32[]{:S(2)}) %copy-start) | copy-done | bytes 143384
  0.9 0.7 %shard_map.28 = (bf16[40,768]{1,0:T(8,128)(2,1)S(1)}, bf16[40,768]{1,0:T(8,128)(2,1)S(1)}, bf16[40,768]{1,0:T(8,128)(2,1)S(1)}, bf16[40,768]{1,0:T(8,128)(2,1)S(1)}) custom-call(bf16[2,7,40,128]{3,2,1,0:T(8,128)(2,1)S(1)} %bitcast.1), custom_call_target="tpu_custom_call" | custom-call | tf_op jit(solution)/shard_map/pallas_call | solution.py:467
  1.6 3.0 %collective-permute-start = (bf16[40,768]{1,0:T(8,128)(2,1)S(1)}, bf16[40,768]{1,0:T(8,128)(2,1)S(1)}, u32[]{:S(2)}, u32[]{:S(2)}) collective-permute-start(bf16[40,768]{1,0:T(8,128)(2,1)S(1)} %get-tuple-element.14), channel_id=1, source_target_pairs={{0,1},{1,2},{2,3},{3,0},{4,5},{5,6},{6,7},{7,4},{8,9},{9,10},{10,1... | collective-permute-start | bytes 184328 | tf_op jit(solution)/shard_map/ppermute | solution.py:477
  4.6 1.5 %collective-permute-start.1 = (bf16[40,768]{1,0:T(8,128)(2,1)S(1)}, bf16[40,768]{1,0:T(8,128)(2,1)S(1)}, u32[]{:S(2)}, u32[]{:S(2)}) collective-permute-start(bf16[40,768]{1,0:T(8,128)(2,1)S(1)} %get-tuple-element.15), channel_id=1, source_target_pairs={{0,2},{1,3},{2,0},{3,1},{4,6},{5,7},{6,4},{7,5},{8,10},{9,11},{10,... | collective-permute-start | bytes 184328 | tf_op jit(solution)/shard_map/ppermute | solution.py:477
  6.1 1.4 %collective-permute-start.2 = (bf16[40,768]{1,0:T(8,128)(2,1)S(1)}, bf16[40,768]{1,0:T(8,128)(2,1)S(1)}, u32[]{:S(2)}, u32[]{:S(2)}) collective-permute-start(bf16[40,768]{1,0:T(8,128)(2,1)S(1)} %get-tuple-element.16), channel_id=1, source_target_pairs={{0,3},{1,0},{2,1},{3,2},{4,7},{5,4},{6,5},{7,6},{8,11},{9,8},{10,9... | collective-permute-start | bytes 184328 | tf_op jit(solution)/shard_map/ppermute | solution.py:477
  7.5 0.3 collective-permute-done.refs_1_
  7.8 1.1 %collective-permute-done.1.refs_2_ = bf16[40,768]{1,0:T(8,128)(2,1)S(1)} collective-permute-done((bf16[40,768]{1,0:T(8,128)(2,1)S(1)}, bf16[40,768]{1,0:T(8,128)(2,1)S(1)}, u32[]{:S(2)}, u32[]{:S(2)}) %collective-permute-start.1) | collective-permute-done | bytes 61472 | tf_op jit(solution)/shard_map/ppermute | solution.py:477
  8.9 1.5 %collective-permute-done.2.refs_3_ = bf16[40,768]{1,0:T(8,128)(2,1)S(1)} collective-permute-done((bf16[40,768]{1,0:T(8,128)(2,1)S(1)}, bf16[40,768]{1,0:T(8,128)(2,1)S(1)}, u32[]{:S(2)}, u32[]{:S(2)}) %collective-permute-start.2) | collective-permute-done | bytes 61472 | tf_op jit(solution)/shard_map/ppermute | solution.py:477
  10.3 0.0 copy-start.1
  10.3 2.0 %collective-permute-start.3 = (bf16[160,256]{1,0:T(8,128)(2,1)S(1)}, bf16[160,256]{1,0:T(8,128)(2,1)S(1)}, u32[]{:S(2)}, u32[]{:S(2)}) collective-permute-start(bf16[160,256]{1,0:T(8,128)(2,1)S(1)} %maximum_maximum_fusion), channel_id=1, source_target_pairs={{3,7},{7,3},{4,8},{8,4},{11,15},{15,11},{12,16},{16,12},{19,23},{2... | collective-permute-start | bytes 245768 | tf_op jit(solution)/shard_map/ppermute | solution.py:496
  12.3 0.0 copy-done.1
  12.3 9.4 %shard_map.29.refs_6_ = f32[2,160,128]{2,1,0:T(8,128)S(1)} custom-call(bf16[40,768]{1,0:T(8,128)(2,1)S(1)} %get-tuple-element.13.refs_0_, bf16[40,768]{1,0:T(8,128)(2,1)S(1)} %collective-permute-done.refs_1_, bf16[40,768]{1,0:T(8,128)(2,1)S(1)} %collective-permute-done.1.refs_2_, bf16[40,768]{1,0:T(8,128)(2,1)S(1)} %collective-permute-done.2.refs_3_, ...), custom_call_target="tpu_custom_call" | custom-call | tf_op jit(solution)/shard_map/pallas_call | solution.py:436
  21.7 0.0 collective-permute-done.3.refs_5_
  21.7 9.6 %shard_map.30 = (f32[20,128]{1,0:T(8,128)S(1)}, f32[20,128]{1,0:T(8,128)S(1)}, f32[20,128]{1,0:T(8,128)S(1)}, f32[20,128]{1,0:T(8,128)S(1)}) custom-call(bf16[40,768]{1,0:T(8,128)(2,1)S(1)} %get-tuple-element.13.refs_0_, bf16[40,768]{1,0:T(8,128)(2,1)S(1)} %collective-permute-done.refs_1_, bf16[40,768]{1,0:T(8,128)(2,1)S(1)} %collective-permute-done.1.refs_2_, ...), custom_call_target="tpu_custom_call" | custom-call | tf_op jit(solution)/shard_map/pallas_call | solution.py:436
  31.4 0.1 collective-permute-start.4
  31.4 1.6 %collective-permute-start.5 = (f32[20,128]{1,0:T(8,128)S(1)}, f32[20,128]{1,0:T(8,128)S(1)}, u32[]{:S(2)}, u32[]{:S(2)}) collective-permute-start(f32[20,128]{1,0:T(8,128)S(1)} %get-tuple-element.19), channel_id=1, source_target_pairs={{0,2},{1,3},{2,0},{3,1},{4,6},{5,7},{6,4},{7,5},{8,10},{9,11},{10,... | collective-permute-start | bytes 30728 | tf_op jit(solution)/shard_map/ppermute | solution.py:506
  33.0 1.9 %collective-permute-start.6 = (f32[20,128]{1,0:T(8,128)S(1)}, f32[20,128]{1,0:T(8,128)S(1)}, u32[]{:S(2)}, u32[]{:S(2)}) collective-permute-start(f32[20,128]{1,0:T(8,128)S(1)} %get-tuple-element.20), channel_id=1, source_target_pairs={{0,3},{1,0},{2,1},{3,2},{4,7},{5,4},{6,5},{7,6},{8,11},{9,8},{10,9... | collective-permute-start | bytes 30728 | tf_op jit(solution)/shard_map/ppermute | solution.py:506
  34.9 1.1 %collective-permute-done.4.refs_1_ = f32[20,128]{1,0:T(8,128)S(1)} collective-permute-done((f32[20,128]{1,0:T(8,128)S(1)}, f32[20,128]{1,0:T(8,128)S(1)}, u32[]{:S(2)}, u32[]{:S(2)}) %collective-permute-start.4) | collective-permute-done | bytes 10272 | tf_op jit(solution)/shard_map/ppermute | solution.py:506
  36.0 0.0 collective-permute-done.5.refs_2_
  36.0 0.7 %collective-permute-done.6.refs_3_ = f32[20,128]{1,0:T(8,128)S(1)} collective-permute-done((f32[20,128]{1,0:T(8,128)S(1)}, f32[20,128]{1,0:T(8,128)S(1)}, u32[]{:S(2)}, u32[]{:S(2)}) %collective-permute-start.6) | collective-permute-done | bytes 10272 | tf_op jit(solution)/shard_map/ppermute | solution.py:506
  36.7 0.8 %shard_map.31 = f32[2,40,128]{2,1,0:T(8,128)} custom-call(f32[20,128]{1,0:T(8,128)S(1)} %get-tuple-element.17.refs_0_, f32[20,128]{1,0:T(8,128)S(1)} %collective-permute-done.4.refs_1_, f32[20,128]{1,0:T(8,128)S(1)} %collective-permute-done.5.refs_2_, f32[20,128]{1,0:T(8,128)S(1)} %collective-permute-done.6.refs_3_), custom_call_target="tpu_custom_call" | custom-call | tf_op jit(solution)/shard_map/pallas_call | solution.py:507
  (5 shorter events, 0.0 us)
Async XLA Ops:
  0.0 0.9 %copy-start = (bf16[2,40,7,128]{3,1,2,0:T(8,128)(2,1)S(1)}, bf16[2,40,7,128]{3,1,2,0:T(8,128)(2,1)}, u32[]{:S(2)}) copy-start(bf16[2,40,7,128]{3,1,2,0:T(8,128)(2,1)} %param.2) | copy-start | bytes 430084
  1.6 6.2 %collective-permute-start = (bf16[40,768]{1,0:T(8,128)(2,1)S(1)}, bf16[40,768]{1,0:T(8,128)(2,1)S(1)}, u32[]{:S(2)}, u32[]{:S(2)}) collective-permute-start(bf16[40,768]{1,0:T(8,128)(2,1)S(1)} %get-tuple-element.14), channel_id=1, source_target_pairs={{0,1},{1,2},{2,3},{3,0},{4,5},{5,6},{6,7},{7,4},{8,9},{9,10},{10,1... | collective-permute-start | bytes 184328 | tf_op jit(solution)/shard_map/ppermute | solution.py:477
  4.6 4.3 %collective-permute-start.1 = (bf16[40,768]{1,0:T(8,128)(2,1)S(1)}, bf16[40,768]{1,0:T(8,128)(2,1)S(1)}, u32[]{:S(2)}, u32[]{:S(2)}) collective-permute-start(bf16[40,768]{1,0:T(8,128)(2,1)S(1)} %get-tuple-element.15), channel_id=1, source_target_pairs={{0,2},{1,3},{2,0},{3,1},{4,6},{5,7},{6,4},{7,5},{8,10},{9,11},{10,... | collective-permute-start | bytes 184328 | tf_op jit(solution)/shard_map/ppermute | solution.py:477
  6.1 4.2 %collective-permute-start.2 = (bf16[40,768]{1,0:T(8,128)(2,1)S(1)}, bf16[40,768]{1,0:T(8,128)(2,1)S(1)}, u32[]{:S(2)}, u32[]{:S(2)}) collective-permute-start(bf16[40,768]{1,0:T(8,128)(2,1)S(1)} %get-tuple-element.16), channel_id=1, source_target_pairs={{0,3},{1,0},{2,1},{3,2},{4,7},{5,4},{6,5},{7,6},{8,11},{9,8},{10,9... | collective-permute-start | bytes 184328 | tf_op jit(solution)/shard_map/ppermute | solution.py:477
  10.3 2.0 %copy-start.1 = (s32[160]{0:T(256)S(1)}, s32[160]{0:T(256)}, u32[]{:S(2)}) copy-start(s32[160]{0:T(256)} %refs_4_.3) | copy-start | bytes 1924
  10.3 11.4 %collective-permute-start.3 = (bf16[160,256]{1,0:T(8,128)(2,1)S(1)}, bf16[160,256]{1,0:T(8,128)(2,1)S(1)}, u32[]{:S(2)}, u32[]{:S(2)}) collective-permute-start(bf16[160,256]{1,0:T(8,128)(2,1)S(1)} %maximum_maximum_fusion), channel_id=1, source_target_pairs={{3,7},{7,3},{4,8},{8,4},{11,15},{15,11},{12,16},{16,12},{19,23},{2... | collective-permute-start | bytes 245768 | tf_op jit(solution)/shard_map/ppermute | solution.py:496
  31.4 4.6 %collective-permute-start.4 = (f32[20,128]{1,0:T(8,128)S(1)}, f32[20,128]{1,0:T(8,128)S(1)}, u32[]{:S(2)}, u32[]{:S(2)}) collective-permute-start(f32[20,128]{1,0:T(8,128)S(1)} %get-tuple-element.18), channel_id=1, source_target_pairs={{0,1},{1,2},{2,3},{3,0},{4,5},{5,6},{6,7},{7,4},{8,9},{9,10},{10,1... | collective-permute-start | bytes 30728 | tf_op jit(solution)/shard_map/ppermute | solution.py:506
  31.4 4.6 %collective-permute-start.5 = (f32[20,128]{1,0:T(8,128)S(1)}, f32[20,128]{1,0:T(8,128)S(1)}, u32[]{:S(2)}, u32[]{:S(2)}) collective-permute-start(f32[20,128]{1,0:T(8,128)S(1)} %get-tuple-element.19), channel_id=1, source_target_pairs={{0,2},{1,3},{2,0},{3,1},{4,6},{5,7},{6,4},{7,5},{8,10},{9,11},{10,... | collective-permute-start | bytes 30728 | tf_op jit(solution)/shard_map/ppermute | solution.py:506
  33.0 3.7 %collective-permute-start.6 = (f32[20,128]{1,0:T(8,128)S(1)}, f32[20,128]{1,0:T(8,128)S(1)}, u32[]{:S(2)}, u32[]{:S(2)}) collective-permute-start(f32[20,128]{1,0:T(8,128)S(1)} %get-tuple-element.20), channel_id=1, source_target_pairs={{0,3},{1,0},{2,1},{3,2},{4,7},{5,4},{6,5},{7,6},{8,11},{9,8},{10,9... | collective-permute-start | bytes 30728 | tf_op jit(solution)/shard_map/ppermute | solution.py:506

commit v7 on v6

--- a/solution.py
+++ b/solution.py
@@ -60,6 +60,23 @@
         if self.halves == 1:
             return 0
         return jnp.where(self.swapped(chunk), 1 - slot, slot)
+
+
+def taper_kernel(plan, days_ref, taper):
+    n_date = plan.n_date
+    me = lax.axis_index("date")
+    row = days_ref[...].astype(f32).reshape(1, DATES)
+    lane_of = lax.broadcasted_iota(jnp.int32, (8, DATES), 1)
+    sub_of = lax.broadcasted_iota(jnp.int32, (8, DATES), 0)
+    for r in range(n_date):
+        first = lax.rem(me + n_date - r, n_date) * plan.own
+        for b in range(0, plan.own, 8):
+            high = min(8, plan.own - b)
+            picked = jnp.where(lane_of == sub_of + (first + b), row, 0.0)
+            days = jnp.sum(picked, axis=1, keepdims=True)[:high]
+            at = r * plan.own + b
+            taper[0, at : at + high] = jnp.broadcast_to(jnp.exp(days * (1.0 / taper_days)), (high, LANES))
+            taper[1, at : at + high] = jnp.broadcast_to(jnp.exp(days * (-1.0 / taper_days)), (high, LANES))
 
 
 def pack_kernel(plan, x_ref, *refs):
@@ -138,7 +155,7 @@
     n_date, own, pix = plan.n_date, plan.own, plan.pix
     groups, blocks, per, span = plan.groups, plan.blocks, plan.per, plan.span
     last = slot == plan.halves - 1
-    main, days_ref, refs = refs[:n_date], refs[n_date], refs[n_date + 1 :]
+    main, taper_ref, refs = refs[:n_date], refs[n_date], refs[n_date + 1 :]
     edge_ref = before_ref = None
     if last:
         edge_ref, refs = refs[0], refs[1:]
@@ -209,15 +226,6 @@
                 at_part = slice(part * PART, (part + 1) * PART)
                 s_ref[:, at_part] = jnp.where(valid, got, s_ref[:, at_part])
 
-    sub8 = lax.broadcasted_iota(jnp.int32, (8, LANES), 0)
-    for b in range(0, DATES, 8):
-        days = jnp.zeros((8, LANES), f32)
-        for t in range(8):
-            r, at = divmod(b + t, own)
-            day = days_ref[lax.rem(me + n_date - r, n_date) * own + at].astype(f32)
-            days = jnp.where(sub8 == t, day, days)
-        ty_ref[0, b : b + 8] = jnp.exp(days * (1.0 / taper_days))
-        ty_ref[1, b : b + 8] = jnp.exp(days * (-1.0 / taper_days))
     sr, si = s_ref[:, 0:PART], s_ref[:, PART : 2 * PART]
     left_ref[0:DATES, 0:PART] = sr.astype(bf16)
     left_ref[0:DATES, PART : 2 * PART] = si.astype(bf16)
@@ -239,7 +247,7 @@
     power = power + lax.dot_general(low, rep, nt, preferred_element_type=f32)
     root = lax.rsqrt(power + epsilon)
     for k in range(2):
-        y = ty_ref[k] * root
+        y = taper_ref[k] * root
         ty_ref[k] = y
         for b, row in enumerate(to_rows(y)):
             tv_ref[k, b : b + 1, :] = row
@@ -425,7 +433,7 @@
         outs[r][...] = value
 
 
-def link(plan, slot, main, days, *more):
+def link(plan, slot, main, taper, *more):
     last = slot == plan.halves - 1
     matrix = pltpu.VMEM((plan.blocks, DATES, LANES), f32)
     samples = pltpu.VMEM((DATES, 2 * PART), f32)
@@ -436,7 +444,7 @@
     return pl.pallas_call(
         functools.partial(link_kernel, plan, slot),
         out_shape=shapes,
-        in_specs=[VMEM] * plan.n_date + [pl.BlockSpec(memory_space=pltpu.SMEM)] + [VMEM] * len(more),
+        in_specs=[VMEM] * (plan.n_date + 1 + len(more)),
         out_specs=[VMEM] * len(shapes),
         scratch_shapes=[
             samples,
@@ -456,7 +464,7 @@
             pltpu.VMEM((2 * DATES, PART), f32),
         ],
         compiler_params=pltpu.CompilerParams(vmem_limit_bytes=24 * 2**20),
-    )(*main, days, *more)
+    )(*main, taper, *more)
 
 
 def local(acquisitions, acquisition_day):
@@ -473,6 +481,14 @@
         compiler_params=pltpu.CompilerParams(vmem_limit_bytes=24 * 2**20),
     )(jnp.transpose(acquisitions, (0, 2, 1, 3)))
     main = list(main)
+    main[0], acquisition_day = lax.optimization_barrier((main[0], acquisition_day))
+    taper = pl.pallas_call(
+        functools.partial(taper_kernel, plan),
+        out_shape=jax.ShapeDtypeStruct((2, DATES, LANES), f32),
+        in_specs=[VMEM],
+        out_specs=VMEM,
+    )(acquisition_day)
+    main[0], taper = lax.optimization_barrier((main[0], taper))
     for r in range(1, n_date):
         main[r] = lax.ppermute(main[r], "date", [(i, (i + r) % n_date) for i in range(n_date)])
     swap = []
@@ -496,10 +512,10 @@
     edge = lax.ppermute(edge, ("space", "date"), swap)
 
     if plan.halves == 1:
-        out = link(plan, 0, main, acquisition_day, edge)
+        out = link(plan, 0, main, taper, edge)
     else:
-        (before,) = link(plan, 0, main, acquisition_day)
-        out = link(plan, 1, main, acquisition_day, edge, before)
+        (before,) = link(plan, 0, main, taper)
+        out = link(plan, 1, main, taper, edge, before)
 
     pieces = list(out)
     for k in range(1, n_date):

time: 37.6 us -> 36.3 us (0.965)
  waiting for transfers between devices: 4.58 us -> 3 us
  Pallas kernels: 20.4 us -> 20.8 us
    ppermute x3, waiting for transfers between devices: 2.78 us -> 1.29 us  [local(): lax.ppermute(main[r], 'date', [(i, (i + r) % n_date) for i in range(n_dat...]
    pallas_call x0 -> x1, Pallas kernels: none -> 1.45 us  [local(): pl.pallas_call(functools.partial(taper_kernel, plan), out_shape=jax.Shape...]
    pallas_call x2, Pallas kernels: 19 us -> 17.9 us  [link(): pl.pallas_call(functools.partial(link_kernel, plan, slot), out_shape=shap...]
  transfers between devices with their start and end apart: 7 -> 7, of which waited for: 5 -> 3; matrix products, arithmetic and copies ran while one was open for 0% -> 0% of each run, Pallas kernels for 25% -> 28%
where the time goes in v7:
time: 36.3 us; the launch traced here: 36.2 us
  Pallas kernels  20.8 us (57%)
  starting transfers between devices  11.4 us (31%)
  waiting for transfers between devices  3 us (8%)
  local copies, waits for them, and re-layouts  0.93 us (3%)
    pallas_call x2, Pallas kernels, link(): pl.pallas_call(functools.partial(link_kernel, plan, slot), out_shape=shap...  17.9 us
    ppermute x3, starting transfers between devices, local(): lax.ppermute(main[r], 'date', [(i, (i + r) % n_date) for i in range(n_dat...  5.94 us
    ppermute x3, starting transfers between devices, local(): lax.ppermute(out[k], 'date', [(i, (i + k) % n_date) for i in range(n_date)])  3.5 us
    ppermute x1, starting transfers between devices, local(): edge = lax.ppermute(edge, ('space', 'date'), swap)  1.99 us
    ppermute x3, waiting for transfers between devices, local(): lax.ppermute(out[k], 'date', [(i, (i + k) % n_date) for i in range(n_date)])  1.7 us
    pallas_call x1, Pallas kernels, local(): pl.pallas_call(functools.partial(taper_kernel, plan), out_shape=jax.Shape...  1.45 us
    ppermute x3, waiting for transfers between devices, local(): lax.ppermute(main[r], 'date', [(i, (i + r) % n_date) for i in range(n_dat...  1.29 us
    unnamed x4, local copies, waits for them, and re-layouts  0.91 us
  transfers between devices with their start and end apart: 7, of which 3 were waited for; matrix products, arithmetic and copies ran while one was open for 0% of the time, Pallas kernels for 28%

profile of v7, /device:TPU:0, one launch (start us, length us, event | category | flops | bytes accessed | tf_op | source)
XLA Modules:
  0.0 36.2 jit_solution(16347564166661407023)
XLA Ops:
  0.0 0.0 copy-start.1
  0.0 0.9 %copy-done.1 = bf16[2,40,7,128]{3,1,2,0:T(8,128)(2,1)S(1)} copy-done((bf16[2,40,7,128]{3,1,2,0:T(8,128)(2,1)S(1)}, bf16[2,40,7,128]{3,1,2,0:T(8,128)(2,1)}, u32[]{:S(2)}) %copy-start.1) | copy-done | bytes 143384
  0.9 0.7 %shard_map.28 = (bf16[40,768]{1,0:T(8,128)(2,1)S(1)}, bf16[40,768]{1,0:T(8,128)(2,1)S(1)}, bf16[40,768]{1,0:T(8,128)(2,1)S(1)}, bf16[40,768]{1,0:T(8,128)(2,1)S(1)}) custom-call(bf16[2,7,40,128]{3,2,1,0:T(8,128)(2,1)S(1)} %bitcast.1), custom_call_target="tpu_custom_call" | custom-call | tf_op jit(solution)/shard_map/pallas_call | solution.py:475
  1.6 3.0 %collective-permute-start = (bf16[40,768]{1,0:T(8,128)(2,1)S(1)}, bf16[40,768]{1,0:T(8,128)(2,1)S(1)}, u32[]{:S(2)}, u32[]{:S(2)}) collective-permute-start(bf16[40,768]{1,0:T(8,128)(2,1)S(1)} %get-tuple-element.21), channel_id=1, source_target_pairs={{0,1},{1,2},{2,3},{3,0},{4,5},{5,6},{6,7},{7,4},{8,9},{9,10},{10,1... | collective-permute-start | bytes 184328 | tf_op jit(solution)/shard_map/ppermute | solution.py:493
  4.6 1.5 %collective-permute-start.1 = (bf16[40,768]{1,0:T(8,128)(2,1)S(1)}, bf16[40,768]{1,0:T(8,128)(2,1)S(1)}, u32[]{:S(2)}, u32[]{:S(2)}) collective-permute-start(bf16[40,768]{1,0:T(8,128)(2,1)S(1)} %get-tuple-element.22), channel_id=1, source_target_pairs={{0,2},{1,3},{2,0},{3,1},{4,6},{5,7},{6,4},{7,5},{8,10},{9,11},{10,... | collective-permute-start | bytes 184328 | tf_op jit(solution)/shard_map/ppermute | solution.py:493
  6.1 1.4 %collective-permute-start.2 = (bf16[40,768]{1,0:T(8,128)(2,1)S(1)}, bf16[40,768]{1,0:T(8,128)(2,1)S(1)}, u32[]{:S(2)}, u32[]{:S(2)}) collective-permute-start(bf16[40,768]{1,0:T(8,128)(2,1)S(1)} %get-tuple-element.23), channel_id=1, source_target_pairs={{0,3},{1,0},{2,1},{3,2},{4,7},{5,4},{6,5},{7,6},{8,11},{9,8},{10,9... | collective-permute-start | bytes 184328 | tf_op jit(solution)/shard_map/ppermute | solution.py:493
  7.5 1.5 %shard_map.29.refs_4_ = f32[2,160,128]{2,1,0:T(8,128)} custom-call(s32[160]{0:T(256)} %days_ref), custom_call_target="tpu_custom_call" | custom-call | tf_op jit(solution)/shard_map/pallas_call | solution.py:485
  9.0 0.0 copy-start
  9.0 0.0 collective-permute-done.refs_1_
  9.0 0.0 collective-permute-done.1.refs_2_
  9.0 1.3 %collective-permute-done.2.refs_3_ = bf16[40,768]{1,0:T(8,128)(2,1)S(1)} collective-permute-done((bf16[40,768]{1,0:T(8,128)(2,1)S(1)}, bf16[40,768]{1,0:T(8,128)(2,1)S(1)}, u32[]{:S(2)}, u32[]{:S(2)}) %collective-permute-start.2) | collective-permute-done | bytes 61472 | tf_op jit(solution)/shard_map/ppermute | solution.py:493
  10.3 2.0 %collective-permute-start.3 = (bf16[160,256]{1,0:T(8,128)(2,1)S(1)}, bf16[160,256]{1,0:T(8,128)(2,1)S(1)}, u32[]{:S(2)}, u32[]{:S(2)}) collective-permute-start(bf16[160,256]{1,0:T(8,128)(2,1)S(1)} %maximum_maximum_fusion), channel_id=1, source_target_pairs={{3,7},{7,3},{4,8},{8,4},{11,15},{15,11},{12,16},{16,12},{19,23},{2... | collective-permute-start | bytes 245768 | tf_op jit(solution)/shard_map/ppermute | solution.py:512
  12.3 0.0 copy-done
  12.3 8.8 %shard_map.30.refs_6_ = f32[2,160,128]{2,1,0:T(8,128)S(1)} custom-call(bf16[40,768]{1,0:T(8,128)(2,1)S(1)} %get-tuple-element.20.refs_0_, bf16[40,768]{1,0:T(8,128)(2,1)S(1)} %collective-permute-done.refs_1_, bf16[40,768]{1,0:T(8,128)(2,1)S(1)} %collective-permute-done.1.refs_2_, bf16[40,768]{1,0:T(8,128)(2,1)S(1)} %collective-permute-done.2.refs_3_, ...), custom_call_target="tpu_custom_call" | custom-call | tf_op jit(solution)/shard_map/pallas_call | solution.py:444
  21.2 0.0 collective-permute-done.3.refs_5_
  21.2 9.1 %shard_map.31 = (f32[20,128]{1,0:T(8,128)S(1)}, f32[20,128]{1,0:T(8,128)S(1)}, f32[20,128]{1,0:T(8,128)S(1)}, f32[20,128]{1,0:T(8,128)S(1)}) custom-call(bf16[40,768]{1,0:T(8,128)(2,1)S(1)} %get-tuple-element.20.refs_0_, bf16[40,768]{1,0:T(8,128)(2,1)S(1)} %collective-permute-done.refs_1_, bf16[40,768]{1,0:T(8,128)(2,1)S(1)} %collective-permute-done.1.refs_2_, ...), custom_call_target="tpu_custom_call" | custom-call | tf_op jit(solution)/shard_map/pallas_call | solution.py:444
  30.2 0.1 collective-permute-start.4
  30.3 1.0 %collective-permute-start.5 = (f32[20,128]{1,0:T(8,128)S(1)}, f32[20,128]{1,0:T(8,128)S(1)}, u32[]{:S(2)}, u32[]{:S(2)}) collective-permute-start(f32[20,128]{1,0:T(8,128)S(1)} %get-tuple-element.27), channel_id=1, source_target_pairs={{0,2},{1,3},{2,0},{3,1},{4,6},{5,7},{6,4},{7,5},{8,10},{9,11},{10,... | collective-permute-start | bytes 30728 | tf_op jit(solution)/shard_map/ppermute | solution.py:522
  31.3 2.5 %collective-permute-start.6 = (f32[20,128]{1,0:T(8,128)S(1)}, f32[20,128]{1,0:T(8,128)S(1)}, u32[]{:S(2)}, u32[]{:S(2)}) collective-permute-start(f32[20,128]{1,0:T(8,128)S(1)} %get-tuple-element.28), channel_id=1, source_target_pairs={{0,3},{1,0},{2,1},{3,2},{4,7},{5,4},{6,5},{7,6},{8,11},{9,8},{10,9... | collective-permute-start | bytes 30728 | tf_op jit(solution)/shard_map/ppermute | solution.py:522
  33.7 1.1 %collective-permute-done.4.refs_1_ = f32[20,128]{1,0:T(8,128)S(1)} collective-permute-done((f32[20,128]{1,0:T(8,128)S(1)}, f32[20,128]{1,0:T(8,128)S(1)}, u32[]{:S(2)}, u32[]{:S(2)}) %collective-permute-start.4) | collective-permute-done | bytes 10272 | tf_op jit(solution)/shard_map/ppermute | solution.py:522
  34.9 0.0 collective-permute-done.5.refs_2_
  34.9 0.6 %collective-permute-done.6.refs_3_ = f32[20,128]{1,0:T(8,128)S(1)} collective-permute-done((f32[20,128]{1,0:T(8,128)S(1)}, f32[20,128]{1,0:T(8,128)S(1)}, u32[]{:S(2)}, u32[]{:S(2)}) %collective-permute-start.6) | collective-permute-done | bytes 10272 | tf_op jit(solution)/shard_map/ppermute | solution.py:522
  35.4 0.8 %shard_map.32 = f32[2,40,128]{2,1,0:T(8,128)} custom-call(f32[20,128]{1,0:T(8,128)S(1)} %get-tuple-element.25.refs_0_, f32[20,128]{1,0:T(8,128)S(1)} %collective-permute-done.4.refs_1_, f32[20,128]{1,0:T(8,128)S(1)} %collective-permute-done.5.refs_2_, f32[20,128]{1,0:T(8,128)S(1)} %collective-permute-done.6.refs_3_), custom_call_target="tpu_custom_call" | custom-call | tf_op jit(solution)/shard_map/pallas_call | solution.py:523
  (5 shorter events, 0.0 us)
Async XLA Ops:
  0.0 0.9 %copy-start.1 = (bf16[2,40,7,128]{3,1,2,0:T(8,128)(2,1)S(1)}, bf16[2,40,7,128]{3,1,2,0:T(8,128)(2,1)}, u32[]{:S(2)}) copy-start(bf16[2,40,7,128]{3,1,2,0:T(8,128)(2,1)} %param.2) | copy-start | bytes 430084
  1.6 7.4 %collective-permute-start = (bf16[40,768]{1,0:T(8,128)(2,1)S(1)}, bf16[40,768]{1,0:T(8,128)(2,1)S(1)}, u32[]{:S(2)}, u32[]{:S(2)}) collective-permute-start(bf16[40,768]{1,0:T(8,128)(2,1)S(1)} %get-tuple-element.21), channel_id=1, source_target_pairs={{0,1},{1,2},{2,3},{3,0},{4,5},{5,6},{6,7},{7,4},{8,9},{9,10},{10,1... | collective-permute-start | bytes 184328 | tf_op jit(solution)/shard_map/ppermute | solution.py:493
  4.6 4.4 %collective-permute-start.1 = (bf16[40,768]{1,0:T(8,128)(2,1)S(1)}, bf16[40,768]{1,0:T(8,128)(2,1)S(1)}, u32[]{:S(2)}, u32[]{:S(2)}) collective-permute-start(bf16[40,768]{1,0:T(8,128)(2,1)S(1)} %get-tuple-element.22), channel_id=1, source_target_pairs={{0,2},{1,3},{2,0},{3,1},{4,6},{5,7},{6,4},{7,5},{8,10},{9,11},{10,... | collective-permute-start | bytes 184328 | tf_op jit(solution)/shard_map/ppermute | solution.py:493
  6.1 4.2 %collective-permute-start.2 = (bf16[40,768]{1,0:T(8,128)(2,1)S(1)}, bf16[40,768]{1,0:T(8,128)(2,1)S(1)}, u32[]{:S(2)}, u32[]{:S(2)}) collective-permute-start(bf16[40,768]{1,0:T(8,128)(2,1)S(1)} %get-tuple-element.23), channel_id=1, source_target_pairs={{0,3},{1,0},{2,1},{3,2},{4,7},{5,4},{6,5},{7,6},{8,11},{9,8},{10,9... | collective-permute-start | bytes 184328 | tf_op jit(solution)/shard_map/ppermute | solution.py:493
  9.0 3.3 %copy-start = (f32[2,160,128]{2,1,0:T(8,128)S(1)}, f32[2,160,128]{2,1,0:T(8,128)}, u32[]{:S(2)}) copy-start(f32[2,160,128]{2,1,0:T(8,128)} %shard_map.29.refs_4_) | copy-start | bytes 491524
  10.3 10.8 %collective-permute-start.3 = (bf16[160,256]{1,0:T(8,128)(2,1)S(1)}, bf16[160,256]{1,0:T(8,128)(2,1)S(1)}, u32[]{:S(2)}, u32[]{:S(2)}) collective-permute-start(bf16[160,256]{1,0:T(8,128)(2,1)S(1)} %maximum_maximum_fusion), channel_id=1, source_target_pairs={{3,7},{7,3},{4,8},{8,4},{11,15},{15,11},{12,16},{16,12},{19,23},{2... | collective-permute-start | bytes 245768 | tf_op jit(solution)/shard_map/ppermute | solution.py:512
  30.2 4.6 %collective-permute-start.4 = (f32[20,128]{1,0:T(8,128)S(1)}, f32[20,128]{1,0:T(8,128)S(1)}, u32[]{:S(2)}, u32[]{:S(2)}) collective-permute-start(f32[20,128]{1,0:T(8,128)S(1)} %get-tuple-element.26), channel_id=1, source_target_pairs={{0,1},{1,2},{2,3},{3,0},{4,5},{5,6},{6,7},{7,4},{8,9},{9,10},{10,1... | collective-permute-start | bytes 30728 | tf_op jit(solution)/shard_map/ppermute | solution.py:522
  30.3 4.6 %collective-permute-start.5 = (f32[20,128]{1,0:T(8,128)S(1)}, f32[20,128]{1,0:T(8,128)S(1)}, u32[]{:S(2)}, u32[]{:S(2)}) collective-permute-start(f32[20,128]{1,0:T(8,128)S(1)} %get-tuple-element.27), channel_id=1, source_target_pairs={{0,2},{1,3},{2,0},{3,1},{4,6},{5,7},{6,4},{7,5},{8,10},{9,11},{10,... | collective-permute-start | bytes 30728 | tf_op jit(solution)/shard_map/ppermute | solution.py:522
  31.3 4.2 %collective-permute-start.6 = (f32[20,128]{1,0:T(8,128)S(1)}, f32[20,128]{1,0:T(8,128)S(1)}, u32[]{:S(2)}, u32[]{:S(2)}) collective-permute-start(f32[20,128]{1,0:T(8,128)S(1)} %get-tuple-element.28), channel_id=1, source_target_pairs={{0,3},{1,0},{2,1},{3,2},{4,7},{5,4},{6,5},{7,6},{8,11},{9,8},{10,9... | collective-permute-start | bytes 30728 | tf_op jit(solution)/shard_map/ppermute | solution.py:522

commit v8 on v7

--- a/solution.py
+++ b/solution.py
@@ -62,26 +62,9 @@
         return jnp.where(self.swapped(chunk), 1 - slot, slot)
 
 
-def taper_kernel(plan, days_ref, taper):
-    n_date = plan.n_date
-    me = lax.axis_index("date")
-    row = days_ref[...].astype(f32).reshape(1, DATES)
-    lane_of = lax.broadcasted_iota(jnp.int32, (8, DATES), 1)
-    sub_of = lax.broadcasted_iota(jnp.int32, (8, DATES), 0)
-    for r in range(n_date):
-        first = lax.rem(me + n_date - r, n_date) * plan.own
-        for b in range(0, plan.own, 8):
-            high = min(8, plan.own - b)
-            picked = jnp.where(lane_of == sub_of + (first + b), row, 0.0)
-            days = jnp.sum(picked, axis=1, keepdims=True)[:high]
-            at = r * plan.own + b
-            taper[0, at : at + high] = jnp.broadcast_to(jnp.exp(days * (1.0 / taper_days)), (high, LANES))
-            taper[1, at : at + high] = jnp.broadcast_to(jnp.exp(days * (-1.0 / taper_days)), (high, LANES))
-
-
-def pack_kernel(plan, x_ref, *refs):
+def pack_kernel(plan, steps, x_ref, *refs):
     n_date, width = plan.n_date, plan.width
-    main, plane = refs[:n_date], refs[n_date]
+    main, plane = refs[:-1], refs[-1]
     me = lax.axis_index("date")
     plane[...] = x_ref[...].astype(f32)
     lane = lax.broadcasted_iota(jnp.int32, (1, LANES), 1)
@@ -96,7 +79,7 @@
                     at = lane + (tile * LANES - start)
                     tiles[tile] = jnp.where((at >= low) & (at < high), moved, tiles[tile])
 
-    for r in range(n_date):
+    for slot, r in enumerate(steps):
         chunk = plan.chunk(lax.rem(me + r, n_date))
         swapped = plan.swapped(chunk)
         window = chunk * plan.cols - RIM
@@ -124,7 +107,25 @@
             )
             for k, tile in enumerate(tiles):
                 at = part * plan.stride + k * LANES
-                main[r][:, at : at + LANES] = tile.astype(bf16)
+                main[slot][:, at : at + LANES] = tile.astype(bf16)
+
+
+def own_kernel(plan, x_ref, days_ref, main, taper, plane):
+    pack_kernel(plan, [0], x_ref, main, plane)
+    n_date = plan.n_date
+    me = lax.axis_index("date")
+    row = days_ref[...].astype(f32).reshape(1, DATES)
+    lane_of = lax.broadcasted_iota(jnp.int32, (8, DATES), 1)
+    sub_of = lax.broadcasted_iota(jnp.int32, (8, DATES), 0)
+    for r in range(n_date):
+        first = lax.rem(me + n_date - r, n_date) * plan.own
+        for b in range(0, plan.own, 8):
+            high = min(8, plan.own - b)
+            picked = jnp.where(lane_of == sub_of + (first + b), row, 0.0)
+            days = jnp.sum(picked, axis=1, keepdims=True)[:high]
+            at = r * plan.own + b
+            taper[0, at : at + high] = jnp.broadcast_to(jnp.exp(days * (1.0 / taper_days)), (high, LANES))
+            taper[1, at : at + high] = jnp.broadcast_to(jnp.exp(days * (-1.0 / taper_days)), (high, LANES))
 
 
 def unpack_kernel(plan, *refs):
@@ -205,25 +206,23 @@
         is_left = plan.swapped(chunk)
         depth = jnp.where(is_left, chunk, n_date - 1 - chunk)
         missing = RIM - depth * plan.cols
-        wide = plan.tail_width
+        wide, lanes = plan.tail_width, plan.tail_lanes
         base = plan.tail - plan.pieces[1][0] if plan.halves == 2 else 0
 
         @pl.when(missing > 0)
         def _():
-            at = lax.broadcasted_iota(jnp.int32, (1, PART), 1) - base
+            at = lax.broadcasted_iota(jnp.int32, (1, lanes), 1) + (PART - lanes - base)
             col = at
             for _line in range(1, LINES):
                 col = jnp.where(col >= wide, col - wide, col)
             low = jnp.where(is_left, 0, wide - missing)
             valid = (col >= low) & (col < low + missing) & (at >= 0) & (at < LINES * wide)
             outermost = lax.axis_index("space") == jnp.where(is_left, 0, lax.axis_size("space") - 1)
-            shift = jnp.where(is_left, missing - wide, wide - missing) + base
+            shift = jnp.where(is_left, missing - wide, wide - missing) + base + lanes
             for part in range(2):
-                got = edge_ref[:, part * plan.tail_lanes : (part + 1) * plan.tail_lanes].astype(f32)
-                if plan.tail_lanes < PART:
-                    got = jnp.concatenate([got, jnp.zeros((DATES, PART - plan.tail_lanes), f32)], axis=1)
-                got = jnp.where(outermost, 0.0, pltpu.roll(got, lax.rem(shift + PART, PART), 1))
-                at_part = slice(part * PART, (part + 1) * PART)
+                got = edge_ref[:, part * lanes : (part + 1) * lanes].astype(f32)
+                got = jnp.where(outermost, 0.0, pltpu.roll(got, lax.rem(shift, lanes), 1))
+                at_part = slice((part + 1) * PART - lanes, (part + 1) * PART)
                 s_ref[:, at_part] = jnp.where(valid, got, s_ref[:, at_part])
 
     sr, si = s_ref[:, 0:PART], s_ref[:, PART : 2 * PART]
@@ -472,22 +471,28 @@
     plan = Plan(acquisitions.shape, n_date)
     own = plan.own
 
-    main = pl.pallas_call(
-        functools.partial(pack_kernel, plan),
-        out_shape=[jax.ShapeDtypeStruct((own, 2 * plan.stride), bf16)] * n_date,
+    samples = jnp.transpose(acquisitions, (0, 2, 1, 3))
+    message = jax.ShapeDtypeStruct((own, 2 * plan.stride), bf16)
+    plane = pltpu.VMEM((2, LINES, own, LANES), f32)
+    params = pltpu.CompilerParams(vmem_limit_bytes=24 * 2**20)
+    sent = pl.pallas_call(
+        functools.partial(pack_kernel, plan, list(range(1, n_date))),
+        out_shape=[message] * (n_date - 1),
         in_specs=[VMEM],
-        out_specs=[VMEM] * n_date,
-        scratch_shapes=[pltpu.VMEM((2, LINES, own, LANES), f32)],
-        compiler_params=pltpu.CompilerParams(vmem_limit_bytes=24 * 2**20),
-    )(jnp.transpose(acquisitions, (0, 2, 1, 3)))
-    main = list(main)
-    main[0], acquisition_day = lax.optimization_barrier((main[0], acquisition_day))
-    taper = pl.pallas_call(
-        functools.partial(taper_kernel, plan),
-        out_shape=jax.ShapeDtypeStruct((2, DATES, LANES), f32),
-        in_specs=[VMEM],
-        out_specs=VMEM,
-    )(acquisition_day)
+        out_specs=[VMEM] * (n_date - 1),
+        scratch_shapes=[plane],
+        compiler_params=params,
+    )(samples)
+    first, acquisition_day = lax.optimization_barrier((sent[0], acquisition_day))
+    own_main, taper = pl.pallas_call(
+        functools.partial(own_kernel, plan),
+        out_shape=[message, jax.ShapeDtypeStruct((2, DATES, LANES), f32)],
+        in_specs=[VMEM, VMEM],
+        out_specs=[VMEM, VMEM],
+        scratch_shapes=[plane],
+        compiler_params=params,
+    )(samples, acquisition_day)
+    main = [own_main, first, *sent[1:]]
     main[0], taper = lax.optimization_barrier((main[0], taper))
     for r in range(1, n_date):
         main[r] = lax.ppermute(main[r], "date", [(i, (i + r) % n_date) for i in range(n_date)])

time: 36.3 us -> 36.2 us (level)
  Pallas kernels: 20.8 us -> 19.4 us
  waiting for transfers between devices: 3 us -> 4.15 us
    pallas_call x2, Pallas kernels: 2.13 us -> 0.81 us  [the longest x1 0.53 us: local(): pl.pallas_call(functools.partial(pack_kernel, plan, list(range(1, n_date)...]
    ppermute x3, waiting for transfers between devices: 1.29 us -> 2.46 us  [local(): lax.ppermute(main[r], 'date', [(i, (i + r) % n_date) for i in range(n_dat...]
  transfers between devices with their start and end apart: 7 -> 7, of which waited for: 3 -> 4; matrix products, arithmetic and copies ran while one was open for 0% -> 0% of each run, Pallas kernels for 28% -> 25%
where the time goes in v8:
time: 36.2 us; the launch traced here: 36 us
  Pallas kernels  19.4 us (54%)
  starting transfers between devices  11.4 us (31%)
  waiting for transfers between devices  4.15 us (11%)
  local copies, waits for them, and re-layouts  0.93 us (3%)
    pallas_call x2, Pallas kernels, link(): pl.pallas_call(functools.partial(link_kernel, plan, slot), out_shape=shap...  17.9 us
    ppermute x3, starting transfers between devices, local(): lax.ppermute(main[r], 'date', [(i, (i + r) % n_date) for i in range(n_dat...  5.94 us
    ppermute x3, starting transfers between devices, local(): lax.ppermute(out[k], 'date', [(i, (i + k) % n_date) for i in range(n_date)])  3.51 us
    ppermute x3, waiting for transfers between devices, local(): lax.ppermute(main[r], 'date', [(i, (i + r) % n_date) for i in range(n_dat...  2.46 us
    ppermute x1, starting transfers between devices, local(): edge = lax.ppermute(edge, ('space', 'date'), swap)  1.99 us
    ppermute x3, waiting for transfers between devices, local(): lax.ppermute(out[k], 'date', [(i, (i + k) % n_date) for i in range(n_date)])  1.69 us
    unnamed x4, local copies, waits for them, and re-layouts  0.91 us
    pallas_call x1, Pallas kernels, local(): pl.pallas_call(functools.partial(unpack_kernel, plan), out_shape=jax.Shap...  0.75 us
  transfers between devices with their start and end apart: 7, of which 4 were waited for; matrix products, arithmetic and copies ran while one was open for 0% of the time, Pallas kernels for 25%

profile of v8, /device:TPU:0, one launch (start us, length us, event | category | flops | bytes accessed | tf_op | source)
XLA Modules:
  0.0 36.0 jit_solution(15380285231650618674)
XLA Ops:
  0.0 0.0 copy-start
  0.0 0.9 %copy-done = bf16[2,40,7,128]{3,1,2,0:T(8,128)(2,1)S(1)} copy-done((bf16[2,40,7,128]{3,1,2,0:T(8,128)(2,1)S(1)}, bf16[2,40,7,128]{3,1,2,0:T(8,128)(2,1)}, u32[]{:S(2)}) %copy-start) | copy-done | bytes 143384
  0.9 0.5 %shard_map.28 = (bf16[40,768]{1,0:T(8,128)(2,1)S(1)}, bf16[40,768]{1,0:T(8,128)(2,1)S(1)}, bf16[40,768]{1,0:T(8,128)(2,1)S(1)}) custom-call(bf16[2,7,40,128]{3,2,1,0:T(8,128)(2,1)S(1)} %bitcast.1), custom_call_target="tpu_custom_call" | custom-call | tf_op jit(solution)/shard_map/pallas_call | solution.py:478
  1.4 3.0 %collective-permute-start = (bf16[40,768]{1,0:T(8,128)(2,1)S(1)}, bf16[40,768]{1,0:T(8,128)(2,1)S(1)}, u32[]{:S(2)}, u32[]{:S(2)}) collective-permute-start(bf16[40,768]{1,0:T(8,128)(2,1)S(1)} %get-tuple-element.19), channel_id=1, source_target_pairs={{0,1},{1,2},{2,3},{3,0},{4,5},{5,6},{6,7},{7,4},{8,9},{9,10},{10,1... | collective-permute-start | bytes 184328 | tf_op jit(solution)/shard_map/ppermute | solution.py:498
  4.4 0.0 copy-start.1
  4.4 1.5 %collective-permute-start.1 = (bf16[40,768]{1,0:T(8,128)(2,1)S(1)}, bf16[40,768]{1,0:T(8,128)(2,1)S(1)}, u32[]{:S(2)}, u32[]{:S(2)}) collective-permute-start(bf16[40,768]{1,0:T(8,128)(2,1)S(1)} %get-tuple-element.20), channel_id=1, source_target_pairs={{0,2},{1,3},{2,0},{3,1},{4,6},{5,7},{6,4},{7,5},{8,10},{9,11},{10,... | collective-permute-start | bytes 184328 | tf_op jit(solution)/shard_map/ppermute | solution.py:498
  6.0 1.4 %collective-permute-start.2 = (bf16[40,768]{1,0:T(8,128)(2,1)S(1)}, bf16[40,768]{1,0:T(8,128)(2,1)S(1)}, u32[]{:S(2)}, u32[]{:S(2)}) collective-permute-start(bf16[40,768]{1,0:T(8,128)(2,1)S(1)} %get-tuple-element.21), channel_id=1, source_target_pairs={{0,3},{1,0},{2,1},{3,2},{4,7},{5,4},{6,5},{7,6},{8,11},{9,8},{10,9... | collective-permute-start | bytes 184328 | tf_op jit(solution)/shard_map/ppermute | solution.py:498
  7.4 0.0 copy-done.1
  7.4 0.3 shard_map.29
  7.7 0.0 collective-permute-done.refs_1_
  7.7 1.0 %collective-permute-done.1.refs_2_ = bf16[40,768]{1,0:T(8,128)(2,1)S(1)} collective-permute-done((bf16[40,768]{1,0:T(8,128)(2,1)S(1)}, bf16[40,768]{1,0:T(8,128)(2,1)S(1)}, u32[]{:S(2)}, u32[]{:S(2)}) %collective-permute-start.1) | collective-permute-done | bytes 61472 | tf_op jit(solution)/shard_map/ppermute | solution.py:498
  8.7 1.5 %collective-permute-done.2.refs_3_ = bf16[40,768]{1,0:T(8,128)(2,1)S(1)} collective-permute-done((bf16[40,768]{1,0:T(8,128)(2,1)S(1)}, bf16[40,768]{1,0:T(8,128)(2,1)S(1)}, u32[]{:S(2)}, u32[]{:S(2)}) %collective-permute-start.2) | collective-permute-done | bytes 61472 | tf_op jit(solution)/shard_map/ppermute | solution.py:498
  10.2 2.0 %collective-permute-start.3 = (bf16[160,256]{1,0:T(8,128)(2,1)S(1)}, bf16[160,256]{1,0:T(8,128)(2,1)S(1)}, u32[]{:S(2)}, u32[]{:S(2)}) collective-permute-start(bf16[160,256]{1,0:T(8,128)(2,1)S(1)} %maximum_maximum_fusion), channel_id=1, source_target_pairs={{3,7},{7,3},{4,8},{8,4},{11,15},{15,11},{12,16},{16,12},{19,23},{2... | collective-permute-start | bytes 245768 | tf_op jit(solution)/shard_map/ppermute | solution.py:517
  12.2 8.8 %shard_map.30.refs_6_ = f32[2,160,128]{2,1,0:T(8,128)S(1)} custom-call(bf16[40,768]{1,0:T(8,128)(2,1)S(1)} %get-tuple-element.18.refs_0_, bf16[40,768]{1,0:T(8,128)(2,1)S(1)} %collective-permute-done.refs_1_, bf16[40,768]{1,0:T(8,128)(2,1)S(1)} %collective-permute-done.1.refs_2_, bf16[40,768]{1,0:T(8,128)(2,1)S(1)} %collective-permute-done.2.refs_3_, ...), custom_call_target="tpu_custom_call" | custom-call | tf_op jit(solution)/shard_map/pallas_call | solution.py:443
  21.0 0.0 collective-permute-done.3.refs_5_
  21.0 9.0 %shard_map.31 = (f32[20,128]{1,0:T(8,128)S(1)}, f32[20,128]{1,0:T(8,128)S(1)}, f32[20,128]{1,0:T(8,128)S(1)}, f32[20,128]{1,0:T(8,128)S(1)}) custom-call(bf16[40,768]{1,0:T(8,128)(2,1)S(1)} %get-tuple-element.18.refs_0_, bf16[40,768]{1,0:T(8,128)(2,1)S(1)} %collective-permute-done.refs_1_, bf16[40,768]{1,0:T(8,128)(2,1)S(1)} %collective-permute-done.1.refs_2_, ...), custom_call_target="tpu_custom_call" | custom-call | tf_op jit(solution)/shard_map/pallas_call | solution.py:443
  30.1 0.1 collective-permute-start.4
  30.1 1.0 %collective-permute-start.5 = (f32[20,128]{1,0:T(8,128)S(1)}, f32[20,128]{1,0:T(8,128)S(1)}, u32[]{:S(2)}, u32[]{:S(2)}) collective-permute-start(f32[20,128]{1,0:T(8,128)S(1)} %get-tuple-element.25), channel_id=1, source_target_pairs={{0,2},{1,3},{2,0},{3,1},{4,6},{5,7},{6,4},{7,5},{8,10},{9,11},{10,... | collective-permute-start | bytes 30728 | tf_op jit(solution)/shard_map/ppermute | solution.py:527
  31.1 2.5 %collective-permute-start.6 = (f32[20,128]{1,0:T(8,128)S(1)}, f32[20,128]{1,0:T(8,128)S(1)}, u32[]{:S(2)}, u32[]{:S(2)}) collective-permute-start(f32[20,128]{1,0:T(8,128)S(1)} %get-tuple-element.26), channel_id=1, source_target_pairs={{0,3},{1,0},{2,1},{3,2},{4,7},{5,4},{6,5},{7,6},{8,11},{9,8},{10,9... | collective-permute-start | bytes 30728 | tf_op jit(solution)/shard_map/ppermute | solution.py:527
  33.6 1.1 %collective-permute-done.4.refs_1_ = f32[20,128]{1,0:T(8,128)S(1)} collective-permute-done((f32[20,128]{1,0:T(8,128)S(1)}, f32[20,128]{1,0:T(8,128)S(1)}, u32[]{:S(2)}, u32[]{:S(2)}) %collective-permute-start.4) | collective-permute-done | bytes 10272 | tf_op jit(solution)/shard_map/ppermute | solution.py:527
  34.7 0.0 collective-permute-done.5.refs_2_
  34.7 0.6 %collective-permute-done.6.refs_3_ = f32[20,128]{1,0:T(8,128)S(1)} collective-permute-done((f32[20,128]{1,0:T(8,128)S(1)}, f32[20,128]{1,0:T(8,128)S(1)}, u32[]{:S(2)}, u32[]{:S(2)}) %collective-permute-start.6) | collective-permute-done | bytes 10272 | tf_op jit(solution)/shard_map/ppermute | solution.py:527
  35.3 0.8 %shard_map.32 = f32[2,40,128]{2,1,0:T(8,128)} custom-call(f32[20,128]{1,0:T(8,128)S(1)} %get-tuple-element.23.refs_0_, f32[20,128]{1,0:T(8,128)S(1)} %collective-permute-done.4.refs_1_, f32[20,128]{1,0:T(8,128)S(1)} %collective-permute-done.5.refs_2_, f32[20,128]{1,0:T(8,128)S(1)} %collective-permute-done.6.refs_3_), custom_call_target="tpu_custom_call" | custom-call | tf_op jit(solution)/shard_map/pallas_call | solution.py:528
  (5 shorter events, 0.0 us)
Async XLA Ops:
  0.0 0.9 %copy-start = (bf16[2,40,7,128]{3,1,2,0:T(8,128)(2,1)S(1)}, bf16[2,40,7,128]{3,1,2,0:T(8,128)(2,1)}, u32[]{:S(2)}) copy-start(bf16[2,40,7,128]{3,1,2,0:T(8,128)(2,1)} %param.2) | copy-start | bytes 430084
  1.4 6.3 %collective-permute-start = (bf16[40,768]{1,0:T(8,128)(2,1)S(1)}, bf16[40,768]{1,0:T(8,128)(2,1)S(1)}, u32[]{:S(2)}, u32[]{:S(2)}) collective-permute-start(bf16[40,768]{1,0:T(8,128)(2,1)S(1)} %get-tuple-element.19), channel_id=1, source_target_pairs={{0,1},{1,2},{2,3},{3,0},{4,5},{5,6},{6,7},{7,4},{8,9},{9,10},{10,1... | collective-permute-start | bytes 184328 | tf_op jit(solution)/shard_map/ppermute | solution.py:498
  4.4 3.0 %copy-start.1 = (s32[160]{0:T(256)S(1)}, s32[160]{0:T(256)}, u32[]{:S(2)}) copy-start(s32[160]{0:T(256)} %days_ref) | copy-start | bytes 1924
  4.4 4.3 %collective-permute-start.1 = (bf16[40,768]{1,0:T(8,128)(2,1)S(1)}, bf16[40,768]{1,0:T(8,128)(2,1)S(1)}, u32[]{:S(2)}, u32[]{:S(2)}) collective-permute-start(bf16[40,768]{1,0:T(8,128)(2,1)S(1)} %get-tuple-element.20), channel_id=1, source_target_pairs={{0,2},{1,3},{2,0},{3,1},{4,6},{5,7},{6,4},{7,5},{8,10},{9,11},{10,... | collective-permute-start | bytes 184328 | tf_op jit(solution)/shard_map/ppermute | solution.py:498
  6.0 4.2 %collective-permute-start.2 = (bf16[40,768]{1,0:T(8,128)(2,1)S(1)}, bf16[40,768]{1,0:T(8,128)(2,1)S(1)}, u32[]{:S(2)}, u32[]{:S(2)}) collective-permute-start(bf16[40,768]{1,0:T(8,128)(2,1)S(1)} %get-tuple-element.21), channel_id=1, source_target_pairs={{0,3},{1,0},{2,1},{3,2},{4,7},{5,4},{6,5},{7,6},{8,11},{9,8},{10,9... | collective-permute-start | bytes 184328 | tf_op jit(solution)/shard_map/ppermute | solution.py:498
  10.2 10.8 %collective-permute-start.3 = (bf16[160,256]{1,0:T(8,128)(2,1)S(1)}, bf16[160,256]{1,0:T(8,128)(2,1)S(1)}, u32[]{:S(2)}, u32[]{:S(2)}) collective-permute-start(bf16[160,256]{1,0:T(8,128)(2,1)S(1)} %maximum_maximum_fusion), channel_id=1, source_target_pairs={{3,7},{7,3},{4,8},{8,4},{11,15},{15,11},{12,16},{16,12},{19,23},{2... | collective-permute-start | bytes 245768 | tf_op jit(solution)/shard_map/ppermute | solution.py:517
  30.1 4.6 %collective-permute-start.4 = (f32[20,128]{1,0:T(8,128)S(1)}, f32[20,128]{1,0:T(8,128)S(1)}, u32[]{:S(2)}, u32[]{:S(2)}) collective-permute-start(f32[20,128]{1,0:T(8,128)S(1)} %get-tuple-element.24), channel_id=1, source_target_pairs={{0,1},{1,2},{2,3},{3,0},{4,5},{5,6},{6,7},{7,4},{8,9},{9,10},{10,1... | collective-permute-start | bytes 30728 | tf_op jit(solution)/shard_map/ppermute | solution.py:527
  30.1 4.6 %collective-permute-start.5 = (f32[20,128]{1,0:T(8,128)S(1)}, f32[20,128]{1,0:T(8,128)S(1)}, u32[]{:S(2)}, u32[]{:S(2)}) collective-permute-start(f32[20,128]{1,0:T(8,128)S(1)} %get-tuple-element.25), channel_id=1, source_target_pairs={{0,2},{1,3},{2,0},{3,1},{4,6},{5,7},{6,4},{7,5},{8,10},{9,11},{10,... | collective-permute-start | bytes 30728 | tf_op jit(solution)/shard_map/ppermute | solution.py:527
  31.1 4.2 %collective-permute-start.6 = (f32[20,128]{1,0:T(8,128)S(1)}, f32[20,128]{1,0:T(8,128)S(1)}, u32[]{:S(2)}, u32[]{:S(2)}) collective-permute-start(f32[20,128]{1,0:T(8,128)S(1)} %get-tuple-element.26), channel_id=1, source_target_pairs={{0,3},{1,0},{2,1},{3,2},{4,7},{5,4},{6,5},{7,6},{8,11},{9,8},{10,9... | collective-permute-start | bytes 30728 | tf_op jit(solution)/shard_map/ppermute | solution.py:527
